TPU v7x, 128 devices: a whole 4x4x4 slice. The times are simulated.
128 devices in a mesh: sp: 4 (over z), ctx: 8 (over x_hi, y), wa: 4 (over x_lo, core).
Axes of the slice: x: 4 (x_hi: 2, x_lo: 2; x = x_hi * 2 + x_lo), y: 4, z: 4, core: 2. Of those that a mesh axis runs over, the one named last changes fastest.
Arguments:
- tokens: bfloat16 [4096, 2048], P(('sp', 'ctx')), may hold values from -6 to 6
- cotangent: bfloat16 [4096, 2048], P(('sp', 'ctx')), may hold values from -6 to 6
- routes: int32 [4096, 6], P(('sp', 'ctx')), may hold values from 0 to 63, all different within a row; in each aligned block of 128 rows (0 to 127, 128 to 255, ...) at most 16 rows name the same one
- attn_gain: bfloat16 [2048], P(('sp', 'ctx')), may hold values from 0.5 to 1.5
- query_weight: bfloat16 [2048, 2048], P(('sp', 'ctx'), 'wa'), may hold values from -0.125 to 0.125
- key_weight: bfloat16 [2048, 2048], P(('sp', 'ctx'), 'wa'), may hold values from -0.125 to 0.125
- value_weight: bfloat16 [2048, 2048], P(('sp', 'ctx'), 'wa'), may hold values from -0.125 to 0.125
- output_weight: bfloat16 [2048, 2048], P('wa', ('sp', 'ctx')), may hold values from -2 to 2
- mlp_gain: bfloat16 [2048], P(('sp', 'ctx')), may hold values from 0.5 to 1.5
- router_weight: bfloat16 [2048, 64], P(('sp', 'ctx')), may hold values from -0.0625 to 0.0625
- shared_gate: bfloat16 [2048, 2816], P(('sp', 'ctx'), 'wa'), may hold values from -0.125 to 0.125
- shared_up: bfloat16 [2048, 2816], P(('sp', 'ctx'), 'wa'), may hold values from -0.125 to 0.125
- shared_down: bfloat16 [2816, 2048], P('wa', ('sp', 'ctx')), may hold values from -0.21875 to 0.21875
- expert_gate: bfloat16 [64, 2048, 1408], P(('sp', 'ctx'), None, 'wa'), may hold values from -0.125 to 0.125
- expert_up: bfloat16 [64, 2048, 1408], P(('sp', 'ctx'), None, 'wa'), may hold values from -0.125 to 0.125
- expert_down: bfloat16 [64, 1408, 2048], P(('sp', 'ctx'), 'wa'), may hold values from -6 to 6
Outputs:
- block_out: bfloat16 [4096, 2048], P(('sp', 'ctx'))
- tokens_grad: bfloat16 [4096, 2048], P(('sp', 'ctx'))
- attn_gain_grad: float32 [2048], P(('sp', 'ctx'))
- query_weight_grad: float32 [2048, 2048], P(('sp', 'ctx'), 'wa')
- key_weight_grad: float32 [2048, 2048], P(('sp', 'ctx'), 'wa')
- value_weight_grad: float32 [2048, 2048], P(('sp', 'ctx'), 'wa')
- output_weight_grad: float32 [2048, 2048], P('wa', ('sp', 'ctx'))
- mlp_gain_grad: float32 [2048], P(('sp', 'ctx'))
- router_weight_grad: float32 [2048, 64], P(('sp', 'ctx'))
- shared_gate_grad: float32 [2048, 2816], P(('sp', 'ctx'), 'wa')
- shared_up_grad: float32 [2048, 2816], P(('sp', 'ctx'), 'wa')
- shared_down_grad: float32 [2816, 2048], P('wa', ('sp', 'ctx'))
- expert_gate_grad: float32 [64, 2048, 1408], P(('sp', 'ctx'), None, 'wa')
- expert_up_grad: float32 [64, 2048, 1408], P(('sp', 'ctx'), None, 'wa')
- expert_down_grad: float32 [64, 1408, 2048], P(('sp', 'ctx'), 'wa')
Inputs may be any that keep to these rules, and one draw needn't show every extreme that they name: `routes`: each row names 6 different experts and every expert is named by some row. In each aligned block of 128 rows no expert is named more than 16 times, a bound that some block reaches.
All inputs are finite; a program needn't handle non-finite values.
Results may differ from a plain program's by a relative error of at most 0.035.
Values may be sent and summed in bfloat16 or wider, within the bound.
A program may use at most 256 MiB of HBM per device.

v0:
```python
import jax
import jax.numpy as jnp
from jax import lax
from jax.sharding import PartitionSpec as P

D = 2048
HD = 128
TOP = 6


EPSILON = 1e-06
ROPE_BASE = 10000.0
MASKED = -1e30
PRECISE = lax.Precision.HIGHEST


def copy_for_each(x, axis):
    size = lax.axis_size(axis)
    return lax.all_to_all(jnp.broadcast_to(x[None], (size, *x.shape)), axis, 0, 0, tiled=True)


def taken_together(x, axis):
    return copy_for_each(x, axis).astype(jnp.float32).sum(axis=0)


def turned_gather(arrays, axis, dims):
    turned = [jnp.moveaxis(a, dim, 0) for a, dim in zip(arrays, dims)]
    widths = [t[0].size for t in turned]
    both = jnp.concatenate([t.reshape(-1, w) for t, w in zip(turned, widths)], axis=1)
    whole = lax.all_gather(both, axis, axis=0, tiled=True)
    pieces = jnp.split(whole, [sum(widths[:k]) for k in range(1, len(widths))], axis=1)
    return tuple(
        (
            jnp.moveaxis(b.reshape(-1, *t.shape[1:]), 0, dim)
            for b, t, dim in zip(pieces, turned, dims)
        )
    )


def in_one_piece(arrays, axis, dim, along):
    widths = [a.shape[along] for a in arrays]
    both = jnp.concatenate(arrays, axis=along)
    whole = lax.all_gather(both, axis, axis=dim, tiled=True)
    return tuple(jnp.split(whole, [sum(widths[:k]) for k in range(1, len(widths))], axis=along))


def side_by_side(arrays, axis, dim, along):
    widths = [a.shape[along] for a in arrays]
    both = jnp.concatenate(arrays, axis=along)
    whole = lax.psum_scatter(both, axis, scatter_dimension=dim, tiled=True)
    return tuple(jnp.split(whole, [sum(widths[:k]) for k in range(1, len(widths))], axis=along))


def side_by_side_2(arrays, axis, dim, along):
    columns = [a.reshape(*a.shape[:along], -1) for a in arrays]
    both = jnp.concatenate(columns, axis=along)
    whole, at, gathered = (lax.psum_scatter(both, axis, scatter_dimension=dim, tiled=True), 0, [])
    for a, column in zip(arrays, columns):
        share = whole[..., at : at + column.shape[along]]
        gathered.append(share.reshape(*share.shape[:along], *a.shape[along:]))
        at += column.shape[along]
    return tuple(gathered)


def rope_tables(positions):
    half_width = HD // 2
    inverse = 1.0 / ROPE_BASE ** (jnp.arange(half_width, dtype=jnp.float32) * 2.0 / HD)
    angles = positions[:, None] * inverse[None, :]
    return (jnp.cos(angles)[:, None, :], jnp.sin(angles)[:, None, :])


def rotate(values, cosine, sine_part, direction):
    half_width = values.shape[-1] // 2
    leading = values[..., :half_width]
    trailing = values[..., half_width:]
    return jnp.concatenate(
        [
            leading * cosine - direction * trailing * sine_part,
            trailing * cosine + direction * leading * sine_part,
        ],
        axis=-1,
    )


def send_share(rows):
    quarter = D // lax.axis_size("wa")
    start = lax.axis_index("wa") * quarter
    piece = lax.dynamic_slice_in_dim(rows, start, quarter, 1)
    moved = lax.all_to_all(piece, ("sp", "ctx"), split_axis=0, concat_axis=0, tiled=True)
    return lax.all_gather(moved, "wa", axis=1, tiled=True)


def back_share(expert_part, shared_part):
    share = lax.psum_scatter(
        expert_part.astype(jnp.bfloat16), "wa", scatter_dimension=1, tiled=True
    )
    moved = lax.all_to_all(share, ("sp", "ctx"), split_axis=0, concat_axis=0, tiled=True)
    returned = lax.all_gather(moved, "wa", axis=1, tiled=True)
    shared_sum = taken_together(shared_part.astype(jnp.bfloat16), "wa").astype(jnp.float32)
    return (returned, shared_sum)


def send_rows_out(rows):
    return send_share(rows)


def bring_back(expert_part, shared_part):
    return back_share(expert_part, shared_part)


def shards(
    tokens,
    cotangent,
    routes,
    attn_gain,
    query_weight,
    key_weight,
    value_weight,
    output_weight,
    mlp_gain,
    router_weight,
    shared_gate,
    shared_up,
    shared_down,
    expert_gate,
    expert_up,
    expert_down,
):
    local_tokens = tokens.shape[0]
    heads_here = query_weight.shape[1] // HD
    head_cols = heads_here * HD
    experts_all = router_weight.shape[1]
    experts_here = expert_gate.shape[0]
    devices_seq = lax.axis_size("sp") * lax.axis_size("ctx")
    capacity = max(2, 4 * local_tokens * TOP // (3 * experts_all))
    score_scale = HD ** (-0.5)
    seq_len = local_tokens * devices_seq
    device_pos = lax.axis_index("sp") * lax.axis_size("ctx") + lax.axis_index("ctx")
    gathered = turned_gather(
        (
            attn_gain,
            query_weight,
            key_weight,
            value_weight,
            output_weight,
            mlp_gain,
            router_weight,
            shared_gate,
            shared_up,
            shared_down,
        ),
        ("sp", "ctx"),
        (0, 0, 0, 0, 1, 0, 0, 0, 0, 1),
    )
    (
        full_attn_gain,
        full_query,
        full_key,
        full_value,
        full_output,
        full_mlp_gain,
        full_router,
        full_sgate,
        full_sup,
        full_sdown,
    ) = gathered
    tokens_f = tokens.astype(jnp.float32)
    inv_one = lax.rsqrt(jnp.mean(tokens_f * tokens_f, axis=-1, keepdims=True) + EPSILON)
    unit_one = tokens_f * inv_one
    gain_one = full_attn_gain.astype(jnp.float32)
    normed = (unit_one * gain_one).astype(jnp.bfloat16)
    query_pos = device_pos * local_tokens + jnp.arange(local_tokens, dtype=jnp.int32)
    cosine, sine_part = rope_tables(query_pos.astype(jnp.float32))
    query_raw = jnp.dot(normed, full_query, preferred_element_type=jnp.float32).reshape(
        local_tokens, heads_here, HD
    )
    key_raw = jnp.dot(normed, full_key, preferred_element_type=jnp.float32).reshape(
        local_tokens, heads_here, HD
    )
    queries = rotate(query_raw, cosine, sine_part, 1.0).astype(jnp.bfloat16)
    keys_local = (
        rotate(key_raw, cosine, sine_part, 1.0)
        .astype(jnp.bfloat16)
        .reshape(local_tokens, head_cols)
    )
    values_local = jnp.dot(normed, full_value, preferred_element_type=jnp.float32).astype(
        jnp.bfloat16
    )
    keys_all, values_all = in_one_piece((keys_local, values_local), ("sp", "ctx"), 0, 1)
    keys_all = keys_all.reshape(seq_len, heads_here, HD)
    values_all = values_all.reshape(seq_len, heads_here, HD)
    visible = jnp.arange(seq_len, dtype=jnp.int32)[None, :] <= query_pos[:, None]

    def masked_scores():
        scores = (
            jnp.einsum("qhd,khd->hqk", queries, keys_all, preferred_element_type=jnp.float32)
            * score_scale
        )
        return jnp.where(visible[None], scores, MASKED)

    scores = masked_scores()
    row_max = jnp.max(scores, axis=-1, keepdims=True)
    weights = jnp.exp(scores - row_max)
    totals = jnp.sum(weights, axis=-1, keepdims=True)
    log_total = row_max + jnp.log(totals)
    probs_low = (weights / totals).astype(jnp.bfloat16)
    attended = (
        jnp.einsum("hqk,khd->qhd", probs_low, values_all, preferred_element_type=jnp.float32)
        .astype(jnp.bfloat16)
        .reshape(local_tokens, head_cols)
    )
    attn_part = jnp.dot(attended, full_output, preferred_element_type=jnp.float32)
    attn_out = taken_together(attn_part.astype(jnp.bfloat16), "wa").astype(jnp.float32)
    hidden_state = tokens_f + attn_out
    inv_two = lax.rsqrt(jnp.mean(hidden_state * hidden_state, axis=-1, keepdims=True) + EPSILON)
    unit_two = hidden_state * inv_two
    gain_two = full_mlp_gain.astype(jnp.float32)
    mlp_in = (unit_two * gain_two).astype(jnp.bfloat16)
    logits = jnp.dot(mlp_in, full_router, preferred_element_type=jnp.float32)
    logit_max = jnp.max(logits, axis=-1, keepdims=True)
    logit_exp = jnp.exp(logits - logit_max)
    router_probs = logit_exp / jnp.sum(logit_exp, axis=-1, keepdims=True)
    chosen = routes[:, :, None] == jnp.arange(experts_all, dtype=jnp.int32)[None, None, :]
    chosen_float = chosen.astype(jnp.float32)
    chosen_int = chosen.astype(jnp.int32)
    gate_values = jnp.sum(chosen_float * router_probs[:, None, :], axis=-1)
    running = jnp.cumsum(chosen_int.reshape(local_tokens * TOP, experts_all), axis=0).reshape(
        local_tokens, TOP, experts_all
    )
    slot_index = jnp.sum((running - 1) * chosen_int, axis=-1)
    destination = (routes * capacity + slot_index).reshape(-1)
    assign_ids = jnp.arange(local_tokens * TOP, dtype=jnp.int32)
    owner_assign = jnp.zeros((experts_all * capacity,), jnp.int32).at[destination].set(assign_ids)
    filled = jnp.zeros((experts_all * capacity,), jnp.bfloat16).at[destination].set(1.0)
    send_rows = mlp_in[owner_assign // TOP] * filled[:, None]
    arrived = send_rows_out(send_rows).reshape(devices_seq, experts_here, capacity, D)
    shared_pre = jnp.dot(mlp_in, full_sgate, preferred_element_type=jnp.float32)
    shared_lin = jnp.dot(mlp_in, full_sup, preferred_element_type=jnp.float32)
    shared_sig = jax.nn.sigmoid(shared_pre)
    shared_act = (shared_pre * shared_sig * shared_lin).astype(jnp.bfloat16)
    shared_part = jnp.dot(shared_act, full_sdown, preferred_element_type=jnp.float32)
    expert_pre = jnp.einsum(
        "secd,edf->secf", arrived, expert_gate, preferred_element_type=jnp.float32
    )
    expert_lin = jnp.einsum(
        "secd,edf->secf", arrived, expert_up, preferred_element_type=jnp.float32
    )
    expert_sig = jax.nn.sigmoid(expert_pre)
    expert_act = (expert_pre * expert_sig * expert_lin).astype(jnp.bfloat16)
    expert_part = jnp.einsum(
        "secf,efd->secd", expert_act, expert_down, preferred_element_type=jnp.float32
    ).reshape(-1, D)
    returned, shared_out = bring_back(expert_part, shared_part)
    picked = returned[destination].reshape(local_tokens, TOP, D).astype(jnp.float32)
    routed = jnp.sum(gate_values[:, :, None] * picked, axis=1)
    block_out = (hidden_state + (routed + shared_out)).astype(jnp.bfloat16)
    grad_out = cotangent.astype(jnp.float32)
    gate_grads = jnp.sum(grad_out[:, None, :] * picked, axis=-1)
    routed_grads = (
        (gate_values[:, :, None] * grad_out[:, None, :])
        .astype(jnp.bfloat16)
        .reshape(local_tokens * TOP, D)
    )
    send_grads = routed_grads[owner_assign] * filled[:, None]
    arrived_grads = send_rows_out(send_grads).reshape(devices_seq, experts_here, capacity, D)
    act_grads = jnp.einsum(
        "secd,efd->secf", arrived_grads, expert_down, preferred_element_type=jnp.float32
    )
    expert_down_grad = jnp.einsum(
        "secf,secd->efd", expert_act, arrived_grads, preferred_element_type=jnp.float32
    )
    swish_val = expert_pre * expert_sig
    swish_slope = expert_sig * (1.0 + expert_pre * (1.0 - expert_sig))
    pre_grads = (act_grads * expert_lin * swish_slope).astype(jnp.bfloat16)
    lin_grads = (act_grads * swish_val).astype(jnp.bfloat16)
    expert_gate_grad = jnp.einsum(
        "secd,secf->edf", arrived, pre_grads, preferred_element_type=jnp.float32
    )
    expert_up_grad = jnp.einsum(
        "secd,secf->edf", arrived, lin_grads, preferred_element_type=jnp.float32
    )
    rows_part = jnp.einsum(
        "secf,edf->secd", pre_grads, expert_gate, preferred_element_type=jnp.float32
    ) + jnp.einsum("secf,edf->secd", lin_grads, expert_up, preferred_element_type=jnp.float32)
    shared_act_grads = jnp.einsum(
        "td,fd->tf", cotangent, full_sdown, preferred_element_type=jnp.float32
    )
    shared_down_grad = jnp.einsum(
        "tf,td->fd", shared_act, cotangent, preferred_element_type=jnp.float32
    )
    shared_slope = shared_sig * (1.0 + shared_pre * (1.0 - shared_sig))
    shared_pre_grads = (shared_act_grads * shared_lin * shared_slope).astype(jnp.bfloat16)
    shared_lin_grads = (shared_act_grads * shared_pre * shared_sig).astype(jnp.bfloat16)
    shared_gate_grad = jnp.einsum(
        "td,tf->df", mlp_in, shared_pre_grads, preferred_element_type=jnp.float32
    )
    shared_up_grad = jnp.einsum(
        "td,tf->df", mlp_in, shared_lin_grads, preferred_element_type=jnp.float32
    )
    shared_in_part = jnp.einsum(
        "tf,df->td", shared_pre_grads, full_sgate, preferred_element_type=jnp.float32
    ) + jnp.einsum("tf,df->td", shared_lin_grads, full_sup, preferred_element_type=jnp.float32)
    rows_back, shared_in_grad = bring_back(rows_part.reshape(-1, D), shared_in_part)
    routed_in_grad = jnp.sum(
        rows_back[destination].reshape(local_tokens, TOP, D).astype(jnp.float32), axis=1
    )
    prob_grads = jnp.sum(chosen_float * gate_grads[:, :, None], axis=1)
    logit_grads = router_probs * (
        prob_grads - jnp.sum(router_probs * prob_grads, axis=-1, keepdims=True)
    )
    router_float = full_router.astype(jnp.float32)
    router_in_grad = jnp.einsum("te,de->td", logit_grads, router_float, precision=PRECISE)
    router_weight_grad = jnp.einsum(
        "td,te->de", mlp_in.astype(jnp.float32), logit_grads, precision=PRECISE
    )
    mlp_in_grad = router_in_grad + shared_in_grad + routed_in_grad
    gain_two_grad = jnp.sum(mlp_in_grad * unit_two, axis=0)
    scaled_two = mlp_in_grad * gain_two
    hidden_grad = grad_out + inv_two * (
        scaled_two - unit_two * jnp.mean(scaled_two * unit_two, axis=-1, keepdims=True)
    )
    out_grad = hidden_grad.astype(jnp.bfloat16)
    output_weight_grad = jnp.einsum(
        "tc,td->cd", attended, out_grad, preferred_element_type=jnp.float32
    )
    attended_grad = (
        jnp.einsum("td,cd->tc", out_grad, full_output, preferred_element_type=jnp.float32)
        .astype(jnp.bfloat16)
        .reshape(local_tokens, heads_here, HD)
    )
    probs_again = jnp.exp(masked_scores() - log_total)
    value_terms = jnp.einsum(
        "hqk,qhd->khd",
        probs_again.astype(jnp.bfloat16),
        attended_grad,
        preferred_element_type=jnp.float32,
    )
    prob_grad = jnp.einsum(
        "qhd,khd->hqk", attended_grad, values_all, preferred_element_type=jnp.float32
    )
    score_grads = (
        probs_again * (prob_grad - jnp.sum(probs_again * prob_grad, axis=-1, keepdims=True))
    ).astype(jnp.bfloat16)
    query_grads = (
        jnp.einsum("hqk,khd->qhd", score_grads, keys_all, preferred_element_type=jnp.float32)
        * score_scale
    ).astype(jnp.bfloat16)
    key_terms = (
        jnp.einsum("hqk,qhd->khd", score_grads, queries, preferred_element_type=jnp.float32)
        * score_scale
    )
    key_sum, value_sum = tuple(
        (
            part.astype(jnp.float32)
            for part in side_by_side(
                (
                    key_terms.reshape(seq_len, head_cols).astype(jnp.bfloat16),
                    value_terms.reshape(seq_len, head_cols).astype(jnp.bfloat16),
                ),
                ("sp", "ctx"),
                0,
                1,
            )
        )
    )
    query_in = (
        rotate(query_grads, cosine, sine_part, -1.0)
        .astype(jnp.bfloat16)
        .reshape(local_tokens, head_cols)
    )
    key_in = (
        rotate(
            key_sum.astype(jnp.bfloat16).reshape(local_tokens, heads_here, HD),
            cosine,
            sine_part,
            -1.0,
        )
        .astype(jnp.bfloat16)
        .reshape(local_tokens, head_cols)
    )
    value_in = value_sum.astype(jnp.bfloat16)
    query_weight_grad = jnp.einsum(
        "td,tc->dc", normed, query_in, preferred_element_type=jnp.float32
    )
    key_weight_grad = jnp.einsum("td,tc->dc", normed, key_in, preferred_element_type=jnp.float32)
    value_weight_grad = jnp.einsum(
        "td,tc->dc", normed, value_in, preferred_element_type=jnp.float32
    )
    normed_part = (
        jnp.einsum("tc,dc->td", query_in, full_query, preferred_element_type=jnp.float32)
        + jnp.einsum("tc,dc->td", key_in, full_key, preferred_element_type=jnp.float32)
        + jnp.einsum("tc,dc->td", value_in, full_value, preferred_element_type=jnp.float32)
    )
    normed_grad = taken_together(normed_part.astype(jnp.bfloat16), "wa").astype(jnp.float32)
    gain_one_grad = jnp.sum(normed_grad * unit_one, axis=0)
    scaled_one = normed_grad * gain_one
    tokens_grad = (
        hidden_grad
        + inv_one
        * (scaled_one - unit_one * jnp.mean(scaled_one * unit_one, axis=-1, keepdims=True))
    ).astype(jnp.bfloat16)
    reduced = (
        *tuple(
            (
                part.astype(jnp.float32)
                for part in side_by_side_2(
                    (
                        gain_one_grad.astype(jnp.bfloat16),
                        query_weight_grad.astype(jnp.bfloat16),
                        key_weight_grad.astype(jnp.bfloat16),
                        value_weight_grad.astype(jnp.bfloat16),
                    ),
                    ("sp", "ctx"),
                    0,
                    1,
                )
            )
        ),
        lax.psum_scatter(
            output_weight_grad.astype(jnp.bfloat16), ("sp", "ctx"), scatter_dimension=1, tiled=True
        ).astype(jnp.float32),
        *tuple(
            (
                part.astype(jnp.float32)
                for part in side_by_side_2(
                    (
                        gain_two_grad.astype(jnp.bfloat16),
                        router_weight_grad.astype(jnp.bfloat16),
                        shared_gate_grad.astype(jnp.bfloat16),
                        shared_up_grad.astype(jnp.bfloat16),
                    ),
                    ("sp", "ctx"),
                    0,
                    1,
                )
            )
        ),
        lax.psum_scatter(
            shared_down_grad.astype(jnp.bfloat16), ("sp", "ctx"), scatter_dimension=1, tiled=True
        ).astype(jnp.float32),
    )
    return (
        block_out,
        tokens_grad,
        reduced[0],
        reduced[1],
        reduced[2],
        reduced[3],
        reduced[4],
        reduced[5],
        reduced[6],
        reduced[7],
        reduced[8],
        reduced[9],
        expert_gate_grad,
        expert_up_grad,
        expert_down_grad,
    )


def solution(mesh):
    placed = (
        P(("sp", "ctx"), None),
        P(("sp", "ctx"), None),
        P(("sp", "ctx"), None),
        P(("sp", "ctx")),
        P(("sp", "ctx"), "wa"),
        P(("sp", "ctx"), "wa"),
        P(("sp", "ctx"), "wa"),
        P("wa", ("sp", "ctx")),
        P(("sp", "ctx")),
        P(("sp", "ctx"), None),
        P(("sp", "ctx"), "wa"),
        P(("sp", "ctx"), "wa"),
        P("wa", ("sp", "ctx")),
        P(("sp", "ctx"), None, "wa"),
        P(("sp", "ctx"), None, "wa"),
        P(("sp", "ctx"), "wa", None),
    )
    return jax.shard_map(
        shards,
        mesh=mesh,
        in_specs=placed,
        out_specs=(
            P(("sp", "ctx"), None),
            P(("sp", "ctx"), None),
            P(("sp", "ctx")),
            P(("sp", "ctx"), "wa"),
            P(("sp", "ctx"), "wa"),
            P(("sp", "ctx"), "wa"),
            P("wa", ("sp", "ctx")),
            P(("sp", "ctx")),
            P(("sp", "ctx"), None),
            P(("sp", "ctx"), "wa"),
            P(("sp", "ctx"), "wa"),
            P("wa", ("sp", "ctx")),
            P(("sp", "ctx"), None, "wa"),
            P(("sp", "ctx"), None, "wa"),
            P(("sp", "ctx"), "wa", None),
        ),
        check_vma=False,
    )
```

profile of v0, /device:TPU:1, one launch (start us, length us, event | category | flops | bytes accessed | tf_op | source)
XLA Modules:
  0.0 1938.7 jit_solution(9596637014842112212)
XLA Ops:
  13.9 164.0 %all-gather.7.cloned.1.call-done = bf16[2048,4226]{1,0:T(8,128)(2,1)} async-done(((bf16[64,4226]{1,0:T(8,128)(2,1)}), bf16[2048,4226]{1,0:T(8,128)(2,1)}) %all-gather.7.cloned.1.call-update) | async-done | bytes 17309712 | tf_op jit(solution)/shard_map/all_gather | solution.py:30
  179.7 3.5 fusion.57
  198.7 100.1 %all-gather.9.cloned.1.call-done = bf16[4096,1024]{1,0:T(8,128)(2,1)} async-done(((bf16[128,1024]{1,0:T(8,128)(2,1)}), bf16[4096,1024]{1,0:T(8,128)(2,1)}) %all-gather.9.cloned.1.call-update) | async-done | bytes 8388624 | tf_op jit(solution)/shard_map/all_gather | solution.py:43
  298.9 6.0 slice_bitcast_fusion
  304.9 6.3 copy.293
  311.2 4.7 fusion.136
  329.0 5.7 all-to-all-start
  338.1 5.4 mul.424
  343.5 8.3 mul.438
  353.1 4.4 reduce-window.6
  369.5 4.1 scatter_custom_fusion
  374.2 9.3 scatter_custom_fusion.1
  395.4 6.2 gather_fusion
  401.7 4.8 multiply_convert_fusion.2
  406.5 11.1 gather_fusion.2
  420.5 22.7 %all_to_all.68 = bf16[32,32,512]{2,1,0:T(8,128)(2,1)} all-to-all(bf16[32,32,512]{2,1,0:T(8,128)(2,1)S(1)} %bitcast.196), channel_id=1, replica_groups=mesh['sp'=4,'ctx'=8,'wa'=4] {'sp','ctx'}, dimensions={0} | all-to-all | bytes 2097152 | tf_op jit(solution)/shard_map/all_to_all | solution.py:89
  443.4 42.8 %all_to_all.69 = bf16[32,32,512]{2,1,0:T(8,128)(2,1)} all-to-all(bf16[32,32,512]{2,1,0:T(8,128)(2,1)} %bitcast.195), channel_id=1, replica_groups=mesh['sp'=4,'ctx'=8,'wa'=4] {'sp','ctx'}, dimensions={0} | all-to-all | bytes 2097152 | tf_op jit(solution)/shard_map/all_to_all | solution.py:89
  486.2 14.2 all-gather.11.cloned.1.call-done
  500.4 6.7 fusion.16
  507.1 3.5 fusion.14
  510.5 38.7 %all-gather.15.cloned.1.call-done = bf16[1024,2048]{1,0:T(8,128)(2,1)} async-done(((bf16[1024,512]{1,0:T(8,128)(2,1)}), bf16[1024,2048]{1,0:T(8,128)(2,1)}) %all-gather.15.cloned.1.call-update) | async-done | bytes 4194320 | tf_op jit(solution)/shard_map/all_gather | solution.py:90
  549.3 6.8 fusion.67
  563.5 3.5 convert_bitcast_fusion
  569.3 40.3 %reduce-scatter.16.cloned.1.call-done = bf16[1024,512]{1,0:T(8,128)(2,1)} async-done(((bf16[1024,2048]{1,0:T(8,128)(2,1)}), bf16[1024,512]{1,0:T(8,128)(2,1)}) %reduce-scatter.16.cloned.1.call-update) | async-done | bytes 1048592 | tf_op jit(solution)/shard_map/reduce_scatter | solution.py:94
  609.6 34.1 %all_to_all.70 = bf16[32,32,512]{2,1,0:T(8,128)(2,1)} all-to-all(bf16[32,32,512]{2,1,0:T(8,128)(2,1)} %bitcast.204), channel_id=1, replica_groups=mesh['sp'=4,'ctx'=8,'wa'=4] {'sp','ctx'}, dimensions={0} | all-to-all | bytes 2097152 | tf_op jit(solution)/shard_map/all_to_all | solution.py:97
  643.8 22.4 %reduce-scatter.14.cloned.1.call-done = bf16[1024,512]{1,0:T(8,128)(2,1)} async-done(((bf16[1024,2048]{1,0:T(8,128)(2,1)}), bf16[1024,512]{1,0:T(8,128)(2,1)}) %reduce-scatter.14.cloned.1.call-update) | async-done | bytes 1048592 | tf_op jit(solution)/shard_map/reduce_scatter | solution.py:94
  666.2 33.4 %all_to_all.71 = bf16[32,32,512]{2,1,0:T(8,128)(2,1)} all-to-all(bf16[32,32,512]{2,1,0:T(8,128)(2,1)} %bitcast.203), channel_id=1, replica_groups=mesh['sp'=4,'ctx'=8,'wa'=4] {'sp','ctx'}, dimensions={0} | all-to-all | bytes 2097152 | tf_op jit(solution)/shard_map/all_to_all | solution.py:97
  699.6 4.0 fusion.78
  703.6 4.8 fusion.35
  708.4 5.5 multiply_convert_fusion.5
  714.0 3.7 fusion.33
  717.7 3.6 fusion.45
  722.9 7.9 all-to-all-start.4
  730.9 4.4 fusion.49
  735.3 36.5 %all-to-all-done.4 = bf16[4,128,2048]{2,1,0:T(8,128)(2,1)S(1)} async-done(((bf16[4,128,2048]{2,1,0:T(8,128)(2,1)}), bf16[4,128,2048]{2,1,0:T(8,128)(2,1)S(1)}, u32[]{:S(2)}, u32[]{:S(2)}) %all-to-all-start.4) | async-done | bytes 2097184 | tf_op jit(solution)/shard_map/all_to_all | solution.py:19
  774.4 6.2 all-to-all-start.3
  783.6 28.6 %all-to-all-done.3 = bf16[4,128,2048]{2,1,0:T(8,128)(2,1)} async-done(((bf16[4,128,2048]{2,1,0:T(8,128)(2,1)}), bf16[4,128,2048]{2,1,0:T(8,128)(2,1)}, u32[]{:S(2)}, u32[]{:S(2)}) %all-to-all-start.3) | async-done | bytes 2097184 | tf_op jit(solution)/shard_map/all_to_all | solution.py:19
  815.3 9.8 gather_fusion.3
  825.2 6.5 reshape.343
  831.7 9.8 gather_fusion.1
  841.5 6.6 reshape.342
  848.2 7.4 multiply_reduce_fusion.1
  855.8 7.1 reduce_sum.196
  870.3 6.9 convolution_convert_fusion
  877.2 4.9 multiply_reduce_fusion
  884.5 3.4 multiply_convert_fusion
  887.9 7.8 pad_maximum_fusion
  895.7 11.9 copy.271
  915.3 3.4 convolution_convert_fusion.2
  919.9 29.9 %concatenate.39 = bf16[2048,1473]{0,1:T(8,128)(2,1)} concatenate(bf16[2048,1]{0,1:T(2,128)(2,1)S(1)} %convert_element_type.389, bf16[2048,64]{0,1:T(8,128)(2,1)} %convolution_convert_fusion.9, bf16[2048,704]{0,1:T(8,128)(2,1)S(1)} %convolution_convert_fusion.3, bf16[2048,704]{0,1:T(8,128)(2,1)} %convolution_convert_fusion.2), dimensions={1} | concatenate | bytes 12066816 | tf_op jit(solution)/shard_map/concatenate | solution.py:56
  949.7 8.6 copy.275
  958.4 4.8 fusion.91
  963.2 120.1 %reduce-scatter.22.cloned.1.call-done = bf16[128,1024]{1,0:T(8,128)(2,1)} async-done(((bf16[4096,1024]{1,0:T(8,128)(2,1)}), bf16[128,1024]{1,0:T(8,128)(2,1)}) %reduce-scatter.22.cloned.1.call-update) | async-done | bytes 262160
  1095.6 28.6 %all-to-all-start.7 = ((bf16[4,128,2048]{2,1,0:T(8,128)(2,1)}), bf16[4,128,2048]{2,1,0:T(8,128)(2,1)}, u32[]{:S(2)}, u32[]{:S(2)}) async-start(bf16[4,128,2048]{2,1,0:T(8,128)(2,1)} %broadcast_in_dim.41), calls=%async_computation.9 | async-start | bytes 4194304 | tf_op jit(solution)/shard_map/all_to_all | solution.py:19
  1130.9 19.7 %all-to-all-done.7 = bf16[4,128,2048]{2,1,0:T(8,128)(2,1)} async-done(((bf16[4,128,2048]{2,1,0:T(8,128)(2,1)}), bf16[4,128,2048]{2,1,0:T(8,128)(2,1)}, u32[]{:S(2)}, u32[]{:S(2)}) %all-to-all-start.7) | async-done | bytes 2097184 | tf_op jit(solution)/shard_map/all_to_all | solution.py:19
  1153.1 36.7 %concatenate.38 = bf16[2048,1537]{0,1:T(8,128)(2,1)} concatenate(bf16[2048,1]{0,1:T(2,128)(2,1)S(1)} %convert_element_type.377, bf16[2048,512]{0,1:T(8,128)(2,1)} %convolution_convert_fusion.6, bf16[2048,512]{0,1:T(8,128)(2,1)} %convolution_convert_fusion.5, bf16[2048,512]{0,1:T(8,128)(2,1)} %convolution_convert_fusion.4), dimensions={1} | concatenate | bytes 12591104 | tf_op jit(solution)/shard_map/concatenate | solution.py:56
  1189.8 9.4 copy.273
  1199.2 131.0 %reduce-scatter.20.cloned.1.call-done = bf16[704,64]{0,1:T(8,128)(2,1)} async-done(((bf16[704,2048]{0,1:T(8,128)(2,1)}), bf16[704,64]{0,1:T(8,128)(2,1)}) %reduce-scatter.20.cloned.1.call-update) | async-done | bytes 90128 | tf_op jit(solution)/shard_map/reduce_scatter | solution.py:438
  1331.8 6.6 convolution_bitcast_fusion.1
  1338.4 4.3 convolution_bitcast_fusion
  1342.7 4.3 fusion.18
  1347.0 147.9 %reduce-scatter.18.cloned.1.call-done = bf16[512,64]{0,1:T(8,128)(2,1)} async-done(((bf16[512,2048]{0,1:T(8,128)(2,1)}), bf16[512,64]{0,1:T(8,128)(2,1)}) %reduce-scatter.18.cloned.1.call-update) | async-done | bytes 65552 | tf_op jit(solution)/shard_map/reduce_scatter | solution.py:419
  1496.3 252.4 %reduce-scatter.26.cloned.1.call-done = bf16[64,1473]{1,0:T(8,128)(2,1)} async-done(((bf16[2048,1473]{1,0:T(8,128)(2,1)}), bf16[64,1473]{1,0:T(8,128)(2,1)}) %reduce-scatter.26.cloned.1.call-update) | async-done | bytes 188560
  1762.0 164.6 %reduce-scatter.24.cloned.1.call-done = bf16[64,1537]{1,0:T(8,128)(2,1)} async-done(((bf16[2048,1537]{1,0:T(8,128)(2,1)}), bf16[64,1537]{1,0:T(8,128)(2,1)}) %reduce-scatter.24.cloned.1.call-update) | async-done | bytes 196752
  (289 shorter events, 150.4 us)
Async XLA Ops:
  7.2 542.1 %copy-start = (bf16[2,352,2048]{2,1,0:T(8,128)(2,1)S(1)}, bf16[2,352,2048]{2,1,0:T(8,128)(2,1)}, u32[]{:S(2)}) copy-start(bf16[2,352,2048]{2,1,0:T(8,128)(2,1)} %param.31) | copy-start | bytes 8650756
  7.2 177.8 %copy-start.4 = (bf16[128,2048]{1,0:T(8,128)(2,1)S(1)}, bf16[128,2048]{1,0:T(8,128)(2,1)}, u32[]{:S(2)}) copy-start(bf16[128,2048]{1,0:T(8,128)(2,1)} %param.16) | copy-start | bytes 1572868
  7.2 170.8 %all-gather.7.cloned.1.call-start = ((), (), s32[]{:S(2)}) async-start(), calls=%async_computation.15 | async-start | bytes 18382848 | tf_op jit(solution)/shard_map/all_gather | solution.py:30
  11.1 287.7 %all-gather.9.cloned.1.call-start = ((), (), s32[]{:S(2)}) async-start(), calls=%async_computation.16 | async-start | bytes 8650752 | tf_op jit(solution)/shard_map/all_gather | solution.py:43
  12.9 175.4 %copy-start.53 = (f32[128]{0:T(128)}, f32[128]{0:T(128)S(1)}, u32[]{:S(2)}) copy-start(f32[128]{0:T(128)S(1)} %add_rsqrt_fusion.1) | copy-start | bytes 1540
  179.7 13.8 copy-start.43
  315.9 5.2 copy-start.11
  317.2 6.7 copy-start.58
  324.5 10.3 copy-start.47
  329.0 55.8 %all-to-all-start = ((bf16[4,128,2048]{2,1,0:T(8,128)(2,1)}), bf16[4,128,2048]{2,1,0:T(8,128)(2,1)}, u32[]{:S(2)}, u32[]{:S(2)}) async-start(bf16[4,128,2048]{2,1,0:T(8,128)(2,1)} %broadcast_in_dim.34), calls=%async_computation | async-start | bytes 4194304 | tf_op jit(solution)/shard_map/all_to_all | solution.py:19
  334.8 165.6 %all-gather.11.cloned.1.call-start = ((), (), s32[]{:S(2)}) async-start(), calls=%async_computation.17 | async-start | bytes 5242880 | tf_op jit(solution)/shard_map/all_gather | solution.py:90
  368.9 5.3 copy-start.51
  443.3 106.0 %all-gather.15.cloned.1.call-start = ((), (), s32[]{:S(2)}) async-start(), calls=%async_computation.20 | async-start | bytes 5242880 | tf_op jit(solution)/shard_map/all_gather | solution.py:90
  486.1 123.5 %reduce-scatter.16.cloned.1.call-start = ((), (), s32[]{:S(2)}) async-start(), calls=%async_computation.21 | async-start | bytes 5242880 | tf_op jit(solution)/shard_map/reduce_scatter | solution.py:94
  500.4 6.7 copy-start.9
  500.4 6.7 copy-start.24
  549.3 6.8 copy-start.23
  563.4 102.8 %reduce-scatter.14.cloned.1.call-start = ((), (), s32[]{:S(2)}) async-start(), calls=%async_computation.18 | async-start | bytes 5242880 | tf_op jit(solution)/shard_map/reduce_scatter | solution.py:94
  569.2 130.4 %copy-start.14 = (bf16[128,2048]{1,0:T(8,128)(2,1)S(1)}, bf16[128,2048]{1,0:T(8,128)(2,1)}, u32[]{:S(2)}) copy-start(bf16[128,2048]{1,0:T(8,128)(2,1)} %param.17) | copy-start | bytes 1572868
  569.2 246.1 %all-gather.17.cloned.1.call-start = ((), (), s32[]{:S(2)}) async-start(), calls=%async_computation.22 | async-start | bytes 5242880 | tf_op jit(solution)/shard_map/all_gather | solution.py:98
  643.7 188.0 %all-gather.13.cloned.1.call-start = ((), (), s32[]{:S(2)}) async-start(), calls=%async_computation.19 | async-start | bytes 5242880 | tf_op jit(solution)/shard_map/all_gather | solution.py:98
  714.0 7.4 copy-start.27
  714.0 7.4 copy-start.28
  722.9 7.9 copy-start.29
  722.9 48.8 %all-to-all-start.4 = ((bf16[4,128,2048]{2,1,0:T(8,128)(2,1)}), bf16[4,128,2048]{2,1,0:T(8,128)(2,1)S(1)}, u32[]{:S(2)}, u32[]{:S(2)}) async-start(bf16[4,128,2048]{2,1,0:T(8,128)(2,1)} %broadcast_in_dim.39), calls=%async_computation.5 | async-start | bytes 4194304 | tf_op jit(solution)/shard_map/all_to_all | solution.py:19
  735.3 46.4 %copy-start.52 = (s32[768]{0:T(1024)S(1)}, s32[768]{0:T(1024)}, u32[]{:S(2)}) copy-start(s32[768]{0:T(1024)} %copy-done.51) | copy-start | bytes 9220
  735.3 46.4 %copy-start.50 = (f32[4,128]{1,0:T(4,128)S(1)}, f32[4,128]{1,0:T(4,128)}, u32[]{:S(2)}) copy-start(f32[4,128]{1,0:T(4,128)} %copy-done.49) | copy-start | bytes 6148
  735.3 46.4 %copy-start.59 = (f32[4,128]{1,0:T(4,128)S(1)}, f32[4,128]{1,0:T(4,128)}, u32[]{:S(2)}) copy-start(f32[4,128]{1,0:T(4,128)} %copy-done.58) | copy-start | bytes 6148
  774.4 37.9 %all-to-all-start.3 = ((bf16[4,128,2048]{2,1,0:T(8,128)(2,1)}), bf16[4,128,2048]{2,1,0:T(8,128)(2,1)}, u32[]{:S(2)}, u32[]{:S(2)}) async-start(bf16[4,128,2048]{2,1,0:T(8,128)(2,1)} %broadcast_in_dim.38), calls=%async_computation.4 | async-start | bytes 4194304 | tf_op jit(solution)/shard_map/all_to_all | solution.py:19
  780.6 302.7 %reduce-scatter.22.cloned.1.call-start = ((), (), s32[]{:S(2)}) async-start(), calls=%async_computation.25 | async-start | bytes 8650752
  841.5 6.6 copy-start.17
  841.5 6.6 copy-start.35
  848.1 7.6 copy-start.42
  848.1 7.6 copy-start.57
  848.1 7.6 copy-start.61
  855.7 7.2 copy-start.39
  855.8 7.2 copy-start.62
  855.8 7.2 copy-start.8
  855.8 7.2 copy-start.15
  855.8 7.2 copy-start.37
  855.8 7.2 copy-start.65
  867.1 44.2 %copy-start.6 = (f32[128,2048]{1,0:T(8,128)}, f32[128,2048]{1,0:T(8,128)S(1)}, u32[]{:S(2)}) copy-start(f32[128,2048]{1,0:T(8,128)S(1)} %get-tuple-element.120) | copy-start | bytes 3145732
  870.2 6.9 copy-start.12
  870.2 11.8 slice-start
  907.7 422.5 %reduce-scatter.20.cloned.1.call-start = ((), (), s32[]{:S(2)}) async-start(), calls=%async_computation.24 | async-start | bytes 3244032 | tf_op jit(solution)/shard_map/reduce_scatter | solution.py:438
  911.3 583.5 %reduce-scatter.18.cloned.1.call-start = ((), (), s32[]{:S(2)}) async-start(), calls=%async_computation.23 | async-start | bytes 2162688 | tf_op jit(solution)/shard_map/reduce_scatter | solution.py:419
  913.4 5.3 copy-start.38
  913.4 5.3 copy-start.40
  913.4 5.3 copy-start.63
  913.5 835.3 %reduce-scatter.26.cloned.1.call-start = ((), (), s32[]{:S(2)}) async-start(), calls=%async_computation.27 | async-start | bytes 6488064
  958.4 126.2 %copy-start.31 = (f32[128,64]{1,0:T(8,128)S(1)}, f32[128,64]{1,0:T(8,128)}, u32[]{:S(2)}) copy-start(f32[128,64]{1,0:T(8,128)} %get-tuple-element.152) | copy-start | bytes 98308
  958.4 126.2 %copy-start.32 = (f32[128,64]{1,0:T(8,128)S(1)}, f32[128,64]{1,0:T(8,128)}, u32[]{:S(2)}) copy-start(f32[128,64]{1,0:T(8,128)} %get-tuple-element.153) | copy-start | bytes 98308
  1085.1 6.1 copy-start.33
  1094.0 30.5 %copy-start.5 = (bf16[128,2048]{1,0:T(8,128)(2,1)S(1)}, bf16[128,2048]{1,0:T(8,128)(2,1)}, u32[]{:S(2)}) copy-start(bf16[128,2048]{1,0:T(8,128)(2,1)} %param.16) | copy-start | bytes 1572868
  1094.0 30.5 %copy-start.44 = (f32[2048]{0:T(1024)S(1)}, f32[2048]{0:T(1024)}, u32[]{:S(2)}) copy-start(f32[2048]{0:T(1024)} %copy-done.43) | copy-start | bytes 24580
  1094.0 30.5 %copy-start.55 = (f32[128]{0:T(128)S(1)}, f32[128]{0:T(128)}, u32[]{:S(2)}) copy-start(f32[128]{0:T(128)} %copy-done.53) | copy-start | bytes 1540
  1095.6 33.2 %copy-start.34 = (bf16[128,1024]{1,0:T(8,128)(2,1)S(1)}, bf16[128,1024]{1,0:T(8,128)(2,1)}, u32[]{:S(2)}) copy-start(bf16[128,1024]{1,0:T(8,128)(2,1)} %reduce-scatter.22.cloned.1.call-done) | copy-start | bytes 786436
  1095.6 55.0 %all-to-all-start.7 = ((bf16[4,128,2048]{2,1,0:T(8,128)(2,1)}), bf16[4,128,2048]{2,1,0:T(8,128)(2,1)}, u32[]{:S(2)}, u32[]{:S(2)}) async-start(bf16[4,128,2048]{2,1,0:T(8,128)(2,1)} %broadcast_in_dim.41), calls=%async_computation.9 | async-start | bytes 4194304 | tf_op jit(solution)/shard_map/all_to_all | solution.py:19
  1124.2 802.5 %reduce-scatter.24.cloned.1.call-start = ((), (), s32[]{:S(2)}) async-start(), calls=%async_computation.26 | async-start | bytes 7028736
  1152.7 37.1 %copy-start.13 = (f32[128,2048]{1,0:T(8,128)}, f32[128,2048]{1,0:T(8,128)S(1)}, u32[]{:S(2)}) copy-start(f32[128,2048]{1,0:T(8,128)S(1)} %convert_reduce_fusion) | copy-start | bytes 3145732
  1199.2 132.6 %copy-start.22 = (bf16[32,2,16,352]{3,2,0,1:T(8,128)(2,1)S(1)}, bf16[32,2,16,352]{3,2,0,1:T(8,128)(2,1)}, u32[]{:S(2)}) copy-start(bf16[32,2,16,352]{3,2,0,1:T(8,128)(2,1)} %copy-done.21) | copy-start | bytes 2162692
  1331.8 6.6 copy-start.10
  1331.8 6.6 copy-start.20
  1342.7 589.0 %copy-start.1 = (bf16[2,352,2048]{2,1,0:T(8,128)(2,1)S(1)}, bf16[2,352,2048]{2,1,0:T(8,128)(2,1)}, u32[]{:S(2)}) copy-start(bf16[2,352,2048]{2,1,0:T(8,128)(2,1)} %param.31) | copy-start | bytes 8650756
  (23 other events, 57.9 us)
Sparse Core Ops, SparseCore 0:
  11.8 166.1 all-gather.6
  197.0 101.7 all-gather.8
  443.4 56.8 all-gather.10
  501.9 47.3 all-gather.14
  563.5 46.0 reduce-scatter.15
  612.0 54.1 reduce-scatter.13
  667.9 55.0 all-gather.16
  724.6 72.0 all-gather.12
  907.8 175.3 reduce-scatter.21
  1088.6 241.5 reduce-scatter.19
  1332.6 162.1 reduce-scatter.17
  1500.6 248.0 reduce-scatter.25
  1751.3 175.3 reduce-scatter.23
where the time goes:
time: 1980 us; the launch traced here: 1940 us
  waiting for transfers between devices  1280 us (65%)
  local copies, waits for them, and re-layouts  246 us (12%)
  matrix products  140 us (7%)
  blocking collectives  133 us (7%)
  other arithmetic  74.5 us (4%)
  starting transfers between devices  49.4 us (2%)
    unnamed x16, waiting for transfers between devices  537 us
    all_gather x1, waiting for transfers between devices, turned_gather(): whole = lax.all_gather(both, axis, axis=0, tiled=True)  164 us
    reduce_scatter x1, waiting for transfers between devices, shards(): lax.psum_scatter(output_weight_grad.astype(jnp.bfloat16), ('sp', 'ctx'),...  148 us
    reduce_scatter x1, waiting for transfers between devices, shards(): lax.psum_scatter(shared_down_grad.astype(jnp.bfloat16), ('sp', 'ctx'), sc...  131 us
    all_gather x1, waiting for transfers between devices, in_one_piece(): whole = lax.all_gather(both, axis, axis=dim, tiled=True)  100 us
    all_to_all x4, waiting for transfers between devices, copy_for_each(): lax.all_to_all(jnp.broadcast_to(x[None], (size, *x.shape)), axis, 0, 0, t...  84.9 us
    all_to_all x2, blocking collectives, back_share(): lax.all_to_all(share, ('sp', 'ctx'), split_axis=0, concat_axis=0, tiled=T...  67.4 us
    concatenate x2, local copies, waits for them, and re-layouts, side_by_side_2(): both = jnp.concatenate(columns, axis=along)  66.5 us
  transfers between devices with their start and end apart: 17, of which 14 were waited for; matrix products, arithmetic and copies ran while one was open for 14% of the time, Pallas kernels for 0%

commit v1 on v0

--- a/solution.py
+++ b/solution.py
@@ -1,6 +1,10 @@
+import functools
+
 import jax
 import jax.numpy as jnp
 from jax import lax
+from jax.experimental import pallas as pl
+from jax.experimental.pallas import tpu as pltpu
 from jax.sharding import PartitionSpec as P
 
 D = 2048
@@ -14,13 +18,380 @@
 PRECISE = lax.Precision.HIGHEST
 
 
-def copy_for_each(x, axis):
-    size = lax.axis_size(axis)
-    return lax.all_to_all(jnp.broadcast_to(x[None], (size, *x.shape)), axis, 0, 0, tiled=True)
-
-
-def taken_together(x, axis):
-    return copy_for_each(x, axis).astype(jnp.float32).sum(axis=0)
+MESH = pl.DeviceIdType.MESH
+VMEM_LIMIT = 60 * 1024 * 1024
+
+ORDERS = (
+    (("z", "A"), ("z", "B"), ("y", "A"), ("y", "B")),
+    (("z", "B"), ("z", "A"), ("y", "B"), ("y", "A")),
+    (("y", "A"), ("y", "B"), ("z", "A"), ("z", "B")),
+    (("y", "B"), ("y", "A"), ("z", "B"), ("z", "A")),
+)
+
+
+def paired(i, kind):
+    return i + 1 - 2 * (i % 2) if kind == "A" else 3 - i
+
+
+def own_place():
+    c = lax.axis_index("ctx")
+    return lax.axis_index("sp"), c // 4, c % 4
+
+
+def neighbour(axis, kind):
+    z, xh, y = own_place()
+    if axis == "z":
+        return {"sp": paired(z, kind)}
+    if axis == "y":
+        return {"ctx": 4 * xh + paired(y, kind)}
+    return {"ctx": 4 * (1 - xh) + y}
+
+
+def greet_cube():
+    barrier = pltpu.get_barrier_semaphore()
+    for axis in ("z", "y"):
+        for kind in ("A", "B"):
+            pl.semaphore_signal(barrier, inc=1, device_id=neighbour(axis, kind), device_id_type=MESH)
+    pl.semaphore_signal(barrier, inc=1, device_id=neighbour("x", "A"), device_id_type=MESH)
+    pl.semaphore_wait(barrier, 5)
+
+
+def pair_slots(i, kind):
+    if kind == "A":
+        return [(pl.ds((i // 2) * 2, 2), pl.ds(0, 2))]
+    return [(pl.ds(i, 1), pl.ds(0, 1)), (pl.ds(3 - i, 1), pl.ds(1, 1))]
+
+
+def pair_members(i, kind):
+    if kind == "A":
+        return [(i // 2) * 2, (i // 2) * 2 + 1]
+    return [i, 3 - i]
+
+
+def slot_in_pair(i, kind):
+    return i % 2 if kind == "A" else 0
+
+
+def gather_kernel(parts, count, *refs):
+    ins, outs = refs[:count], refs[count : 2 * count]
+    send_sem, recv_sem, local_sem = refs[2 * count :]
+    z, xh, y = own_place()
+    used = [0]
+    started = []
+
+    def start(src, dst, where):
+        k = used[0]
+        used[0] += 1
+        copy = pltpu.make_async_remote_copy(
+            src_ref=src, dst_ref=dst, send_sem=send_sem.at[k], recv_sem=recv_sem.at[k],
+            device_id=where, device_id_type=MESH,
+        )
+        copy.start()
+        started.append(copy)
+        return copy
+
+    def step(lane, p, s):
+        ring1, ring2 = ORDERS[p][0][0], ORDERS[p][2][0]
+        axis, kind = ORDERS[p][s]
+        where = neighbour(axis, kind)
+        xl = xh if lane == 0 else 1 - xh
+        zs, ys = [pl.ds(z, 1)], [pl.ds(y, 1)]
+        full = [pl.ds(0, 4)]
+        if s == 1:
+            other = [d for d, _ in pair_slots(z if ring1 == "z" else y, ORDERS[p][0][1])]
+            zs, ys = (other, ys) if ring1 == "z" else (zs, other)
+        if s >= 2:
+            zs, ys = (full, ys) if ring1 == "z" else (zs, full)
+        if s == 3:
+            other = [d for d, _ in pair_slots(z if ring2 == "z" else y, ORDERS[p][2][1])]
+            zs, ys = (other, ys) if ring2 == "z" else (zs, other)
+        copies = []
+        for a, rows, cols in parts[p]:
+            for zd in zs:
+                for yd in ys:
+                    place = outs[a].at[zd, pl.ds(xl, 1), yd, rows, cols]
+                    copies.append(start(place, place, where))
+        return copies
+
+    greet_cube()
+    local = [
+        pltpu.make_async_copy(ins[a], outs[a].at[z, xh, y], local_sem.at[a]) for a in range(count)
+    ]
+    for copy in local:
+        copy.start()
+    across = [
+        [
+            start(ins[a].at[rows, cols], outs[a].at[z, xh, y, rows, cols], neighbour("x", "A"))
+            for a, rows, cols in part
+        ]
+        for part in parts
+    ]
+    for copy in local:
+        copy.wait()
+    flying = {}
+
+    def advance(lane, s):
+        for p in range(4):
+            if s == 0 and lane == 1:
+                for copy in across[p]:
+                    copy.wait_recv()
+            if s > 0:
+                for copy in flying[lane, p]:
+                    copy.wait_recv()
+            flying[lane, p] = step(lane, p, s) if s < 4 else []
+
+    advance(0, 0)
+    advance(0, 1)
+    advance(1, 0)
+    advance(0, 2)
+    advance(1, 1)
+    advance(0, 3)
+    advance(1, 2)
+    advance(1, 3)
+    advance(0, 4)
+    advance(1, 4)
+    for copy in started:
+        copy.wait_send()
+
+
+def gather_cube(arrays, parts, collective_id, name):
+    count = len(arrays)
+    copies = 11 * sum(len(part) for part in parts)
+    return pl.pallas_call(
+        functools.partial(gather_kernel, parts, count),
+        out_shape=[jax.ShapeDtypeStruct((4, 2, 4, *a.shape), a.dtype) for a in arrays],
+        in_specs=[pl.BlockSpec(memory_space=pl.ANY)] * count,
+        out_specs=[pl.BlockSpec(memory_space=pl.ANY)] * count,
+        scratch_shapes=[
+            pltpu.SemaphoreType.DMA((copies,)),
+            pltpu.SemaphoreType.DMA((copies,)),
+            pltpu.SemaphoreType.DMA((count,)),
+        ],
+        compiler_params=pltpu.CompilerParams(collective_id=collective_id, has_side_effects=True),
+        name=name,
+    )(*arrays)
+
+
+def reduce_kernel(parts, count, *refs):
+    entries = [(p, *entry) for p in range(4) for entry in parts[p]]
+    size = 5 * len(entries)
+    ins, outs = refs[:count], refs[count : 2 * count]
+    bufs = refs[2 * count : 2 * count + size]
+    send_sem, recv_sem = refs[2 * count + size :]
+    z, xh, y = own_place()
+    used = [0]
+    started = []
+    flying = {}
+
+    def start(src, dst, where):
+        k = used[0]
+        used[0] += 1
+        copy = pltpu.make_async_remote_copy(
+            src_ref=src, dst_ref=dst, send_sem=send_sem.at[k], recv_sem=recv_sem.at[k],
+            device_id=where, device_id_type=MESH,
+        )
+        copy.start()
+        started.append(copy)
+        return copy
+
+    def first(lane, e):
+        p, a, rows, cols = entries[e]
+        ring2, near = ORDERS[p][2]
+        axis, kind = ORDERS[p][3]
+        xl = xh if lane == 0 else 1 - xh
+        theirs = paired(z if ring2 == "z" else y, kind)
+        copies = []
+        for src, dst in pair_slots(theirs, near):
+            if ring2 == "z":
+                block, place = ins[a].at[src, xl, :, rows, cols], bufs[5 * e].at[lane, dst]
+            else:
+                block, place = ins[a].at[:, xl, src, rows, cols], bufs[5 * e].at[lane, :, dst]
+            copies.append(start(block, place, neighbour(axis, kind)))
+        flying[lane, e] = copies
+
+    def second(lane, e):
+        p, a, rows, cols = entries[e]
+        ring2 = ORDERS[p][2][0]
+        axis, kind = ORDERS[p][2]
+        xl = xh if lane == 0 else 1 - xh
+        mine = z if ring2 == "z" else y
+        buf = bufs[5 * e]
+        for copy in flying[lane, e]:
+            copy.wait_recv()
+        slot = slot_in_pair(mine, kind)
+
+        def add(j, place):
+            def one(i, carry):
+                if ring2 == "z":
+                    buf[lane, j, i] = buf[lane, j, i] + ins[a][place, xl, i, rows, cols]
+                else:
+                    buf[lane, i, j] = buf[lane, i, j] + ins[a][i, xl, place, rows, cols]
+                return carry
+
+            lax.fori_loop(0, 4, one, 0)
+
+        add(1 - slot, paired(mine, kind))
+        half = buf.at[lane, 1 - slot] if ring2 == "z" else buf.at[lane, :, 1 - slot]
+        flying[lane, e] = [start(half, bufs[5 * e + 1].at[lane], neighbour(axis, kind))]
+        add(slot, mine)
+
+    def third(lane, e):
+        p = entries[e][0]
+        ring1, ring2 = ORDERS[p][0][0], ORDERS[p][2][0]
+        axis, kind = ORDERS[p][1]
+        before, buf = bufs[5 * e], bufs[5 * e + 1]
+        for copy in flying[lane, e]:
+            copy.wait_recv()
+        slot = slot_in_pair(z if ring2 == "z" else y, ORDERS[p][2][1])
+
+        def one(i, carry):
+            other = before[lane, slot, i] if ring2 == "z" else before[lane, i, slot]
+            buf[lane, i] = buf[lane, i] + other
+            return carry
+
+        lax.fori_loop(0, 4, one, 0)
+        theirs = paired(z if ring1 == "z" else y, kind)
+        flying[lane, e] = [
+            start(buf.at[lane, src], bufs[5 * e + 2].at[lane, dst], neighbour(axis, kind))
+            for src, dst in pair_slots(theirs, ORDERS[p][0][1])
+        ]
+
+    def fourth(lane, e):
+        p = entries[e][0]
+        ring1 = ORDERS[p][0][0]
+        axis, kind = ORDERS[p][0]
+        mine = z if ring1 == "z" else y
+        before, buf = bufs[5 * e + 1], bufs[5 * e + 2]
+        for copy in flying[lane, e]:
+            copy.wait_recv()
+        slot = slot_in_pair(mine, kind)
+        buf[lane, 1 - slot] = buf[lane, 1 - slot] + before[lane, paired(mine, kind)]
+        flying[lane, e] = [
+            start(buf.at[lane, 1 - slot], bufs[5 * e + 3].at[lane], neighbour(axis, kind))
+        ]
+        buf[lane, slot] = buf[lane, slot] + before[lane, mine]
+
+    def last(lane, e):
+        p, a, rows, cols = entries[e]
+        ring1 = ORDERS[p][0][0]
+        before, buf = bufs[5 * e + 2], bufs[5 * e + 3]
+        for copy in flying[lane, e]:
+            copy.wait_recv()
+        slot = slot_in_pair(z if ring1 == "z" else y, ORDERS[p][0][1])
+        if lane == 1:
+            buf[1] = buf[1] + before[1, slot]
+            flying["x", e] = start(buf.at[1], bufs[5 * e + 4], neighbour("x", "A"))
+        else:
+            flying["x", e].wait_recv()
+            total = (
+                buf[0].astype(jnp.float32)
+                + before[0, slot].astype(jnp.float32)
+                + bufs[5 * e + 4][...].astype(jnp.float32)
+            )
+            outs[a][rows, cols] = total.astype(outs[a].dtype)
+
+    greet_cube()
+    for stage in (first, second, third, fourth, last):
+        for lane in (1, 0):
+            for e in range(len(entries)):
+                stage(lane, e)
+    for copy in started:
+        copy.wait_send()
+
+
+def reduce_cube(arrays, parts, collective_id, name, dtype=jnp.float32):
+    count = len(arrays)
+    scratch = []
+    for p in range(4):
+        pair = (2, 4) if ORDERS[p][2][0] == "z" else (4, 2)
+        for a, rows, cols in parts[p]:
+            for lead in ((2, *pair), (2, 4), (2, 2), (2,), ()):
+                scratch.append(pltpu.VMEM((*lead, rows.size, cols.size), arrays[a].dtype))
+    copies = 13 * sum(len(part) for part in parts)
+    return pl.pallas_call(
+        functools.partial(reduce_kernel, parts, count),
+        out_shape=[jax.ShapeDtypeStruct(a.shape[3:], dtype) for a in arrays],
+        in_specs=[pl.BlockSpec(memory_space=pltpu.VMEM)] * count,
+        out_specs=[pl.BlockSpec(memory_space=pltpu.VMEM)] * count,
+        scratch_shapes=scratch
+        + [pltpu.SemaphoreType.DMA((copies,)), pltpu.SemaphoreType.DMA((copies,))],
+        compiler_params=pltpu.CompilerParams(
+            collective_id=collective_id, has_side_effects=True, vmem_limit_bytes=VMEM_LIMIT
+        ),
+        name=name,
+    )(*arrays)
+
+
+def row_parts(arrays):
+    parts = []
+    for p in range(4):
+        part = []
+        for a, array in enumerate(arrays):
+            rows, columns = array.shape[-2:]
+            part.append((a, pl.ds(p * rows // 4, rows // 4), pl.ds(0, columns)))
+        parts.append(part)
+    return parts
+
+
+def whole_parts(arrays):
+    return [[(a, pl.ds(0, x.shape[-2]), pl.ds(0, x.shape[-1]))] for a, x in enumerate(arrays)]
+
+
+def half_parts(arrays):
+    return [
+        [(a, pl.ds(0, x.shape[-2]), pl.ds(h * x.shape[-1] // 2, x.shape[-1] // 2))]
+        for a, x in enumerate(arrays)
+        for h in range(2)
+    ]
+
+
+def sum_wa_kernel(x, out, half, got, far, send_sem, recv_sem):
+    w = lax.axis_index("wa")
+    core = w % 2
+    beside = {"wa": w + 1 - 2 * core}
+    across = {"wa": (w + 2) % 4}
+    width = x.shape[1] // 2
+    barrier = pltpu.get_barrier_semaphore()
+    for place in (beside, across):
+        pl.semaphore_signal(barrier, inc=1, device_id=place, device_id_type=MESH)
+    pl.semaphore_wait(barrier, 2)
+
+    def send(src, dst, where, k):
+        copy = pltpu.make_async_remote_copy(
+            src_ref=src, dst_ref=dst, send_sem=send_sem.at[k], recv_sem=recv_sem.at[k],
+            device_id=where, device_id_type=MESH,
+        )
+        copy.start()
+        return copy
+
+    mine = pl.ds(pl.multiple_of(core * width, width), width)
+    theirs = pl.ds(pl.multiple_of((1 - core) * width, width), width)
+    one = send(x.at[:, theirs], got, beside, 0)
+    one.wait_recv()
+    half[...] = x[:, mine] + got[...]
+    two = send(half, far, across, 1)
+    two.wait_recv()
+    out[:, mine] = half[...] + far[...]
+    three = send(out.at[:, mine], out.at[:, mine], beside, 2)
+    three.wait_recv()
+    for copy in (one, two, three):
+        copy.wait_send()
+
+
+def sum_wa(x, collective_id, name):
+    rows, columns = x.shape
+    return pl.pallas_call(
+        sum_wa_kernel,
+        out_shape=jax.ShapeDtypeStruct(x.shape, x.dtype),
+        in_specs=[pl.BlockSpec(memory_space=pltpu.VMEM)],
+        out_specs=pl.BlockSpec(memory_space=pltpu.VMEM),
+        scratch_shapes=[pltpu.VMEM((rows, columns // 2), x.dtype)] * 3
+        + [pltpu.SemaphoreType.DMA((3,)), pltpu.SemaphoreType.DMA((3,))],
+        compiler_params=pltpu.CompilerParams(
+            collective_id=collective_id, has_side_effects=True, vmem_limit_bytes=VMEM_LIMIT
+        ),
+        name=name,
+    )(x)
 
 
 def turned_gather(arrays, axis, dims):
@@ -37,31 +408,6 @@
     )
 
 
-def in_one_piece(arrays, axis, dim, along):
-    widths = [a.shape[along] for a in arrays]
-    both = jnp.concatenate(arrays, axis=along)
-    whole = lax.all_gather(both, axis, axis=dim, tiled=True)
-    return tuple(jnp.split(whole, [sum(widths[:k]) for k in range(1, len(widths))], axis=along))
-
-
-def side_by_side(arrays, axis, dim, along):
-    widths = [a.shape[along] for a in arrays]
-    both = jnp.concatenate(arrays, axis=along)
-    whole = lax.psum_scatter(both, axis, scatter_dimension=dim, tiled=True)
-    return tuple(jnp.split(whole, [sum(widths[:k]) for k in range(1, len(widths))], axis=along))
-
-
-def side_by_side_2(arrays, axis, dim, along):
-    columns = [a.reshape(*a.shape[:along], -1) for a in arrays]
-    both = jnp.concatenate(columns, axis=along)
-    whole, at, gathered = (lax.psum_scatter(both, axis, scatter_dimension=dim, tiled=True), 0, [])
-    for a, column in zip(arrays, columns):
-        share = whole[..., at : at + column.shape[along]]
-        gathered.append(share.reshape(*share.shape[:along], *a.shape[along:]))
-        at += column.shape[along]
-    return tuple(gathered)
-
-
 def rope_tables(positions):
     half_width = HD // 2
     inverse = 1.0 / ROPE_BASE ** (jnp.arange(half_width, dtype=jnp.float32) * 2.0 / HD)
@@ -90,22 +436,18 @@
     return lax.all_gather(moved, "wa", axis=1, tiled=True)
 
 
-def back_share(expert_part, shared_part):
+def back_share(expert_part, shared_part, collective_id, name):
     share = lax.psum_scatter(
         expert_part.astype(jnp.bfloat16), "wa", scatter_dimension=1, tiled=True
     )
     moved = lax.all_to_all(share, ("sp", "ctx"), split_axis=0, concat_axis=0, tiled=True)
     returned = lax.all_gather(moved, "wa", axis=1, tiled=True)
-    shared_sum = taken_together(shared_part.astype(jnp.bfloat16), "wa").astype(jnp.float32)
+    shared_sum = sum_wa(shared_part.astype(jnp.bfloat16), collective_id, name).astype(jnp.float32)
     return (returned, shared_sum)
 
 
-def send_rows_out(rows):
-    return send_share(rows)
-
-
-def bring_back(expert_part, shared_part):
-    return back_share(expert_part, shared_part)
+def gather_whole(arrays):
+    return gather_cube(arrays, whole_parts(arrays), 1, "gather_attention_weights")
 
 
 def shards(
@@ -136,34 +478,15 @@
     score_scale = HD ** (-0.5)
     seq_len = local_tokens * devices_seq
     device_pos = lax.axis_index("sp") * lax.axis_size("ctx") + lax.axis_index("ctx")
-    gathered = turned_gather(
-        (
-            attn_gain,
-            query_weight,
-            key_weight,
-            value_weight,
-            output_weight,
-            mlp_gain,
-            router_weight,
-            shared_gate,
-            shared_up,
-            shared_down,
-        ),
+    full_query, full_key, full_value, output_turned = (
+        whole.reshape(D, head_cols)
+        for whole in gather_whole((query_weight, key_weight, value_weight, output_weight.T))
+    )
+    full_sgate, full_sup, full_sdown, full_router, full_attn_gain, full_mlp_gain = turned_gather(
+        (shared_gate, shared_up, shared_down, router_weight, attn_gain, mlp_gain),
         ("sp", "ctx"),
-        (0, 0, 0, 0, 1, 0, 0, 0, 0, 1),
-    )
-    (
-        full_attn_gain,
-        full_query,
-        full_key,
-        full_value,
-        full_output,
-        full_mlp_gain,
-        full_router,
-        full_sgate,
-        full_sup,
-        full_sdown,
-    ) = gathered
+        (0, 0, 1, 0, 0, 0),
+    )
     tokens_f = tokens.astype(jnp.float32)
     inv_one = lax.rsqrt(jnp.mean(tokens_f * tokens_f, axis=-1, keepdims=True) + EPSILON)
     unit_one = tokens_f * inv_one
@@ -186,7 +509,9 @@
     values_local = jnp.dot(normed, full_value, preferred_element_type=jnp.float32).astype(
         jnp.bfloat16
     )
-    keys_all, values_all = in_one_piece((keys_local, values_local), ("sp", "ctx"), 0, 1)
+    keys_all, values_all = gather_cube(
+        (keys_local, values_local), half_parts((keys_local, values_local)), 2, "gather_keys_values"
+    )
     keys_all = keys_all.reshape(seq_len, heads_here, HD)
     values_all = values_all.reshape(seq_len, heads_here, HD)
     visible = jnp.arange(seq_len, dtype=jnp.int32)[None, :] <= query_pos[:, None]
@@ -209,8 +534,10 @@
         .astype(jnp.bfloat16)
         .reshape(local_tokens, head_cols)
     )
-    attn_part = jnp.dot(attended, full_output, preferred_element_type=jnp.float32)
-    attn_out = taken_together(attn_part.astype(jnp.bfloat16), "wa").astype(jnp.float32)
+    attn_part = jnp.einsum(
+        "tc,dc->td", attended, output_turned, preferred_element_type=jnp.float32
+    )
+    attn_out = sum_wa(attn_part.astype(jnp.bfloat16), 3, "sum_attention").astype(jnp.float32)
     hidden_state = tokens_f + attn_out
     inv_two = lax.rsqrt(jnp.mean(hidden_state * hidden_state, axis=-1, keepdims=True) + EPSILON)
     unit_two = hidden_state * inv_two
@@ -233,7 +560,7 @@
     owner_assign = jnp.zeros((experts_all * capacity,), jnp.int32).at[destination].set(assign_ids)
     filled = jnp.zeros((experts_all * capacity,), jnp.bfloat16).at[destination].set(1.0)
     send_rows = mlp_in[owner_assign // TOP] * filled[:, None]
-    arrived = send_rows_out(send_rows).reshape(devices_seq, experts_here, capacity, D)
+    arrived = send_share(send_rows).reshape(devices_seq, experts_here, capacity, D)
     shared_pre = jnp.dot(mlp_in, full_sgate, preferred_element_type=jnp.float32)
     shared_lin = jnp.dot(mlp_in, full_sup, preferred_element_type=jnp.float32)
     shared_sig = jax.nn.sigmoid(shared_pre)
@@ -250,7 +577,7 @@
     expert_part = jnp.einsum(
         "secf,efd->secd", expert_act, expert_down, preferred_element_type=jnp.float32
     ).reshape(-1, D)
-    returned, shared_out = bring_back(expert_part, shared_part)
+    returned, shared_out = back_share(expert_part, shared_part, 4, "sum_shared")
     picked = returned[destination].reshape(local_tokens, TOP, D).astype(jnp.float32)
     routed = jnp.sum(gate_values[:, :, None] * picked, axis=1)
     block_out = (hidden_state + (routed + shared_out)).astype(jnp.bfloat16)
@@ -262,7 +589,7 @@
         .reshape(local_tokens * TOP, D)
     )
     send_grads = routed_grads[owner_assign] * filled[:, None]
-    arrived_grads = send_rows_out(send_grads).reshape(devices_seq, experts_here, capacity, D)
+    arrived_grads = send_share(send_grads).reshape(devices_seq, experts_here, capacity, D)
     act_grads = jnp.einsum(
         "secd,efd->secf", arrived_grads, expert_down, preferred_element_type=jnp.float32
     )
@@ -286,21 +613,17 @@
         "td,fd->tf", cotangent, full_sdown, preferred_element_type=jnp.float32
     )
     shared_down_grad = jnp.einsum(
-        "tf,td->fd", shared_act, cotangent, preferred_element_type=jnp.float32
+        "tf,td->df", shared_act, cotangent, preferred_element_type=jnp.float32
     )
     shared_slope = shared_sig * (1.0 + shared_pre * (1.0 - shared_sig))
     shared_pre_grads = (shared_act_grads * shared_lin * shared_slope).astype(jnp.bfloat16)
     shared_lin_grads = (shared_act_grads * shared_pre * shared_sig).astype(jnp.bfloat16)
-    shared_gate_grad = jnp.einsum(
-        "td,tf->df", mlp_in, shared_pre_grads, preferred_element_type=jnp.float32
-    )
-    shared_up_grad = jnp.einsum(
-        "td,tf->df", mlp_in, shared_lin_grads, preferred_element_type=jnp.float32
-    )
     shared_in_part = jnp.einsum(
         "tf,df->td", shared_pre_grads, full_sgate, preferred_element_type=jnp.float32
     ) + jnp.einsum("tf,df->td", shared_lin_grads, full_sup, preferred_element_type=jnp.float32)
-    rows_back, shared_in_grad = bring_back(rows_part.reshape(-1, D), shared_in_part)
+    rows_back, shared_in_grad = back_share(
+        rows_part.reshape(-1, D), shared_in_part, 5, "sum_shared_grad"
+    )
     routed_in_grad = jnp.sum(
         rows_back[destination].reshape(local_tokens, TOP, D).astype(jnp.float32), axis=1
     )
@@ -310,8 +633,11 @@
     )
     router_float = full_router.astype(jnp.float32)
     router_in_grad = jnp.einsum("te,de->td", logit_grads, router_float, precision=PRECISE)
-    router_weight_grad = jnp.einsum(
-        "td,te->de", mlp_in.astype(jnp.float32), logit_grads, precision=PRECISE
+    beside_grads = jnp.concatenate(
+        [shared_pre_grads, shared_lin_grads, logit_grads.astype(jnp.bfloat16)], axis=1
+    )
+    mlp_weight_grads = jnp.einsum(
+        "td,tf->df", mlp_in, beside_grads, preferred_element_type=jnp.float32
     )
     mlp_in_grad = router_in_grad + shared_in_grad + routed_in_grad
     gain_two_grad = jnp.sum(mlp_in_grad * unit_two, axis=0)
@@ -321,10 +647,10 @@
     )
     out_grad = hidden_grad.astype(jnp.bfloat16)
     output_weight_grad = jnp.einsum(
-        "tc,td->cd", attended, out_grad, preferred_element_type=jnp.float32
+        "tc,td->dc", attended, out_grad, preferred_element_type=jnp.float32
     )
     attended_grad = (
-        jnp.einsum("td,cd->tc", out_grad, full_output, preferred_element_type=jnp.float32)
+        jnp.einsum("td,dc->tc", out_grad, output_turned, preferred_element_type=jnp.float32)
         .astype(jnp.bfloat16)
         .reshape(local_tokens, heads_here, HD)
     )
@@ -349,19 +675,12 @@
         jnp.einsum("hqk,qhd->khd", score_grads, queries, preferred_element_type=jnp.float32)
         * score_scale
     )
-    key_sum, value_sum = tuple(
-        (
-            part.astype(jnp.float32)
-            for part in side_by_side(
-                (
-                    key_terms.reshape(seq_len, head_cols).astype(jnp.bfloat16),
-                    value_terms.reshape(seq_len, head_cols).astype(jnp.bfloat16),
-                ),
-                ("sp", "ctx"),
-                0,
-                1,
-            )
-        )
+    key_value_terms = [
+        part.astype(jnp.bfloat16).reshape(4, 2, 4, local_tokens, head_cols)
+        for part in (key_terms, value_terms)
+    ]
+    key_sum, value_sum = reduce_cube(
+        key_value_terms, half_parts(key_value_terms), 6, "reduce_keys_values", jnp.bfloat16
     )
     query_in = (
         rotate(query_grads, cosine, sine_part, -1.0)
@@ -370,7 +689,7 @@
     )
     key_in = (
         rotate(
-            key_sum.astype(jnp.bfloat16).reshape(local_tokens, heads_here, HD),
+            key_sum.astype(jnp.float32).reshape(local_tokens, heads_here, HD),
             cosine,
             sine_part,
             -1.0,
@@ -378,7 +697,7 @@
         .astype(jnp.bfloat16)
         .reshape(local_tokens, head_cols)
     )
-    value_in = value_sum.astype(jnp.bfloat16)
+    value_in = value_sum
     query_weight_grad = jnp.einsum(
         "td,tc->dc", normed, query_in, preferred_element_type=jnp.float32
     )
@@ -391,7 +710,9 @@
         + jnp.einsum("tc,dc->td", key_in, full_key, preferred_element_type=jnp.float32)
         + jnp.einsum("tc,dc->td", value_in, full_value, preferred_element_type=jnp.float32)
     )
-    normed_grad = taken_together(normed_part.astype(jnp.bfloat16), "wa").astype(jnp.float32)
+    normed_grad = sum_wa(normed_part.astype(jnp.bfloat16), 7, "sum_normed_grad").astype(
+        jnp.float32
+    )
     gain_one_grad = jnp.sum(normed_grad * unit_one, axis=0)
     scaled_one = normed_grad * gain_one
     tokens_grad = (
@@ -399,59 +720,36 @@
         + inv_one
         * (scaled_one - unit_one * jnp.mean(scaled_one * unit_one, axis=-1, keepdims=True))
     ).astype(jnp.bfloat16)
-    reduced = (
-        *tuple(
-            (
-                part.astype(jnp.float32)
-                for part in side_by_side_2(
-                    (
-                        gain_one_grad.astype(jnp.bfloat16),
-                        query_weight_grad.astype(jnp.bfloat16),
-                        key_weight_grad.astype(jnp.bfloat16),
-                        value_weight_grad.astype(jnp.bfloat16),
-                    ),
-                    ("sp", "ctx"),
-                    0,
-                    1,
-                )
-            )
-        ),
-        lax.psum_scatter(
-            output_weight_grad.astype(jnp.bfloat16), ("sp", "ctx"), scatter_dimension=1, tiled=True
-        ).astype(jnp.float32),
-        *tuple(
-            (
-                part.astype(jnp.float32)
-                for part in side_by_side_2(
-                    (
-                        gain_two_grad.astype(jnp.bfloat16),
-                        router_weight_grad.astype(jnp.bfloat16),
-                        shared_gate_grad.astype(jnp.bfloat16),
-                        shared_up_grad.astype(jnp.bfloat16),
-                    ),
-                    ("sp", "ctx"),
-                    0,
-                    1,
-                )
-            )
-        ),
-        lax.psum_scatter(
-            shared_down_grad.astype(jnp.bfloat16), ("sp", "ctx"), scatter_dimension=1, tiled=True
-        ).astype(jnp.float32),
-    )
+    gain_grads = jnp.stack([gain_one_grad, gain_two_grad], axis=1)
+    gain_grads = jnp.pad(gain_grads, ((0, 0), (0, HD - 2)))
+    mlp_grads = [
+        part.astype(jnp.bfloat16).reshape(4, 2, 4, D // devices_seq, -1)
+        for part in (mlp_weight_grads, shared_down_grad, gain_grads)
+    ]
+    mlp_shares, down_share, gain_shares = reduce_cube(
+        mlp_grads, row_parts(mlp_grads), 8, "reduce_mlp_grads"
+    )
+    attention_grads = [
+        part.astype(jnp.bfloat16).reshape(4, 2, 4, D // devices_seq, -1)
+        for part in (query_weight_grad, key_weight_grad, value_weight_grad, output_weight_grad)
+    ]
+    query_share, key_share, value_share, output_share = reduce_cube(
+        attention_grads, whole_parts(attention_grads), 9, "reduce_attention_grads"
+    )
+    hidden_cols = shared_gate.shape[1]
     return (
         block_out,
         tokens_grad,
-        reduced[0],
-        reduced[1],
-        reduced[2],
-        reduced[3],
-        reduced[4],
-        reduced[5],
-        reduced[6],
-        reduced[7],
-        reduced[8],
-        reduced[9],
+        gain_shares[:, 0],
+        query_share,
+        key_share,
+        value_share,
+        output_share.T,
+        gain_shares[:, 1],
+        mlp_shares[:, 2 * hidden_cols :],
+        mlp_shares[:, :hidden_cols],
+        mlp_shares[:, hidden_cols : 2 * hidden_cols],
+        down_share.T,
         expert_gate_grad,
         expert_up_grad,
         expert_down_grad,

time: 1980 us -> 1010 us (0.51); the launches traced: 1940 us -> 992 us
  waiting for transfers between devices: 1280 us -> 127 us
  Pallas kernels: 0 us -> 382 us
  local copies, waits for them, and re-layouts: 246 us -> 181 us
  starting transfers between devices: 49.4 us -> 0.69 us
  other arithmetic: 74.5 us -> 46.9 us
    unnamed x16 -> x7, waiting for transfers between devices: 537 us -> 0.12 us
    pallas_call x0 -> x9, Pallas kernels: none -> 382 us  [the longest x3 173 us: reduce_cube(): pl.pallas_call(functools.partial(reduce_kernel, parts, count), out_shape=...]
    reduce_scatter x2 -> x0, waiting for transfers between devices: 279 us -> none  [the longest x1 148 us: shards(): lax.psum_scatter(output_weight_grad.astype(jnp.bfloat16), ('sp', 'ctx'),...]
    all_gather x1, waiting for transfers between devices: 164 us -> 0.01 us  [turned_gather(): whole = lax.all_gather(both, axis, axis=0, tiled=True)]
    all_gather x1 -> x0, waiting for transfers between devices: 100 us -> none  [in_one_piece(): whole = lax.all_gather(both, axis, axis=dim, tiled=True)]
    all_to_all x4 -> x0, waiting for transfers between devices: 84.9 us -> none  [copy_for_each(): lax.all_to_all(jnp.broadcast_to(x[None], (size, *x.shape)), axis, 0, 0, t...]
    concatenate x4 -> x0, local copies, waits for them, and re-layouts: 66.8 us -> none  [the longest x2 66.5 us: side_by_side_2(): both = jnp.concatenate(columns, axis=along)]
    all_to_all x4 -> x0, starting transfers between devices: 48.4 us -> none  [copy_for_each(): lax.all_to_all(jnp.broadcast_to(x[None], (size, *x.shape)), axis, 0, 0, t...]
  transfers between devices with their start and end apart: 17 -> 7, of which waited for: 14 -> 4; matrix products, arithmetic and copies ran while one was open for 14% -> 12% of each run, Pallas kernels for 0% -> 12%
where the time goes in v1:
time: 1010 us; the launch traced here: 992 us
  Pallas kernels  382 us (38%)
  local copies, waits for them, and re-layouts  181 us (18%)
  waiting for transfers between devices  127 us (13%)
  matrix products  121 us (12%)
  blocking collectives  119 us (12%)
  other arithmetic  46.9 us (5%)
  between operations  15.4 us (2%)
    pallas_call x3, Pallas kernels, reduce_cube(): pl.pallas_call(functools.partial(reduce_kernel, parts, count), out_shape=...  173 us
    pallas_call x2, Pallas kernels, gather_cube(): pl.pallas_call(functools.partial(gather_kernel, parts, count), out_shape=...  137 us
    pallas_call x4, Pallas kernels, sum_wa(): pl.pallas_call(sum_wa_kernel, out_shape=jax.ShapeDtypeStruct(x.shape, x.d...  71.4 us
    all_to_all x2, blocking collectives, back_share(): lax.all_to_all(share, ('sp', 'ctx'), split_axis=0, concat_axis=0, tiled=T...  66.6 us
    reduce_scatter x2, waiting for transfers between devices, back_share(): lax.psum_scatter(expert_part.astype(jnp.bfloat16), 'wa', scatter_dimensio...  63.3 us
    all_gather x2, waiting for transfers between devices, send_share(): return lax.all_gather(moved, 'wa', axis=1, tiled=True)  63.3 us
    all_to_all x2, blocking collectives, send_share(): lax.all_to_all(piece, ('sp', 'ctx'), split_axis=0, concat_axis=0, tiled=T...  52.7 us
    reshape x4, local copies, waits for them, and re-layouts, shards(): part.astype(jnp.bfloat16).reshape(4, 2, 4, local_tokens, head_cols)  30.6 us
  transfers between devices with their start and end apart: 7, of which 4 were waited for; matrix products, arithmetic and copies ran while one was open for 12% of the time, Pallas kernels for 12%

profile of v1, /device:TPU:1, one launch (start us, length us, event | category | flops | bytes accessed | tf_op | source)
XLA Modules:
  0.0 992.3 jit_solution(4200550732816436027)
XLA Ops:
  11.9 81.5 %gather_attention_weights.1 = (bf16[4,2,4,64,512]{4,3,2,1,0:T(8,128)(2,1)}, bf16[4,2,4,64,512]{4,3,2,1,0:T(8,128)(2,1)}, bf16[4,2,4,64,512]{4,3,2,1,0:T(8,128)(2,1)}, bf16[4,2,4,64,512]{4,3,2,1,0:T(8,128)(2,1)}) custom-call(bf16[64,512]{1,0:T(8,128)(2,1)} %refs_0_.1, bf16[64,512]{1,0:T(8,128)(2,1)} %refs_1_.1, bf16[64,512]{1,0:T(8,128)(2,1)} %refs_2_.1, ...), custom_call_target="tpu_custom_call" | custom-call | tf_op jit(solution)/shard_map/gather_attention_weights/pallas_call | solution.py:160
  93.5 4.0 copy.167
  97.4 3.9 copy.165
  101.4 4.4 mul.426
  105.8 8.3 mul.440
  114.8 4.4 reduce-window.6
  122.0 3.4 scatter_custom_fusion
  125.4 9.3 scatter_custom_fusion.1
  146.7 2.8 convolution_convert_fusion.9.refs_1_
  149.4 55.4 %gather_keys_values.1 = (bf16[4,2,4,128,512]{4,3,2,1,0:T(8,128)(2,1)}, bf16[4,2,4,128,512]{4,3,2,1,0:T(8,128)(2,1)}) custom-call(bf16[128,512]{1,0:T(8,128)(2,1)} %copy.203.refs_0_, bf16[128,512]{1,0:T(8,128)(2,1)} %convolution_convert_fusion.9.refs_1_), custom_call_target="tpu_custom_call" | custom-call | tf_op jit(solution)/shard_map/gather_keys_values/pallas_call | solution.py:160
  204.8 6.9 reshape.355
  211.7 7.6 copy.186
  219.3 6.9 reshape.353
  226.2 4.5 fusion.124
  232.0 3.0 copy-done.2
  235.9 2.7 fusion.71
  240.9 21.3 %sum_attention.1 = bf16[128,2048]{1,0:T(8,128)(2,1)} custom-call(bf16[128,2048]{1,0:T(8,128)(2,1)} %convolution_convert_fusion.7.x), custom_call_target="tpu_custom_call" | custom-call | tf_op jit(solution)/shard_map/sum_attention/pallas_call | solution.py:383
  269.3 6.0 gather_fusion
  275.2 4.9 multiply_convert_fusion.2
  280.1 11.1 %gather_fusion.2 = bf16[1024,2048]{1,0:T(8,128)(2,1)} fusion(bf16[768,2048]{1,0:T(8,128)(2,1)} %multiply_convert_fusion.2, s32[1024]{0:T(1024)S(1)} %copy-done.56), kind=kCustom, calls=%fused_computation.2 | custom fusion | bytes 8392704 | tf_op jit(solution)/shard_map/gather | solution.py:591
  291.2 2.9 dynamic-slice_multiply_fusion
  294.1 24.7 %all_to_all.48 = bf16[32,32,512]{2,1,0:T(8,128)(2,1)} all-to-all(bf16[32,32,512]{2,1,0:T(8,128)(2,1)S(1)} %bitcast.219), channel_id=1, replica_groups=mesh['sp'=4,'ctx'=8,'wa'=4] {'sp','ctx'}, dimensions={0} | all-to-all | bytes 2097152 | tf_op jit(solution)/shard_map/all_to_all | solution.py:435
  318.9 28.0 %all_to_all.49 = bf16[32,32,512]{2,1,0:T(8,128)(2,1)} all-to-all(bf16[32,32,512]{2,1,0:T(8,128)(2,1)} %bitcast.218), channel_id=1, replica_groups=mesh['sp'=4,'ctx'=8,'wa'=4] {'sp','ctx'}, dimensions={0} | all-to-all | bytes 2097152 | tf_op jit(solution)/shard_map/all_to_all | solution.py:435
  347.4 23.2 %all-gather.8.cloned.1.call-done = bf16[1024,2048]{1,0:T(8,128)(2,1)} async-done(((bf16[1024,512]{1,0:T(8,128)(2,1)}), bf16[1024,2048]{1,0:T(8,128)(2,1)}) %all-gather.8.cloned.1.call-update) | async-done | bytes 4194320 | tf_op jit(solution)/shard_map/all_gather | solution.py:436
  370.6 6.7 fusion.16
  377.3 3.5 fusion.14
  380.8 40.0 %all-gather.12.cloned.1.call-done = bf16[1024,2048]{1,0:T(8,128)(2,1)} async-done(((bf16[1024,512]{1,0:T(8,128)(2,1)}), bf16[1024,2048]{1,0:T(8,128)(2,1)}) %all-gather.12.cloned.1.call-update) | async-done | bytes 4194320 | tf_op jit(solution)/shard_map/all_gather | solution.py:436
  420.8 6.9 fusion.55
  435.1 3.5 convert_bitcast_fusion
  441.0 40.3 %reduce-scatter.5.cloned.1.call-done = bf16[1024,512]{1,0:T(8,128)(2,1)} async-done(((bf16[1024,2048]{1,0:T(8,128)(2,1)}), bf16[1024,512]{1,0:T(8,128)(2,1)}) %reduce-scatter.5.cloned.1.call-update) | async-done | bytes 1048592 | tf_op jit(solution)/shard_map/reduce_scatter | solution.py:440
  481.2 33.4 %all_to_all.50 = bf16[32,32,512]{2,1,0:T(8,128)(2,1)} all-to-all(bf16[32,32,512]{2,1,0:T(8,128)(2,1)} %bitcast.231), channel_id=1, replica_groups=mesh['sp'=4,'ctx'=8,'wa'=4] {'sp','ctx'}, dimensions={0} | all-to-all | bytes 2097152 | tf_op jit(solution)/shard_map/all_to_all | solution.py:443
  514.7 23.1 %reduce-scatter.3.cloned.1.call-done = bf16[1024,512]{1,0:T(8,128)(2,1)} async-done(((bf16[1024,2048]{1,0:T(8,128)(2,1)}), bf16[1024,512]{1,0:T(8,128)(2,1)}) %reduce-scatter.3.cloned.1.call-update) | async-done | bytes 1048592 | tf_op jit(solution)/shard_map/reduce_scatter | solution.py:440
  537.8 33.1 %all_to_all.51 = bf16[32,32,512]{2,1,0:T(8,128)(2,1)} all-to-all(bf16[32,32,512]{2,1,0:T(8,128)(2,1)} %bitcast.230), channel_id=1, replica_groups=mesh['sp'=4,'ctx'=8,'wa'=4] {'sp','ctx'}, dimensions={0} | all-to-all | bytes 2097152 | tf_op jit(solution)/shard_map/all_to_all | solution.py:443
  572.7 4.8 fusion.36
  577.4 3.0 fusion.67
  580.4 3.3 multiply_convert_fusion.5
  583.8 3.8 fusion.34
  587.5 3.9 fusion.46.x
  591.4 15.6 %sum_shared_grad.1 = bf16[128,2048]{1,0:T(8,128)(2,1)} custom-call(bf16[128,2048]{1,0:T(8,128)(2,1)} %fusion.46.x), custom_call_target="tpu_custom_call" | custom-call | tf_op jit(solution)/shard_map/sum_shared_grad/pallas_call | solution.py:383
  607.0 4.2 fusion.50.x
  611.2 19.1 %sum_shared.1 = bf16[128,2048]{1,0:T(8,128)(2,1)} custom-call(bf16[128,2048]{1,0:T(8,128)(2,1)} %fusion.50.x), custom_call_target="tpu_custom_call" | custom-call | tf_op jit(solution)/shard_map/sum_shared/pallas_call | solution.py:383
  632.2 3.0 copy.193
  635.9 6.8 convolution_bitcast_fusion.1
  642.7 4.3 convolution_bitcast_fusion
  647.0 4.3 fusion.18
  651.3 9.9 gather_fusion.3
  661.1 6.5 reshape.377
  667.7 9.9 gather_fusion.1
  677.5 6.6 reshape.376
  684.2 7.7 multiply_reduce_fusion.1
  692.1 6.1 reduce_sum.157
  702.9 7.1 multiply_reduce_fusion
  710.1 6.7 fusion.2
  719.4 3.2 fusion.3
  726.0 7.8 reshape.437
  733.8 7.5 copy.204.refs_0_
  741.3 7.8 reshape.438
  749.1 7.5 copy.205.refs_1_
  756.7 54.2 %reduce_keys_values.1 = (bf16[128,512]{1,0:T(8,128)(2,1)}, bf16[128,512]{1,0:T(8,128)(2,1)}) custom-call(bf16[4,2,4,128,512]{4,3,2,1,0:T(8,128)(2,1)} %copy.204.refs_0_, bf16[4,2,4,128,512]{4,3,2,1,0:T(8,128)(2,1)} %copy.205.refs_1_), custom_call_target="tpu_custom_call" | custom-call | tf_op jit(solution)/shard_map/reduce_keys_values/pallas_call | solution.py:311
  822.0 15.4 %sum_normed_grad.1 = bf16[128,2048]{1,0:T(8,128)(2,1)} custom-call(bf16[128,2048]{1,0:T(8,128)(2,1)} %fusion.49.x), custom_call_target="tpu_custom_call" | custom-call | tf_op jit(solution)/shard_map/sum_normed_grad/pallas_call | solution.py:383
  838.8 4.2 convolution_convert_fusion
  843.1 8.8 copy.192
  853.2 66.9 %reduce_mlp_grads.1 = (f32[64,1472]{1,0:T(8,128)}, f32[64,704]{1,0:T(8,128)}, f32[64,128]{1,0:T(8,128)}) custom-call(bf16[4,2,4,64,1472]{4,3,2,1,0:T(8,128)(2,1)} %bitcast.194, bf16[4,2,4,64,704]{4,3,2,1,0:T(8,128)(2,1)} %bitcast.201, bf16[4,2,4,64,128]{4,3,2,1,0:T(8,128)(2,1)} %bitcast.220), custom_call_target="tpu_custom_call" | custom-call | tf_op jit(solution)/shard_map/reduce_mlp_grads/pallas_call | solution.py:311
  926.1 52.2 %reduce_attention_grads.1 = (f32[64,512]{1,0:T(8,128)}, f32[64,512]{1,0:T(8,128)}, f32[64,512]{1,0:T(8,128)}, f32[64,512]{1,0:T(8,128)}) custom-call(bf16[4,2,4,64,512]{4,3,2,1,0:T(8,128)(2,1)} %bitcast.211, bf16[4,2,4,64,512]{4,3,2,1,0:T(8,128)(2,1)} %bitcast.212, bf16[4,2,4,64,512]{4,3,2,1,0:T(8,128)(2,1)} %bitcast.213, bf16[4,2,4,64,512]{4,3,2,1,0:T(8,128)(2,1)} %bitcast.210), custom_call_target="tpu_custom_call" | custom-call | tf_op jit(solution)/shard_map/reduce_attention_grads/pallas_call | solution.py:311
  (247 shorter events, 83.4 us)
Async XLA Ops:
  7.2 413.7 %copy-start = (bf16[2,352,2048]{2,1,0:T(8,128)(2,1)S(1)}, bf16[2,352,2048]{2,1,0:T(8,128)(2,1)}, u32[]{:S(2)}) copy-start(bf16[2,352,2048]{2,1,0:T(8,128)(2,1)} %param.31) | copy-start | bytes 8650756
  7.2 130.4 %all-gather.6.cloned.1.call-start = ((), (), s32[]{:S(2)}) async-start(), calls=%async_computation.6 | async-start | bytes 9732096 | tf_op jit(solution)/shard_map/all_gather | solution.py:401
  10.8 359.8 %all-gather.8.cloned.1.call-start = ((), (), s32[]{:S(2)}) async-start(), calls=%async_computation.7 | async-start | bytes 5242880 | tf_op jit(solution)/shard_map/all_gather | solution.py:436
  93.4 7.9 copy-start.11
  105.8 15.9 %copy-start.50 = (s32[128,6]{0,1:T(8,128)S(1)}, s32[128,6]{0,1:T(8,128)}, u32[]{:S(2)}) copy-start(s32[128,6]{0,1:T(8,128)} %param.18) | copy-start | bytes 9220
  105.8 29.0 %copy-start.3 = (bf16[128,2048]{1,0:T(8,128)(2,1)S(1)}, bf16[128,2048]{1,0:T(8,128)(2,1)}, u32[]{:S(2)}) copy-start(bf16[128,2048]{1,0:T(8,128)(2,1)} %param.16) | copy-start | bytes 1572868
  122.0 12.8 %copy-start.58 = (s32[768]{0:T(1024)}, s32[768]{0:T(1024)S(1)}, u32[]{:S(2)}) copy-start(s32[768]{0:T(1024)S(1)} %fusion.108) | copy-start | bytes 9220
  135.0 9.2 copy-start.53
  137.6 6.6 copy-start.43
  137.6 6.6 copy-start.45
  139.4 10.0 %copy-start.38 = (f32[2048]{0:T(1024)}, f32[2048]{0:T(1024)S(1)}, u32[]{:S(2)}) copy-start(f32[2048]{0:T(1024)S(1)} %get-tuple-element.46) | copy-start | bytes 24580
  144.3 81.9 %copy-start.34 = (bf16[128,4,64]{0,2,1:T(8,128)(2,1)}, bf16[128,4,64]{0,2,1:T(8,128)(2,1)S(1)}, u32[]{:S(2)}) copy-start(bf16[128,4,64]{0,2,1:T(8,128)(2,1)S(1)} %get-tuple-element.67) | copy-start | bytes 196612
  144.3 81.9 %copy-start.36 = (bf16[128,4,64]{0,2,1:T(8,128)(2,1)}, bf16[128,4,64]{0,2,1:T(8,128)(2,1)S(1)}, u32[]{:S(2)}) copy-start(bf16[128,4,64]{0,2,1:T(8,128)(2,1)S(1)} %get-tuple-element.68) | copy-start | bytes 196612
  230.7 4.3 copy-start.2
  230.7 4.3 copy-start.55
  230.7 5.2 copy-start.7
  235.9 3.4 copy-start.17
  238.7 24.9 %copy-start.4 = (bf16[128,2048]{1,0:T(8,128)(2,1)S(1)}, bf16[128,2048]{1,0:T(8,128)(2,1)}, u32[]{:S(2)}) copy-start(bf16[128,2048]{1,0:T(8,128)(2,1)} %param.16) | copy-start | bytes 1572868
  238.7 28.4 %copy-start.51 = (s32[128,6]{0,1:T(8,128)S(1)}, s32[128,6]{0,1:T(8,128)}, u32[]{:S(2)}) copy-start(s32[128,6]{0,1:T(8,128)} %param.18) | copy-start | bytes 9220
  238.7 30.6 %copy-start.57 = (s32[1024]{0:T(1024)S(1)}, s32[1024]{0:T(1024)}, u32[]{:S(2)}) copy-start(s32[1024]{0:T(1024)} %get-tuple-element.78) | copy-start | bytes 12292
  263.6 3.0 copy-start.65
  275.2 4.9 copy-start.56
  318.8 102.0 %all-gather.12.cloned.1.call-start = ((), (), s32[]{:S(2)}) async-start(), calls=%async_computation.10 | async-start | bytes 5242880 | tf_op jit(solution)/shard_map/all_gather | solution.py:436
  346.9 134.3 %reduce-scatter.5.cloned.1.call-start = ((), (), s32[]{:S(2)}) async-start(), calls=%async_computation.11 | async-start | bytes 5242880 | tf_op jit(solution)/shard_map/reduce_scatter | solution.py:440
  370.6 6.7 copy-start.8
  370.6 6.7 copy-start.26
  420.8 6.9 copy-start.25
  435.0 102.8 %reduce-scatter.3.cloned.1.call-start = ((), (), s32[]{:S(2)}) async-start(), calls=%async_computation.8 | async-start | bytes 5242880 | tf_op jit(solution)/shard_map/reduce_scatter | solution.py:440
  440.9 130.0 %copy-start.12 = (bf16[128,2048]{1,0:T(8,128)(2,1)S(1)}, bf16[128,2048]{1,0:T(8,128)(2,1)}, u32[]{:S(2)}) copy-start(bf16[128,2048]{1,0:T(8,128)(2,1)} %param.17) | copy-start | bytes 1572868
  440.9 131.2 %copy-start.59 = (s32[768]{0:T(1024)S(1)}, s32[768]{0:T(1024)}, u32[]{:S(2)}) copy-start(s32[768]{0:T(1024)} %copy-done.58) | copy-start | bytes 9220
  440.9 210.4 %all-gather.14.cloned.1.call-start = ((), (), s32[]{:S(2)}) async-start(), calls=%async_computation.12 | async-start | bytes 5242880 | tf_op jit(solution)/shard_map/all_gather | solution.py:444
  514.7 153.0 %all-gather.10.cloned.1.call-start = ((), (), s32[]{:S(2)}) async-start(), calls=%async_computation.9 | async-start | bytes 5242880 | tf_op jit(solution)/shard_map/all_gather | solution.py:444
  583.7 7.7 copy-start.30
  583.7 7.7 copy-start.32
  583.7 23.3 %copy-start.48 = (bf16[128,704]{0,1:T(8,128)(2,1)}, bf16[128,704]{0,1:T(8,128)(2,1)S(1)}, u32[]{:S(2)}) copy-start(bf16[128,704]{0,1:T(8,128)(2,1)S(1)} %get-tuple-element.61) | copy-start | bytes 540676
  591.4 39.0 %copy-start.13 = (bf16[128,2048]{1,0:T(8,128)(2,1)S(1)}, bf16[128,2048]{1,0:T(8,128)(2,1)}, u32[]{:S(2)}) copy-start(bf16[128,2048]{1,0:T(8,128)(2,1)} %param.17) | copy-start | bytes 1572868
  635.9 6.8 copy-start.9
  635.9 6.8 copy-start.23
  642.7 4.3 copy-start.67
  642.7 4.3 copy-start.68
  647.0 4.3 copy-start.52
  677.5 6.6 copy-start.21
  684.1 7.8 copy-start.61
  684.1 7.8 copy-start.63
  692.0 6.1 copy-start.5
  692.0 6.1 copy-start.10
  692.0 6.1 copy-start.66
  698.2 4.1 copy-start.18
  702.9 13.9 %slice-start = ((s8[8388608]{0:T(1024)(128)(4,1)}), s8[4194304]{0:T(1024)(128)(4,1)S(1)}, s32[]{:S(2)}) async-start(s8[8388608]{0:T(1024)(128)(4,1)} %bitcast.192), calls=%async_computation.13 | async-start | bytes 8388608
  702.9 13.9 %slice-start.1 = ((s8[8388608]{0:T(1024)(128)(4,1)}), s8[4194304]{0:T(1024)(128)(4,1)S(1)}, s32[]{:S(2)}) async-start(s8[8388608]{0:T(1024)(128)(4,1)} %bitcast.192), calls=%async_computation.14 | async-start | bytes 8388608
  719.4 3.2 copy-start.6
  756.7 55.3 %copy-start.44 = (f32[128,64]{0,1:T(8,128)S(1)}, f32[128,64]{0,1:T(8,128)}, u32[]{:S(2)}) copy-start(f32[128,64]{0,1:T(8,128)} %get-tuple-element.82) | copy-start | bytes 98308
  756.7 55.3 %copy-start.46 = (f32[128,64]{0,1:T(8,128)S(1)}, f32[128,64]{0,1:T(8,128)}, u32[]{:S(2)}) copy-start(f32[128,64]{0,1:T(8,128)} %get-tuple-element.83) | copy-start | bytes 98308
  756.7 55.3 %copy-start.49 = (f32[128,64]{0,1:T(8,128)S(1)}, f32[128,64]{0,1:T(8,128)}, u32[]{:S(2)}) copy-start(f32[128,64]{0,1:T(8,128)} %get-tuple-element.81) | copy-start | bytes 98308
  756.7 55.4 %copy-start.39 = (f32[2048]{0:T(1024)S(1)}, f32[2048]{0:T(1024)}, u32[]{:S(2)}) copy-start(f32[2048]{0:T(1024)} %copy-done.38) | copy-start | bytes 24580
  756.7 55.4 %copy-start.54 = (f32[128]{0:T(128)S(1)}, f32[128]{0:T(128)}, u32[]{:S(2)}) copy-start(f32[128]{0:T(128)} %copy-done.53) | copy-start | bytes 1540
  812.1 5.2 copy-start.42
  814.3 5.2 copy-start.15
  817.3 3.0 copy-start.29
  819.5 19.3 %copy-start.31 = (bf16[128,704]{0,1:T(8,128)(2,1)S(1)}, bf16[128,704]{0,1:T(8,128)(2,1)}, u32[]{:S(2)}) copy-start(bf16[128,704]{0,1:T(8,128)(2,1)} %copy-done.30) | copy-start | bytes 540676
  819.5 19.3 %copy-start.33 = (bf16[128,704]{0,1:T(8,128)(2,1)S(1)}, bf16[128,704]{0,1:T(8,128)(2,1)}, u32[]{:S(2)}) copy-start(bf16[128,704]{0,1:T(8,128)(2,1)} %copy-done.32) | copy-start | bytes 540676
  853.2 70.1 %copy-start.19 = (bf16[128,2048]{1,0:T(8,128)(2,1)S(1)}, bf16[128,2048]{1,0:T(8,128)(2,1)}, u32[]{:S(2)}) copy-start(bf16[128,2048]{1,0:T(8,128)(2,1)} %sum_normed_grad.1) | copy-start | bytes 1572868
  926.1 59.2 %copy-start.1 = (bf16[2,352,2048]{2,1,0:T(8,128)(2,1)S(1)}, bf16[2,352,2048]{2,1,0:T(8,128)(2,1)}, u32[]{:S(2)}) copy-start(bf16[2,352,2048]{2,1,0:T(8,128)(2,1)} %param.31) | copy-start | bytes 8650756
  926.1 58.5 %copy-start.47 = (f32[64,704]{1,0:T(8,128)S(1)}, f32[64,704]{1,0:T(8,128)}, u32[]{:S(2)}) copy-start(f32[64,704]{1,0:T(8,128)} %get-tuple-element.44) | copy-start | bytes 540676
  (14 other events, 26.4 us)
Sparse Core Ops, SparseCore 0:
  11.6 124.2 all-gather.5
  319.0 51.6 all-gather.7
  372.3 48.5 all-gather.11
  435.1 46.0 reduce-scatter.4
  484.2 53.5 reduce-scatter.2
  539.3 54.9 all-gather.13
  596.0 54.8 all-gather.9

commit v2 on v1

v2 whole, which is shorter than its diff:
```python
import functools

import jax
import jax.numpy as jnp
from jax import lax
from jax.experimental import pallas as pl
from jax.experimental.pallas import tpu as pltpu
from jax.sharding import PartitionSpec as P

D = 2048
HD = 128
TOP = 6


EPSILON = 1e-06
ROPE_BASE = 10000.0
MASKED = -1e30
PRECISE = lax.Precision.HIGHEST
MESH = pl.DeviceIdType.MESH
VMEM_LIMIT = 60 * 1024 * 1024

ORDERS = (
    (("z", "A"), ("z", "B"), ("y", "A"), ("y", "B")),
    (("z", "B"), ("z", "A"), ("y", "B"), ("y", "A")),
    (("y", "A"), ("y", "B"), ("z", "A"), ("z", "B")),
    (("y", "B"), ("y", "A"), ("z", "B"), ("z", "A")),
)


def paired(i, kind):
    return i + 1 - 2 * (i % 2) if kind == "A" else 3 - i


def own_place():
    c = lax.axis_index("ctx")
    return lax.axis_index("sp"), c // 4, c % 4


def neighbour(axis, kind):
    z, xh, y = own_place()
    if axis == "z":
        return {"sp": paired(z, kind)}
    if axis == "y":
        return {"ctx": 4 * xh + paired(y, kind)}
    return {"ctx": 4 * (1 - xh) + y}


def greet_cube():
    barrier = pltpu.get_barrier_semaphore()
    for axis in ("z", "y"):
        for kind in ("A", "B"):
            pl.semaphore_signal(barrier, inc=1, device_id=neighbour(axis, kind), device_id_type=MESH)
    pl.semaphore_signal(barrier, inc=1, device_id=neighbour("x", "A"), device_id_type=MESH)
    pl.semaphore_wait(barrier, 5)


def pair_slots(i, kind):
    if kind == "A":
        return [(pl.ds((i // 2) * 2, 2), pl.ds(0, 2))]
    return [(pl.ds(i, 1), pl.ds(0, 1)), (pl.ds(3 - i, 1), pl.ds(1, 1))]


def pair_members(i, kind):
    if kind == "A":
        return [(i // 2) * 2, (i // 2) * 2 + 1]
    return [i, 3 - i]


def slot_in_pair(i, kind):
    return i % 2 if kind == "A" else 0


def gather_kernel(parts, count, *refs):
    ins, outs = refs[:count], refs[count : 2 * count]
    send_sem, recv_sem, local_sem = refs[2 * count :]
    z, xh, y = own_place()
    used = [0]
    started = []

    def start(src, dst, where):
        k = used[0]
        used[0] += 1
        copy = pltpu.make_async_remote_copy(
            src_ref=src, dst_ref=dst, send_sem=send_sem.at[k], recv_sem=recv_sem.at[k],
            device_id=where, device_id_type=MESH,
        )
        copy.start()
        started.append(copy)
        return copy

    def step(lane, p, s):
        ring1, ring2 = ORDERS[p][0][0], ORDERS[p][2][0]
        axis, kind = ORDERS[p][s]
        where = neighbour(axis, kind)
        xl = xh if lane == 0 else 1 - xh
        zs, ys = [pl.ds(z, 1)], [pl.ds(y, 1)]
        full = [pl.ds(0, 4)]
        if s == 1:
            other = [d for d, _ in pair_slots(z if ring1 == "z" else y, ORDERS[p][0][1])]
            zs, ys = (other, ys) if ring1 == "z" else (zs, other)
        if s >= 2:
            zs, ys = (full, ys) if ring1 == "z" else (zs, full)
        if s == 3:
            other = [d for d, _ in pair_slots(z if ring2 == "z" else y, ORDERS[p][2][1])]
            zs, ys = (other, ys) if ring2 == "z" else (zs, other)
        copies = []
        for a, rows, cols in parts[p]:
            for zd in zs:
                for yd in ys:
                    place = outs[a].at[zd, pl.ds(xl, 1), yd, rows, cols]
                    copies.append(start(place, place, where))
        return copies

    greet_cube()
    local = [
        pltpu.make_async_copy(ins[a], outs[a].at[z, xh, y], local_sem.at[a]) for a in range(count)
    ]
    for copy in local:
        copy.start()
    across = [
        [
            start(ins[a].at[rows, cols], outs[a].at[z, xh, y, rows, cols], neighbour("x", "A"))
            for a, rows, cols in part
        ]
        for part in parts
    ]
    for copy in local:
        copy.wait()
    flying = {}

    def advance(lane, s):
        for p in range(4):
            if s == 0 and lane == 1:
                for copy in across[p]:
                    copy.wait_recv()
            if s > 0:
                for copy in flying[lane, p]:
                    copy.wait_recv()
            flying[lane, p] = step(lane, p, s) if s < 4 else []

    advance(0, 0)
    advance(0, 1)
    advance(1, 0)
    advance(0, 2)
    advance(1, 1)
    advance(0, 3)
    advance(1, 2)
    advance(1, 3)
    advance(0, 4)
    advance(1, 4)
    for copy in started:
        copy.wait_send()


def gather_cube(arrays, parts, collective_id, name):
    count = len(arrays)
    copies = 11 * sum(len(part) for part in parts)
    return pl.pallas_call(
        functools.partial(gather_kernel, parts, count),
        out_shape=[jax.ShapeDtypeStruct((4, 2, 4, *a.shape), a.dtype) for a in arrays],
        in_specs=[pl.BlockSpec(memory_space=pl.ANY)] * count,
        out_specs=[pl.BlockSpec(memory_space=pl.ANY)] * count,
        scratch_shapes=[
            pltpu.SemaphoreType.DMA((copies,)),
            pltpu.SemaphoreType.DMA((copies,)),
            pltpu.SemaphoreType.DMA((count,)),
        ],
        compiler_params=pltpu.CompilerParams(collective_id=collective_id, has_side_effects=True),
        name=name,
    )(*arrays)


def reduce_kernel(parts, count, *refs):
    entries = [(p, *entry) for p in range(4) for entry in parts[p]]
    size = 5 * len(entries)
    ins, outs = refs[:count], refs[count : 2 * count]
    bufs = refs[2 * count : 2 * count + size]
    send_sem, recv_sem = refs[2 * count + size :]
    z, xh, y = own_place()
    used = [0]
    started = []
    flying = {}

    def start(src, dst, where):
        k = used[0]
        used[0] += 1
        copy = pltpu.make_async_remote_copy(
            src_ref=src, dst_ref=dst, send_sem=send_sem.at[k], recv_sem=recv_sem.at[k],
            device_id=where, device_id_type=MESH,
        )
        copy.start()
        started.append(copy)
        return copy

    def first(lane, e):
        p, a, rows, cols = entries[e]
        ring2, near = ORDERS[p][2]
        axis, kind = ORDERS[p][3]
        xl = xh if lane == 0 else 1 - xh
        theirs = paired(z if ring2 == "z" else y, kind)
        copies = []
        for src, dst in pair_slots(theirs, near):
            if ring2 == "z":
                block, place = ins[a].at[src, xl, :, rows, cols], bufs[5 * e].at[lane, dst]
            else:
                block, place = ins[a].at[:, xl, src, rows, cols], bufs[5 * e].at[lane, :, dst]
            copies.append(start(block, place, neighbour(axis, kind)))
        flying[lane, e] = copies

    def second(lane, e):
        p, a, rows, cols = entries[e]
        ring2 = ORDERS[p][2][0]
        axis, kind = ORDERS[p][2]
        xl = xh if lane == 0 else 1 - xh
        mine = z if ring2 == "z" else y
        buf = bufs[5 * e]
        for copy in flying[lane, e]:
            copy.wait_recv()
        slot = slot_in_pair(mine, kind)

        def add(j, place):
            def one(i, carry):
                if ring2 == "z":
                    buf[lane, j, i] = buf[lane, j, i] + ins[a][place, xl, i, rows, cols]
                else:
                    buf[lane, i, j] = buf[lane, i, j] + ins[a][i, xl, place, rows, cols]
                return carry

            lax.fori_loop(0, 4, one, 0)

        add(1 - slot, paired(mine, kind))
        half = buf.at[lane, 1 - slot] if ring2 == "z" else buf.at[lane, :, 1 - slot]
        flying[lane, e] = [start(half, bufs[5 * e + 1].at[lane], neighbour(axis, kind))]
        add(slot, mine)

    def third(lane, e):
        p = entries[e][0]
        ring1, ring2 = ORDERS[p][0][0], ORDERS[p][2][0]
        axis, kind = ORDERS[p][1]
        before, buf = bufs[5 * e], bufs[5 * e + 1]
        for copy in flying[lane, e]:
            copy.wait_recv()
        slot = slot_in_pair(z if ring2 == "z" else y, ORDERS[p][2][1])

        def one(i, carry):
            other = before[lane, slot, i] if ring2 == "z" else before[lane, i, slot]
            buf[lane, i] = buf[lane, i] + other
            return carry

        lax.fori_loop(0, 4, one, 0)
        theirs = paired(z if ring1 == "z" else y, kind)
        flying[lane, e] = [
            start(buf.at[lane, src], bufs[5 * e + 2].at[lane, dst], neighbour(axis, kind))
            for src, dst in pair_slots(theirs, ORDERS[p][0][1])
        ]

    def fourth(lane, e):
        p = entries[e][0]
        ring1 = ORDERS[p][0][0]
        axis, kind = ORDERS[p][0]
        mine = z if ring1 == "z" else y
        before, buf = bufs[5 * e + 1], bufs[5 * e + 2]
        for copy in flying[lane, e]:
            copy.wait_recv()
        slot = slot_in_pair(mine, kind)
        buf[lane, 1 - slot] = buf[lane, 1 - slot] + before[lane, paired(mine, kind)]
        flying[lane, e] = [
            start(buf.at[lane, 1 - slot], bufs[5 * e + 3].at[lane], neighbour(axis, kind))
        ]
        buf[lane, slot] = buf[lane, slot] + before[lane, mine]

    def last(lane, e):
        p, a, rows, cols = entries[e]
        ring1 = ORDERS[p][0][0]
        before, buf = bufs[5 * e + 2], bufs[5 * e + 3]
        for copy in flying[lane, e]:
            copy.wait_recv()
        slot = slot_in_pair(z if ring1 == "z" else y, ORDERS[p][0][1])
        if lane == 1:
            buf[1] = buf[1] + before[1, slot]
            flying["x", e] = start(buf.at[1], bufs[5 * e + 4], neighbour("x", "A"))
        else:
            flying["x", e].wait_recv()
            total = (
                buf[0].astype(jnp.float32)
                + before[0, slot].astype(jnp.float32)
                + bufs[5 * e + 4][...].astype(jnp.float32)
            )
            outs[a][rows, cols] = total.astype(outs[a].dtype)

    greet_cube()
    for stage in (first, second, third, fourth, last):
        for lane in (1, 0):
            for e in range(len(entries)):
                stage(lane, e)
    for copy in started:
        copy.wait_send()


def reduce_cube(arrays, parts, collective_id, name, dtype=jnp.float32):
    count = len(arrays)
    scratch = []
    for p in range(4):
        pair = (2, 4) if ORDERS[p][2][0] == "z" else (4, 2)
        for a, rows, cols in parts[p]:
            for lead in ((2, *pair), (2, 4), (2, 2), (2,), ()):
                scratch.append(pltpu.VMEM((*lead, rows.size, cols.size), arrays[a].dtype))
    copies = 13 * sum(len(part) for part in parts)
    return pl.pallas_call(
        functools.partial(reduce_kernel, parts, count),
        out_shape=[jax.ShapeDtypeStruct(a.shape[3:], dtype) for a in arrays],
        in_specs=[pl.BlockSpec(memory_space=pltpu.VMEM)] * count,
        out_specs=[pl.BlockSpec(memory_space=pltpu.VMEM)] * count,
        scratch_shapes=scratch
        + [pltpu.SemaphoreType.DMA((copies,)), pltpu.SemaphoreType.DMA((copies,))],
        compiler_params=pltpu.CompilerParams(
            collective_id=collective_id, has_side_effects=True, vmem_limit_bytes=VMEM_LIMIT
        ),
        name=name,
    )(*arrays)


def row_parts(arrays):
    parts = []
    for p in range(4):
        part = []
        for a, array in enumerate(arrays):
            rows, columns = array.shape[-2:]
            part.append((a, pl.ds(p * rows // 4, rows // 4), pl.ds(0, columns)))
        parts.append(part)
    return parts


def whole_parts(arrays):
    return [[(a, pl.ds(0, x.shape[-2]), pl.ds(0, x.shape[-1]))] for a, x in enumerate(arrays)]


def half_parts(arrays):
    return [
        [(a, pl.ds(0, x.shape[-2]), pl.ds(h * x.shape[-1] // 2, x.shape[-1] // 2))]
        for a, x in enumerate(arrays)
        for h in range(2)
    ]


def sum_wa_kernel(x, out, half, got, far, send_sem, recv_sem):
    w = lax.axis_index("wa")
    core = w % 2
    beside = {"wa": w + 1 - 2 * core}
    across = {"wa": (w + 2) % 4}
    width = x.shape[1] // 2
    barrier = pltpu.get_barrier_semaphore()
    for place in (beside, across):
        pl.semaphore_signal(barrier, inc=1, device_id=place, device_id_type=MESH)
    pl.semaphore_wait(barrier, 2)

    def send(src, dst, where, k):
        copy = pltpu.make_async_remote_copy(
            src_ref=src, dst_ref=dst, send_sem=send_sem.at[k], recv_sem=recv_sem.at[k],
            device_id=where, device_id_type=MESH,
        )
        copy.start()
        return copy

    mine = pl.ds(pl.multiple_of(core * width, width), width)
    theirs = pl.ds(pl.multiple_of((1 - core) * width, width), width)
    one = send(x.at[:, theirs], got, beside, 0)
    one.wait_recv()
    half[...] = x[:, mine] + got[...]
    two = send(half, far, across, 1)
    two.wait_recv()
    out[:, mine] = half[...] + far[...]
    three = send(out.at[:, mine], out.at[:, mine], beside, 2)
    three.wait_recv()
    for copy in (one, two, three):
        copy.wait_send()


def sum_wa(x, collective_id, name):
    rows, columns = x.shape
    return pl.pallas_call(
        sum_wa_kernel,
        out_shape=jax.ShapeDtypeStruct(x.shape, x.dtype),
        in_specs=[pl.BlockSpec(memory_space=pltpu.VMEM)],
        out_specs=pl.BlockSpec(memory_space=pltpu.VMEM),
        scratch_shapes=[pltpu.VMEM((rows, columns // 2), x.dtype)] * 3
        + [pltpu.SemaphoreType.DMA((3,)), pltpu.SemaphoreType.DMA((3,))],
        compiler_params=pltpu.CompilerParams(
            collective_id=collective_id, has_side_effects=True, vmem_limit_bytes=VMEM_LIMIT
        ),
        name=name,
    )(x)


def head_columns(h):
    return pl.ds(pl.multiple_of(h * HD, HD), HD)


class Copies:
    def __init__(self, send_sem, recv_sem):
        self.send_sem, self.recv_sem, self.started = send_sem, recv_sem, []

    def start(self, src, dst, where):
        k = len(self.started)
        copy = pltpu.make_async_remote_copy(
            src_ref=src, dst_ref=dst, send_sem=self.send_sem.at[k],
            recv_sem=self.recv_sem.at[k], device_id=where, device_id_type=MESH,
        )
        copy.start()
        self.started.append(copy)
        return copy

    def finish(self):
        for copy in self.started:
            copy.wait_send()


def greet(places):
    barrier = pltpu.get_barrier_semaphore()
    for place in places:
        pl.semaphore_signal(barrier, inc=1, device_id=place, device_id_type=MESH)
    pl.semaphore_wait(barrier, len(places))


def along_z():
    z = lax.axis_index("sp")
    return [{"sp": (z + d) % 4} for d in (1, 2, 3)]


def vmem_call(kernel, out_shape, operands, scratch, collective_id, name, **params):
    return pl.pallas_call(
        kernel,
        out_shape=out_shape,
        in_specs=[pl.BlockSpec(memory_space=pltpu.VMEM)] * len(operands),
        out_specs=jax.tree.map(lambda _: pl.BlockSpec(memory_space=pltpu.VMEM), out_shape),
        scratch_shapes=scratch,
        compiler_params=pltpu.CompilerParams(
            collective_id=collective_id,
            has_side_effects=collective_id is not None,
            vmem_limit_bytes=VMEM_LIMIT,
        ),
        name=name,
        **params,
    )(*operands)


def project_kernel(normed, wq, wk, wv, cosine, sine, q, k, v):
    for weight, out in ((wq, q), (wk, k)):
        raw = jnp.dot(normed[...], weight[...], preferred_element_type=jnp.float32)
        for h in range(out.shape[1] // HD):
            one = raw[:, h * HD : (h + 1) * HD]
            turned = one * cosine[...] + pltpu.roll(one, HD // 2, 1) * sine[...]
            out[:, h * HD : (h + 1) * HD] = turned.astype(out.dtype)
    raw = jnp.dot(normed[...], wv[...], preferred_element_type=jnp.float32)
    v[...] = raw.astype(v.dtype)


def project(normed, weights, cosine, sine):
    shape = jax.ShapeDtypeStruct((normed.shape[0], weights[0].shape[1]), jnp.bfloat16)
    return vmem_call(
        project_kernel, [shape] * 3, (normed, *weights, cosine, sine), [], None, "project_heads"
    )


def turn_back_kernel(q, k, cosine, sine, q_in, k_in):
    for src, out in ((q, q_in), (k, k_in)):
        for h in range(out.shape[1] // HD):
            one = src[:, h * HD : (h + 1) * HD].astype(jnp.float32)
            turned = one * cosine[...] - pltpu.roll(one, HD // 2, 1) * sine[...]
            out[:, h * HD : (h + 1) * HD] = turned.astype(out.dtype)


def turn_back(q, k, cosine, sine):
    shape = jax.ShapeDtypeStruct(q.shape, jnp.bfloat16)
    return vmem_call(
        turn_back_kernel, [shape] * 2, (q, k, cosine, sine), [], None, "turn_back_heads"
    )


def spread_kernel(q, k, v, q_out, k_out, v_out, send_sem, recv_sem):
    z, xh, y = own_place()
    places = along_z() + [neighbour("y", "A"), neighbour("y", "B"), neighbour("x", "A")]
    greet(places)
    copies = Copies(send_sem, recv_sem)
    arriving = []
    for d in (1, 2, 3):
        there = (z + d) % 4
        cols = head_columns(there)
        for src, dst in (
            (k, k_out.at[z, xh, y]), (v, v_out.at[z, xh, y]), (q, q_out.at[z])
        ):
            arriving.append(copies.start(src.at[:, cols], dst, {"sp": there}))
    k_out[z, xh, y] = k[:, head_columns(z)]
    v_out[z, xh, y] = v[:, head_columns(z)]
    q_out[z] = q[:, head_columns(z)]
    for copy in arriving:
        copy.wait_recv()

    def block(out, xl, place):
        return out.at[:, xl, place]

    def send(out, xl, place, axis, kind):
        where = neighbour(axis, kind)
        return copies.start(block(out, xl, place), block(out, xl, place), where)

    first, across = {}, []
    for out, kind in ((k_out, "A"), (v_out, "B")):
        first[0, kind] = send(out, xh, y, "y", kind)
        across.append(send(out, xh, y, "x", "A"))
    last = []

    def onward(lane, xl):
        first[lane, "A"].wait_recv()
        for place, _ in pair_slots(y, "A"):
            last.append(send(k_out, xl, place, "y", "B"))
        first[lane, "B"].wait_recv()
        for place, _ in pair_slots(y, "B"):
            last.append(send(v_out, xl, place, "y", "A"))

    onward(0, xh)
    for copy in across:
        copy.wait_recv()
    for out, kind in ((k_out, "A"), (v_out, "B")):
        first[1, kind] = send(out, 1 - xh, y, "y", kind)
    onward(1, 1 - xh)
    for copy in last:
        copy.wait_recv()
    copies.finish()


def spread_heads(q, k, v, collective_id):
    rows = q.shape[0]
    own = jax.ShapeDtypeStruct((4, rows, HD), q.dtype)
    every = jax.ShapeDtypeStruct((4, 2, 4, rows, HD), q.dtype)
    sems = [pltpu.SemaphoreType.DMA((21,))] * 2
    return vmem_call(
        spread_kernel, [own, every, every], (q, k, v), sems, collective_id, "spread_heads"
    )


def collect_kernel(dq, dk, dv, q_out, k_out, v_out, *refs):
    bufs, sums, cross = refs[0:2], refs[2:4], refs[4:6]
    own, (send_sem, recv_sem) = refs[6:8], refs[8:]
    z, xh, y = own_place()
    greet(along_z() + [neighbour("y", "A"), neighbour("y", "B"), neighbour("x", "A")])
    copies = Copies(send_sem, recv_sem)
    ins, near, far = (dk, dv), ("A", "B"), ("B", "A")
    flying = {}
    for lane in (1, 0):
        xl = xh if lane == 0 else 1 - xh
        for a in range(2):
            theirs = paired(y, far[a])
            flying[lane, a] = [
                copies.start(ins[a].at[:, xl, src], bufs[a].at[lane, :, dst], neighbour("y", far[a]))
                for src, dst in pair_slots(theirs, near[a])
            ]
    arriving = []
    for d in (1, 2, 3):
        there = (z + d) % 4
        arriving.append(copies.start(dq.at[there], q_out.at[:, head_columns(z)], {"sp": there}))
    q_out[:, head_columns(z)] = dq[z]
    for lane in (1, 0):
        xl = xh if lane == 0 else 1 - xh
        for a in range(2):
            for copy in flying[lane, a]:
                copy.wait_recv()
            slot = slot_in_pair(y, near[a])
            there = paired(y, near[a])

            def add(j, place):
                def one(i, carry):
                    bufs[a][lane, i, j] = bufs[a][lane, i, j] + ins[a][i, xl, place]
                    return carry

                lax.fori_loop(0, 4, one, 0)

            add(1 - slot, there)
            flying[lane, a] = copies.start(
                bufs[a].at[lane, :, 1 - slot], sums[a].at[lane], neighbour("y", near[a])
            )
            add(slot, y)
    for lane in (1, 0):
        for a in range(2):
            flying[lane, a].wait_recv()
            slot = slot_in_pair(y, near[a])

            def more(i, carry):
                sums[a][lane, i] = sums[a][lane, i] + bufs[a][lane, i, slot]
                return carry

            lax.fori_loop(0, 4, more, 0)
            if lane == 1:
                flying["x", a] = copies.start(sums[a].at[1], cross[a], neighbour("x", "A"))
    for a, out in ((0, k_out), (1, v_out)):
        flying["x", a].wait_recv()

        def total(i, carry):
            own[a][i] = sums[a][0, i] + cross[a][i]
            return carry

        lax.fori_loop(0, 4, total, 0)
        for d in (1, 2, 3):
            there = (z + d) % 4
            arriving.append(copies.start(own[a].at[there], out.at[:, head_columns(z)], {"sp": there}))
        out[:, head_columns(z)] = own[a][z]
    for copy in arriving:
        copy.wait_recv()
    copies.finish()


def collect_heads(dq, dk, dv, collective_id):
    rows = dq.shape[1]
    block = (rows, HD)
    shape = jax.ShapeDtypeStruct((rows, 4 * HD), dq.dtype)
    scratch = [
        pltpu.VMEM((*lead, *block), dq.dtype) for lead in ((2, 4, 2), (2, 4), (4,), (4,)) for _ in range(2)
    ]
    sems = [pltpu.SemaphoreType.DMA((21,))] * 2
    return vmem_call(
        collect_kernel, [shape] * 3, (dq, dk, dv), scratch + sems, collective_id, "collect_heads"
    )


def heads_out_kernel(x, out, send_sem, recv_sem):
    z = lax.axis_index("sp")
    greet(along_z())
    copies = Copies(send_sem, recv_sem)
    for d in (1, 2, 3):
        there = (z + d) % 4
        copies.start(x.at[there], out.at[:, head_columns(z)], {"sp": there})
    out[:, head_columns(z)] = x[z]
    for copy in copies.started:
        copy.wait_recv()
    copies.finish()


def heads_in_kernel(x, out, send_sem, recv_sem):
    z = lax.axis_index("sp")
    greet(along_z())
    copies = Copies(send_sem, recv_sem)
    for d in (1, 2, 3):
        there = (z + d) % 4
        copies.start(x.at[:, head_columns(there)], out.at[z], {"sp": there})
    out[z] = x[:, head_columns(z)]
    for copy in copies.started:
        copy.wait_recv()
    copies.finish()


def heads_out(x, collective_id):
    shape = jax.ShapeDtypeStruct((x.shape[1], 4 * HD), x.dtype)
    sems = [pltpu.SemaphoreType.DMA((3,))] * 2
    return vmem_call(heads_out_kernel, shape, (x,), sems, collective_id, "heads_to_tokens")


def heads_in(x, collective_id):
    shape = jax.ShapeDtypeStruct((4, x.shape[0], HD), x.dtype)
    sems = [pltpu.SemaphoreType.DMA((3,))] * 2
    return vmem_call(heads_in_kernel, shape, (x,), sems, collective_id, "tokens_to_heads")


def attend_kernel(q, k, v, attended, exact, probs, scores):
    rows = q.shape[1]
    span = 8 * rows
    first = lax.axis_index("ctx") * rows
    scale = HD ** (-0.5)
    contract = (((1,), (1,)), ((), ()))
    at = 0
    for block in range(4):
        for c in range(block + 1):
            part = lax.dot_general(
                q[block], k[c * span : (c + 1) * span], contract, preferred_element_type=jnp.float32
            ) * scale
            if c == block:
                row = lax.broadcasted_iota(jnp.int32, part.shape, 0)
                col = lax.broadcasted_iota(jnp.int32, part.shape, 1)
                part = jnp.where(col <= row + first, part, MASKED)
            scores[:, c * span : (c + 1) * span] = part
        width = (block + 1) * span
        top = jnp.max(scores[:, :width], axis=1, keepdims=True)
        total = jnp.zeros_like(top)
        for c in range(block + 1):
            part = jnp.exp(scores[:, c * span : (c + 1) * span] - top)
            total = total + jnp.sum(part, axis=1, keepdims=True)
            scores[:, c * span : (c + 1) * span] = part
        scaled = 1.0 / total
        result = jnp.zeros((rows, HD), jnp.float32)
        for c in range(block + 1):
            low = (scores[:, c * span : (c + 1) * span] * scaled).astype(probs.dtype)
            probs[at] = low
            result = result + jnp.dot(
                low, v[c * span : (c + 1) * span], preferred_element_type=jnp.float32
            )
            at += 1
        exact[block] = result
        attended[block] = result.astype(attended.dtype)


def attend(q, k, v):
    rows = q.shape[1]
    out_shape = [
        jax.ShapeDtypeStruct(q.shape, q.dtype),
        jax.ShapeDtypeStruct(q.shape, jnp.float32),
        jax.ShapeDtypeStruct((10, rows, 8 * rows), q.dtype),
    ]
    scratch = [pltpu.VMEM((rows, 32 * rows), jnp.float32)]
    return vmem_call(attend_kernel, out_shape, (q, k, v), scratch, None, "attend")


def attend_back_kernel(q, k, v, probs, grad, exact, dq, dk, dv, dk_sum, dv_sum):
    rows = q.shape[1]
    span = 8 * rows
    scale = HD ** (-0.5)
    at = 0
    for block in range(4):
        low_grad = grad[block]
        delta = jnp.sum(low_grad.astype(jnp.float32) * exact[block], axis=1, keepdims=True)
        total = jnp.zeros((rows, HD), jnp.float32)
        for c in range(block + 1):
            here = slice(c * span, (c + 1) * span)
            low = probs[at]
            back = lax.dot_general(
                low_grad, v[here], (((1,), (1,)), ((), ())), preferred_element_type=jnp.float32
            )
            terms = (low.astype(jnp.float32) * (back - delta)).astype(q.dtype)
            total = total + jnp.dot(terms, k[here], preferred_element_type=jnp.float32)
            over_rows = (((0,), (0,)), ((), ()))
            key_terms = lax.dot_general(
                terms, q[block], over_rows, preferred_element_type=jnp.float32
            )
            value_terms = lax.dot_general(
                low, low_grad, over_rows, preferred_element_type=jnp.float32
            )
            if c == block:
                dk_sum[here] = key_terms
                dv_sum[here] = value_terms
            else:
                dk_sum[here] = dk_sum[here] + key_terms
                dv_sum[here] = dv_sum[here] + value_terms
            at += 1
        dq[block] = (total * scale).astype(dq.dtype)
    for c in range(4):
        here = slice(c * span, (c + 1) * span)
        dk[here] = (dk_sum[here] * scale).astype(dk.dtype)
        dv[here] = dv_sum[here].astype(dv.dtype)


def attend_back(q, k, v, probs, grad, exact):
    out_shape = [jax.ShapeDtypeStruct(x.shape, x.dtype) for x in (q, k, v)]
    scratch = [pltpu.VMEM(k.shape, jnp.float32)] * 2
    return vmem_call(
        attend_back_kernel, out_shape, (q, k, v, probs, grad, exact), scratch, None, "attend_back"
    )


SLOTS = 16


def token_places():
    z, xh, y = own_place()
    w = lax.axis_index("wa")
    return z, xh, y, w // 2, w % 2


def block_device(dz, dx, dy):
    z, xh, y, place, core = token_places()
    there_z, there_x, there_y = (z + dz) % 4, (xh + dx) % 2, (y + dy) % 4
    there = (place + dx) % 2
    where = {"sp": there_z, "ctx": 4 * there_x + there_y, "wa": 2 * there + core}
    return where, there_z * 8 + there_x * 4 + there_y


def greet_blocks():
    barrier = pltpu.get_barrier_semaphore()

    def one(i, carry):
        where, _ = block_device(i // 8, (i // 4) % 2, i % 4)
        pl.semaphore_signal(barrier, inc=1, device_id=where, device_id_type=MESH)
        return carry

    lax.fori_loop(1, 32, one, 0)
    w = lax.axis_index("wa")
    core = w % 2
    for place in (w + 1 - 2 * core, (w + 2) % 4):
        pl.semaphore_signal(barrier, inc=1, device_id={"wa": place}, device_id_type=MESH)
    pl.semaphore_wait(barrier, 33)


def quarter_columns(place, core):
    quarter = D // 4
    return pl.ds(pl.multiple_of(core * 2 * quarter + place * quarter, quarter), quarter)


def dispatch_kernel(count, *refs):
    ins, outs = refs[:count], refs[count : 2 * count]
    out_sem, in_sem, own_sem, send_sem, recv_sem = refs[2 * count :]
    z, xh, y, place, core = token_places()
    w = lax.axis_index("wa")
    beside, across = {"wa": w + 1 - 2 * core}, {"wa": (w + 2) % 4}
    greet_blocks()
    me = z * 8 + xh * 4 + y
    columns = quarter_columns(place, core)
    here = pl.ds(pl.multiple_of(me * SLOTS, SLOTS), SLOTS)
    own = []
    for a in range(count):
        copy = pltpu.make_async_copy(ins[a].at[me], outs[a].at[:, here, columns], own_sem.at[a])
        copy.start()
        own.append(copy)

        def one(i, carry):
            where, block = block_device(i // 8, (i // 4) % 2, i % 4)
            pltpu.make_async_remote_copy(
                src_ref=ins[a].at[block], dst_ref=outs[a].at[:, here, columns],
                send_sem=out_sem.at[a], recv_sem=in_sem.at[a, i // 4],
                device_id=where, device_id_type=MESH,
            ).start()
            return carry

        lax.fori_loop(1, 32, one, 0)

    copies = Copies(send_sem, recv_sem)
    items = [(a, dz, dx) for a in range(count) for dz in range(4) for dx in range(2)]
    items.sort(key=lambda item: (item[0], item[1] + item[2] == 0))
    passed, last = {}, []

    def arrived(i):
        a, dz, dx = items[i]
        rows = pl.ds(pl.multiple_of(((z - dz + 4) % 4 * 8 + (xh + dx) % 2 * 4) * SLOTS, 4 * SLOTS), 4 * SLOTS)
        few = 3 if dz + dx == 0 else 4
        sample = outs[a].at[:, pl.ds(0, few * SLOTS), columns]
        pltpu.make_async_copy(sample, sample, in_sem.at[a, dz * 2 + dx]).wait()
        if dz + dx == 0:
            own[a].wait()
        part = outs[a].at[:, rows, quarter_columns((place + dx) % 2, core)]
        passed[i] = copies.start(part, part, across)
        last.append(copies.start(part, part, beside))

    def from_across(i):
        a, dz, dx = items[i]
        rows = pl.ds(pl.multiple_of(((z - dz + 4) % 4 * 8 + (xh + dx) % 2 * 4) * SLOTS, 4 * SLOTS), 4 * SLOTS)
        passed[i].wait_recv()
        part = outs[a].at[:, rows, quarter_columns((place + dx + 1) % 2, core)]
        last.append(copies.start(part, part, beside))

    for i in range(len(items) + 2):
        if i < len(items):
            arrived(i)
        if i >= 2:
            from_across(i - 2)
    for copy in last:
        copy.wait_recv()
    copies.finish()
    for a in range(count):
        sample = ins[a].at[pl.ds(0, 31)]
        pltpu.make_async_copy(sample, sample, out_sem.at[a]).wait()


def dispatch(arrays, collective_id):
    count = len(arrays)
    shape = jax.ShapeDtypeStruct((2, 32 * SLOTS, D), arrays[0].dtype)
    return pl.pallas_call(
        functools.partial(dispatch_kernel, count),
        out_shape=[shape] * count,
        in_specs=[pl.BlockSpec(memory_space=pl.ANY)] * count,
        out_specs=[pl.BlockSpec(memory_space=pl.ANY)] * count,
        scratch_shapes=[
            pltpu.SemaphoreType.DMA((count,)),
            pltpu.SemaphoreType.DMA((count, 8)),
            pltpu.SemaphoreType.DMA((count,)),
            pltpu.SemaphoreType.DMA((24 * count,)),
            pltpu.SemaphoreType.DMA((24 * count,)),
        ],
        compiler_params=pltpu.CompilerParams(collective_id=collective_id, has_side_effects=True),
        name="dispatch_rows",
    )(*arrays)


def return_kernel(count, *refs):
    ins, outs = refs[:count], refs[count : 2 * count]
    halves, quarters = refs[2 * count : 3 * count], refs[3 * count : 4 * count]
    out_sem, in_sem, send_sem, recv_sem = refs[4 * count :]
    z, xh, y, place, core = token_places()
    w = lax.axis_index("wa")
    beside, across = {"wa": w + 1 - 2 * core}, {"wa": (w + 2) % 4}
    greet_blocks()
    me = z * 8 + xh * 4 + y
    quarter = D // 4
    group = 4 * SLOTS
    mine = pl.ds(pl.multiple_of(core * 2 * quarter, 2 * quarter), 2 * quarter)
    theirs = pl.ds(pl.multiple_of((1 - core) * 2 * quarter, 2 * quarter), 2 * quarter)
    copies = Copies(send_sem, recv_sem)
    items = [(a, dz, dx) for a in range(count) for dz in range(4) for dx in range(2)]
    items.sort(key=lambda item: (item[0], item[1] + item[2] == 0))

    def rows_of(dz, dx):
        return pl.ds(pl.multiple_of(((z + dz) % 4 * 8 + (xh + dx) % 2 * 4) * SLOTS, group), group)

    def kept(dx):
        return pl.ds(pl.multiple_of((place + dx) % 2 * quarter, quarter), quarter)

    def given(dx):
        return pl.ds(pl.multiple_of((place + dx + 1) % 2 * quarter, quarter), quarter)

    paired_up = [
        copies.start(ins[a].at[:, rows_of(dz, dx), theirs], halves[a].at[:, rows_of(dz, dx)], beside)
        for a, dz, dx in items
    ]
    passed = {}

    def add_core(i):
        a, dz, dx = items[i]
        rows = rows_of(dz, dx)
        paired_up[i].wait_recv()
        for e in range(2):
            halves[a][e, rows] = halves[a][e, rows] + ins[a][e, rows, mine]
        passed[i] = copies.start(
            halves[a].at[:, rows, given(dx)], quarters[a].at[:, rows], across
        )

    def add_across(i):
        a, dz, dx = items[i]
        rows = rows_of(dz, dx)
        passed[i].wait_recv()
        for e in range(2):
            quarters[a][e, rows] = quarters[a][e, rows] + halves[a][e, rows, kept(dx)]
        for dy in range(4):
            where, block = block_device(dz, dx, dy)
            part = pl.ds(pl.multiple_of(block * SLOTS, SLOTS), SLOTS)
            if dz + dx + dy == 0:
                outs[a][me] = quarters[a][:, part]
            else:
                pltpu.make_async_remote_copy(
                    src_ref=quarters[a].at[:, part], dst_ref=outs[a].at[me],
                    send_sem=out_sem.at[a], recv_sem=in_sem.at[a],
                    device_id=where, device_id_type=MESH,
                ).start()

    for i in range(len(items) + 1):
        if i < len(items):
            add_core(i)
        if i >= 1:
            add_across(i - 1)
    copies.finish()
    for a in range(count):
        sample = outs[a].at[pl.ds(0, 31)]
        pltpu.make_async_copy(sample, sample, in_sem.at[a]).wait()
        pltpu.make_async_copy(sample, sample, out_sem.at[a]).wait()


def give_back(arrays, collective_id):
    count = len(arrays)
    shape = jax.ShapeDtypeStruct((32, 2, SLOTS, D // 4), arrays[0].dtype)
    rows = 32 * SLOTS
    scratch = [pltpu.VMEM((2, rows, D // 2), arrays[0].dtype)] * count
    scratch += [pltpu.VMEM((2, rows, D // 4), arrays[0].dtype)] * count
    scratch += [pltpu.SemaphoreType.DMA((count,))] * 2 + [pltpu.SemaphoreType.DMA((16 * count,))] * 2
    return vmem_call(
        functools.partial(return_kernel, count), [shape] * count, arrays, scratch, collective_id,
        "return_rows",
    )


def sum_more_kernel(parts, *refs):
    ins, adds, small = refs[:parts], refs[parts : 2 * parts], refs[2 * parts]
    outs, small_out = refs[2 * parts + 1 : 3 * parts + 1], refs[3 * parts + 1]
    got, half, far = (refs[(3 + i) * parts + 2 : (4 + i) * parts + 2] for i in range(3))
    small_got, small_half, small_far, send_sem, recv_sem = refs[6 * parts + 2 :]
    w = lax.axis_index("wa")
    core, place = w % 2, w // 2
    beside, across = {"wa": w + 1 - 2 * core}, {"wa": (w + 2) % 4}
    width = D // 2
    quarter = D // 4
    mine = pl.ds(pl.multiple_of(core * width, width), width)
    theirs = pl.ds(pl.multiple_of((1 - core) * width, width), width)
    own = pl.ds(pl.multiple_of(place * quarter, quarter), quarter)
    greet([beside, across])
    copies = Copies(send_sem, recv_sem)
    one = [copies.start(ins[a].at[:, theirs], got[a], beside) for a in range(parts)]
    one.append(copies.start(small, small_got, beside))
    two = []
    for a in range(parts):
        one[a].wait_recv()
        half[a][...] = ins[a][:, mine] + got[a][...]
        half[a][:, own] = half[a][:, own] + adds[a][...]
        two.append(copies.start(half[a], far[a], across))
    one[parts].wait_recv()
    small_half[...] = small[...] + small_got[...]
    two.append(copies.start(small_half, small_far, across))
    three = []
    for a in range(parts):
        two[a].wait_recv()
        outs[a][:, mine] = half[a][...] + far[a][...]
        three.append(copies.start(outs[a].at[:, mine], outs[a].at[:, mine], beside))
    two[parts].wait_recv()
    small_out[...] = small_half[...] + small_far[...]
    for copy in three:
        copy.wait_recv()
    copies.finish()


def sum_more(arrays, adds, small, collective_id, name):
    parts = len(arrays)
    rows = arrays[0].shape[0]
    dtype = arrays[0].dtype
    scratch = [pltpu.VMEM((rows, D // 2), dtype)] * (3 * parts)
    scratch += [pltpu.VMEM(small.shape, small.dtype)] * 3
    scratch += [pltpu.SemaphoreType.DMA((3 * parts + 2,))] * 2
    out_shape = [jax.ShapeDtypeStruct(x.shape, x.dtype) for x in (*arrays, small)]
    return vmem_call(
        functools.partial(sum_more_kernel, parts), out_shape, (*arrays, *adds, small), scratch,
        collective_id, name,
    )


def over(left, right, dims):
    return lax.dot_general(
        left, right, ((dims[:1], dims[1:]), ((), ())), preferred_element_type=jnp.float32
    )


def swish_parts(pre, lin, act_grads):
    sig = jax.nn.sigmoid(pre)
    swish = pre * sig
    slope = sig * (1.0 + pre * (1.0 - sig))
    return swish * lin, act_grads * lin * slope, act_grads * swish


def expert_kernel(rows, grads, gate, up, down, part, back, gate_grad, up_grad, down_grad):
    low = part.dtype
    x, g = rows[0], grads[0]
    pre = over(x, gate[0], (1, 0))
    lin = over(x, up[0], (1, 0))
    act, pre_grad, lin_grad = swish_parts(pre, lin, over(g, down[0], (1, 1)))
    act, pre_grad, lin_grad = act.astype(low), pre_grad.astype(low), lin_grad.astype(low)
    for at in range(0, D, 512):
        here = slice(at, at + 512)
        part[0, :, here] = over(act, down[0, :, here], (1, 0)).astype(low)
        back[0, :, here] = (
            over(pre_grad, gate[0, here], (1, 1)) + over(lin_grad, up[0, here], (1, 1))
        ).astype(low)
        down_grad[0, :, here] = over(act, g[:, here], (0, 0))
        gate_grad[0, here] = over(x[:, here], pre_grad, (0, 0))
        up_grad[0, here] = over(x[:, here], lin_grad, (0, 0))


def run_experts(rows, grads, gate, up, down):
    operands = (rows, grads, gate, up, down)
    out_shape = [jax.ShapeDtypeStruct(rows.shape, rows.dtype)] * 2
    out_shape += [jax.ShapeDtypeStruct(x.shape, jnp.float32) for x in (gate, up, down)]

    def spec(x):
        return pl.BlockSpec((1, *x.shape[1:]), lambda e: (e, 0, 0))

    return pl.pallas_call(
        expert_kernel,
        grid=(rows.shape[0],),
        out_shape=out_shape,
        in_specs=[spec(x) for x in operands],
        out_specs=[spec(x) for x in out_shape],
        compiler_params=pltpu.CompilerParams(vmem_limit_bytes=VMEM_LIMIT),
        name="run_experts",
    )(*operands)


def shared_kernel(x, g, gate, up, down, part, back, gate_grad, up_grad, down_grad):
    low = part.dtype
    pre = over(x[...], gate[...], (1, 0))
    lin = over(x[...], up[...], (1, 0))
    act, pre_grad, lin_grad = swish_parts(pre, lin, over(g[...], down[...], (1, 0)))
    act, pre_grad, lin_grad = act.astype(low), pre_grad.astype(low), lin_grad.astype(low)
    for at in range(0, D, 512):
        here = slice(at, at + 512)
        part[:, here] = over(act, down[here], (1, 1)).astype(low)
        back[:, here] = (
            over(pre_grad, gate[here], (1, 1)) + over(lin_grad, up[here], (1, 1))
        ).astype(low)
        down_grad[here] = over(g[:, here], act, (0, 0)).astype(low)
        gate_grad[here] = over(x[:, here], pre_grad, (0, 0)).astype(low)
        up_grad[here] = over(x[:, here], lin_grad, (0, 0)).astype(low)


def run_shared(x, g, gate, up, down):
    out_shape = [jax.ShapeDtypeStruct(a.shape, a.dtype) for a in (x, x, gate, up, down)]
    return vmem_call(shared_kernel, out_shape, (x, g, gate, up, down), [], None, "run_shared")


def turned_gather(arrays, axis):
    widths = [a.shape[1] for a in arrays]
    whole = lax.all_gather(jnp.concatenate(arrays, axis=1), axis, axis=0, tiled=True)
    return jnp.split(whole, [sum(widths[:k]) for k in range(1, len(widths))], axis=1)


def rope_tables(positions):
    half_width = HD // 2
    inverse = 1.0 / ROPE_BASE ** (jnp.arange(half_width, dtype=jnp.float32) * 2.0 / HD)
    angles = positions[:, None] * inverse[None, :]
    cosine, sine = jnp.cos(angles), jnp.sin(angles)
    return jnp.concatenate([cosine, cosine], axis=1), jnp.concatenate([-sine, sine], axis=1)


def dot(left, right, over, dtype=jnp.float32, **kept):
    return lax.dot_general(
        left, right, ((over[:1], over[1:]), ((), ())), preferred_element_type=dtype, **kept
    )


def shards(
    tokens,
    cotangent,
    routes,
    attn_gain,
    query_weight,
    key_weight,
    value_weight,
    output_weight,
    mlp_gain,
    router_weight,
    shared_gate,
    shared_up,
    shared_down,
    expert_gate,
    expert_up,
    expert_down,
):
    low = jnp.bfloat16
    local_tokens = tokens.shape[0]
    head_cols = query_weight.shape[1]
    experts_all = router_weight.shape[1]
    groups = ("sp", "ctx")
    device_pos = lax.axis_index("sp") * lax.axis_size("ctx") + lax.axis_index("ctx")
    place, core = lax.axis_index("wa") // 2, lax.axis_index("wa") % 2
    quarter_at = core * (D // 2) + place * (D // 4)

    def quarter(x):
        return lax.dynamic_slice_in_dim(x, quarter_at, D // 4, 1)

    heads = (query_weight, key_weight, value_weight)
    gains = jnp.pad(jnp.stack([attn_gain, mlp_gain], axis=1), ((0, 0), (0, HD - 2)))
    parts = row_parts(heads)
    parts[0].append((3, pl.ds(0, gains.shape[0]), pl.ds(0, HD)))
    full_query, full_key, full_value, full_gains = (
        whole.reshape(D, -1)
        for whole in gather_cube((*heads, gains), parts, 1, "gather_head_weights")
    )
    turned, full_sgate, full_sup, turned_sdown, full_router = turned_gather(
        (
            output_weight.T,
            shared_gate,
            shared_up,
            shared_down.T,
            router_weight,
        ),
        groups,
    )
    gain_one = full_gains[:, 0].astype(jnp.float32)
    gain_two = full_gains[:, 1].astype(jnp.float32)
    tokens_f = tokens.astype(jnp.float32)
    inv_one = lax.rsqrt(jnp.mean(tokens_f * tokens_f, axis=-1, keepdims=True) + EPSILON)
    unit_one = tokens_f * inv_one
    normed = (unit_one * gain_one).astype(low)
    query_pos = device_pos * local_tokens + jnp.arange(local_tokens, dtype=jnp.int32)
    cosine, sine = rope_tables(query_pos.astype(jnp.float32))
    queries, keys, values = project(normed, (full_query, full_key, full_value), cosine, sine)
    head_queries, head_keys, head_values = spread_heads(queries, keys, values, 2)
    head_keys = head_keys.reshape(-1, HD)
    head_values = head_values.reshape(-1, HD)
    head_attended, exact, probs = attend(head_queries, head_keys, head_values)
    attended = heads_out(head_attended, 3)
    attn_part = dot(attended, turned, (1, 1)).astype(low)
    attn_out = sum_wa(attn_part, 4, "sum_attention").astype(jnp.float32)
    hidden_state = tokens_f + attn_out
    inv_two = lax.rsqrt(jnp.mean(hidden_state * hidden_state, axis=-1, keepdims=True) + EPSILON)
    unit_two = hidden_state * inv_two
    mlp_in = (unit_two * gain_two).astype(low)

    logits = dot(mlp_in, full_router, (1, 0))
    logit_exp = jnp.exp(logits - jnp.max(logits, axis=-1, keepdims=True))
    router_probs = logit_exp / jnp.sum(logit_exp, axis=-1, keepdims=True)
    experts = jnp.arange(experts_all, dtype=jnp.int32)
    chosen = jnp.zeros((local_tokens, experts_all), jnp.bool_)
    for j in range(TOP):
        chosen = chosen | (routes[:, j : j + 1] == experts[None, :])
    ids = jnp.arange(local_tokens, dtype=jnp.int32)
    before = (ids[None, :] < ids[:, None]).astype(low)
    rank = dot(before, chosen.astype(low), (1, 0))
    slot_of = jnp.where(chosen, rank, -1.0).astype(low)
    slot_ids = jnp.arange(experts_all * SLOTS, dtype=jnp.int32)
    widen = (experts[:, None] == slot_ids[None, :] // SLOTS).astype(low)
    taken = dot(slot_of, widen, (1, 0)) == (slot_ids % SLOTS).astype(jnp.float32)[None, :]
    probs_high = router_probs.astype(low)
    probs_rest = (router_probs - probs_high.astype(jnp.float32)).astype(low)
    pick = taken.astype(low)
    gate_high = jnp.where(taken, dot(probs_high, widen, (1, 0)), 0.0).astype(low)
    gate_rest = jnp.where(taken, dot(probs_rest, widen, (1, 0)), 0.0).astype(low)
    grad_quarter = quarter(cotangent)
    send_rows = dot(pick, quarter(mlp_in), (0, 0)).astype(low)
    send_grads = (
        dot(gate_high, grad_quarter, (0, 0)) + dot(gate_rest, grad_quarter, (0, 0))
    ).astype(low)
    shared_part, shared_in_part, *mlp_grads = run_shared(
        mlp_in, cotangent, full_sgate, full_sup, turned_sdown
    )
    mlp_grads = [x.reshape(4, 2, 4, x.shape[0] // 32, x.shape[1]) for x in mlp_grads]
    gate_share, up_share, down_share = reduce_cube(
        mlp_grads, row_parts(mlp_grads), 11, "reduce_mlp_grads"
    )
    by_owner = (32, 2, SLOTS, D // 4)
    rows_in, grads_in = dispatch((send_rows.reshape(by_owner), send_grads.reshape(by_owner)), 5)

    expert_part, rows_part, expert_gate_grad, expert_up_grad, expert_down_grad = run_experts(
        rows_in, grads_in, expert_gate, expert_up, expert_down
    )
    returned, rows_back = (
        x.reshape(-1, D // 4) for x in give_back((expert_part, rows_part), 6)
    )
    routed = (dot(gate_high, returned, (1, 0)) + dot(gate_rest, returned, (1, 0))).astype(low)
    routed_in = dot(pick, rows_back, (1, 0)).astype(low)
    slot_grads = jnp.where(taken, dot(grad_quarter, returned, (1, 1)), 0.0)
    prob_part = dot(slot_grads, widen.astype(jnp.float32), (1, 1), precision=PRECISE)
    prob_part = jnp.pad(prob_part, ((0, 0), (0, HD - experts_all)))
    mixed, mixed_in, prob_grads = sum_more(
        (shared_part, shared_in_part), (routed, routed_in), prob_part, 7, "sum_mlp"
    )
    block_out = (hidden_state + mixed.astype(jnp.float32)).astype(low)
    prob_grads = prob_grads[:, :experts_all]
    logit_grads = router_probs * (
        prob_grads - jnp.sum(router_probs * prob_grads, axis=-1, keepdims=True)
    )
    router_in_grad = dot(
        logit_grads, full_router.astype(jnp.float32), (1, 1), precision=PRECISE
    )
    mlp_in_grad = router_in_grad + mixed_in.astype(jnp.float32)
    gain_two_grad = jnp.sum(mlp_in_grad * unit_two, axis=0)
    scaled_two = mlp_in_grad * gain_two
    hidden_grad = cotangent.astype(jnp.float32) + inv_two * (
        scaled_two - unit_two * jnp.mean(scaled_two * unit_two, axis=-1, keepdims=True)
    )
    out_grad = hidden_grad.astype(low)
    router_grad = dot(mlp_in, logit_grads.astype(low), (0, 0))

    attended_grad = dot(out_grad, turned, (1, 0)).astype(low)
    head_grad = heads_in(attended_grad, 8)
    dq, dk, dv = attend_back(head_queries, head_keys, head_values, probs, head_grad, exact)
    by_block = (4, 2, 4, local_tokens, HD)
    query_grads, key_grads, value_in = collect_heads(
        dq, dk.reshape(by_block), dv.reshape(by_block), 9
    )
    query_in, key_in = turn_back(query_grads, key_grads, cosine, sine)
    normed_part = (
        dot(query_in, full_query, (1, 1))
        + dot(key_in, full_key, (1, 1))
        + dot(value_in, full_value, (1, 1))
    ).astype(low)
    normed_grad = sum_wa(normed_part, 10, "sum_normed_grad").astype(jnp.float32)
    gain_one_grad = jnp.sum(normed_grad * unit_one, axis=0)
    scaled_one = normed_grad * gain_one
    tokens_grad = (
        hidden_grad
        + inv_one
        * (scaled_one - unit_one * jnp.mean(scaled_one * unit_one, axis=-1, keepdims=True))
    ).astype(low)

    gain_grads = jnp.stack([gain_one_grad, gain_two_grad], axis=1)
    small_grads = jnp.pad(
        jnp.concatenate([router_grad, gain_grads], axis=1), ((0, 0), (0, HD - 2 - experts_all))
    )

    def by_shard(x):
        return x.astype(low).reshape(4, 2, 4, x.shape[0] // 32, x.shape[1])

    attention_grads = [
        by_shard(dot(left, right, (0, 0)))
        for left, right in (
            (normed, query_in),
            (normed, key_in),
            (normed, value_in),
            (out_grad, attended),
        )
    ]
    parts = whole_parts(attention_grads)
    attention_grads.append(by_shard(small_grads))
    parts[0].append((4, pl.ds(0, attention_grads[4].shape[3]), pl.ds(0, HD)))
    query_share, key_share, value_share, output_share, small_share = reduce_cube(
        attention_grads, parts, 12, "reduce_attention_grads"
    )
    return (
        block_out,
        tokens_grad,
        small_share[:, experts_all],
        query_share,
        key_share,
        value_share,
        output_share.T,
        small_share[:, experts_all + 1],
        small_share[:, :experts_all],
        gate_share,
        up_share,
        down_share.T,
        expert_gate_grad,
        expert_up_grad,
        expert_down_grad,
    )


def solution(mesh):
    placed = (
        P(("sp", "ctx"), None),
        P(("sp", "ctx"), None),
        P(("sp", "ctx"), None),
        P(("sp", "ctx")),
        P(("sp", "ctx"), "wa"),
        P(("sp", "ctx"), "wa"),
        P(("sp", "ctx"), "wa"),
        P("wa", ("sp", "ctx")),
        P(("sp", "ctx")),
        P(("sp", "ctx"), None),
        P(("sp", "ctx"), "wa"),
        P(("sp", "ctx"), "wa"),
        P("wa", ("sp", "ctx")),
        P(("sp", "ctx"), None, "wa"),
        P(("sp", "ctx"), None, "wa"),
        P(("sp", "ctx"), "wa", None),
    )
    return jax.shard_map(
        shards,
        mesh=mesh,
        in_specs=placed,
        out_specs=(
            P(("sp", "ctx"), None),
            P(("sp", "ctx"), None),
            P(("sp", "ctx")),
            P(("sp", "ctx"), "wa"),
            P(("sp", "ctx"), "wa"),
            P(("sp", "ctx"), "wa"),
            P("wa", ("sp", "ctx")),
            P(("sp", "ctx")),
            P(("sp", "ctx"), None),
            P(("sp", "ctx"), "wa"),
            P(("sp", "ctx"), "wa"),
            P("wa", ("sp", "ctx")),
            P(("sp", "ctx"), None, "wa"),
            P(("sp", "ctx"), None, "wa"),
            P(("sp", "ctx"), "wa", None),
        ),
        check_vma=False,
    )
```

time: 1010 us -> 627 us (0.62)
  local copies, waits for them, and re-layouts: 181 us -> 39.4 us
  Pallas kernels: 382 us -> 513 us
  waiting for transfers between devices: 127 us -> 0.5 us
  blocking collectives: 119 us -> 0 us
  matrix products: 121 us -> 34.6 us
  other arithmetic: 46.9 us -> 13.5 us
    pallas_call x0 -> x13, Pallas kernels: none -> 290 us  [the longest x11 202 us: vmem_call(): pl.pallas_call(kernel, out_shape=out_shape, in_specs=[pl.BlockSpec(memory...]
    all_to_all x4 -> x0, blocking collectives: 119 us -> none  [the longest x2 66.6 us: back_share(): lax.all_to_all(share, ('sp', 'ctx'), split_axis=0, concat_axis=0, tiled=T...]
    dot_general x37 -> x23, matrix products: 121 us -> 34.6 us  [dot(): lax.dot_general(left, right, ((over[:1], over[1:]), ((), ())), preferred_...]
    pallas_call x2 -> x1, Pallas kernels: 137 us -> 68.1 us  [gather_cube(): pl.pallas_call(functools.partial(gather_kernel, parts, count), out_shape=...]
    reduce_scatter x2 -> x0, waiting for transfers between devices: 63.3 us -> none  [back_share(): lax.psum_scatter(expert_part.astype(jnp.bfloat16), 'wa', scatter_dimensio...]
    all_gather x5 -> x1, waiting for transfers between devices: 63.3 us -> 0.48 us  [turned_gather(): lax.all_gather(jnp.concatenate(arrays, axis=1), axis, axis=0, tiled=True)]
    reshape x12 -> x0, local copies, waits for them, and re-layouts: 54.9 us -> none  [the longest x4 30.6 us: shards(): part.astype(jnp.bfloat16).reshape(4, 2, 4, local_tokens, head_cols)]
    pallas_call x3 -> x2, Pallas kernels: 173 us -> 118 us  [reduce_cube(): pl.pallas_call(functools.partial(reduce_kernel, parts, count), out_shape=...]
  transfers between devices with their start and end apart: 7 -> 1, of which waited for: 4 -> 1; matrix products, arithmetic and copies ran while one was open for 12% -> 2% of each run, Pallas kernels for 12% -> 21%
where the time goes in v2:
time: 627 us; the launch traced here: 616 us
  Pallas kernels  513 us (82%)
  local copies, waits for them, and re-layouts  39.4 us (6%)
  matrix products  34.6 us (6%)
  between operations  14.8 us (2%)
  other arithmetic  13.5 us (2%)
    pallas_call x11, Pallas kernels, vmem_call(): pl.pallas_call(kernel, out_shape=out_shape, in_specs=[pl.BlockSpec(memory...  202 us
    pallas_call x2, Pallas kernels, reduce_cube(): pl.pallas_call(functools.partial(reduce_kernel, parts, count), out_shape=...  118 us
    pallas_call x1, Pallas kernels, gather_cube(): pl.pallas_call(functools.partial(gather_kernel, parts, count), out_shape=...  68.1 us
    pallas_call x1, Pallas kernels, dispatch(): pl.pallas_call(functools.partial(dispatch_kernel, count), out_shape=[shap...  60.9 us
    pallas_call x2, Pallas kernels, sum_wa(): pl.pallas_call(sum_wa_kernel, out_shape=jax.ShapeDtypeStruct(x.shape, x.d...  36.2 us
    dot_general x23, matrix products, dot(): lax.dot_general(left, right, ((over[:1], over[1:]), ((), ())), preferred_...  34.6 us
    pallas_call x1, Pallas kernels, run_experts(): pl.pallas_call(expert_kernel, grid=(rows.shape[0],), out_shape=out_shape,...  27.2 us
    unnamed x67, local copies, waits for them, and re-layouts  26.6 us
  transfers between devices with their start and end apart: 1, of which 1 were waited for; matrix products, arithmetic and copies ran while one was open for 2% of the time, Pallas kernels for 21%

profile of v2, /device:TPU:1, one launch (start us, length us, event | category | flops | bytes accessed | tf_op | source)
XLA Modules:
  0.0 615.9 jit_solution(3230444981277135641)
XLA Ops:
  7.2 1.9 concatenate.15
  9.2 0.8 pad_maximum_fusion.3
  10.1 4.6 copy.55.gate
  14.7 2.8 copy.56.up
  17.5 0.6 pad.13.refs_3_
  18.1 68.1 %gather_head_weights.1 = (bf16[4,2,4,64,512]{4,3,2,1,0:T(8,128)(2,1)}, bf16[4,2,4,64,512]{4,3,2,1,0:T(8,128)(2,1)}, bf16[4,2,4,64,512]{4,3,2,1,0:T(8,128)(2,1)}, bf16[4,2,4,64,128]{4,3,2,1,0:T(8,128)(2,1)}) custom-call(bf16[64,512]{1,0:T(8,128)(2,1)} %refs_0_.1, bf16[64,512]{1,0:T(8,128)(2,1)} %refs_1_.1, bf16[64,512]{1,0:T(8,128)(2,1)} %refs_2_.1, ...), custom_call_target="tpu_custom_call" | custom-call | tf_op jit(solution)/shard_map/gather_head_weights/pallas_call | solution.py:158
  86.2 1.5 slice_convert_fusion
  88.7 0.8 pad_maximum_fusion.1
  89.7 1.0 fusion.19.normed
  90.7 4.7 project_heads.1
  95.4 41.2 %spread_heads.1 = (bf16[4,128,128]{2,1,0:T(8,128)(2,1)}, bf16[4,2,4,128,128]{4,3,2,1,0:T(8,128)(2,1)}, bf16[4,2,4,128,128]{4,3,2,1,0:T(8,128)(2,1)}) custom-call(bf16[128,512]{1,0:T(8,128)(2,1)} %get-tuple-element.65.q, bf16[128,512]{1,0:T(8,128)(2,1)} %get-tuple-element.66.k, bf16[128,512]{1,0:T(8,128)(2,1)} %get-tuple-element.67.v), custom_call_target="tpu_custom_call" | custom-call | tf_op jit(solution)/shard_map/spread_heads/pallas_call | solution.py:431
  136.6 7.2 %attend.1 = (bf16[4,128,128]{2,1,0:T(8,128)(2,1)}, f32[4,128,128]{2,1,0:T(8,128)}, bf16[10,128,1024]{2,1,0:T(8,128)(2,1)}) custom-call(bf16[4,128,128]{2,1,0:T(8,128)(2,1)} %get-tuple-element.68.q, bf16[4096,128]{1,0:T(8,128)(2,1)} %bitcast.81, bf16[4096,128]{1,0:T(8,128)(2,1)} %bitcast.83), custom_call_target="tpu_custom_call" | custom-call | tf_op jit(solution)/shard_map/attend/pallas_call | solution.py:431
  143.8 7.3 %heads_to_tokens.1 = bf16[128,512]{1,0:T(8,128)(2,1)} custom-call(bf16[4,128,128]{2,1,0:T(8,128)(2,1)} %get-tuple-element.71.x), custom_call_target="tpu_custom_call" | custom-call | tf_op jit(solution)/shard_map/heads_to_tokens/pallas_call | solution.py:431
  152.0 3.3 convolution_convert_fusion.4.x
  155.3 14.6 %sum_attention.1 = bf16[128,2048]{1,0:T(8,128)(2,1)} custom-call(bf16[128,2048]{1,0:T(8,128)(2,1)} %convolution_convert_fusion.4.x), custom_call_target="tpu_custom_call" | custom-call | tf_op jit(solution)/shard_map/sum_attention/pallas_call | solution.py:381
  170.0 1.4 multiply_reduce_fusion.2
  171.3 1.3 multiply_convert_fusion.x
  172.6 1.8 fusion.83
  175.3 1.5 convolution_convert_fusion.6
  177.3 1.4 add_convert_fusion
  178.7 60.9 %dispatch_rows.1 = (bf16[2,512,2048]{2,1,0:T(8,128)(2,1)}, bf16[2,512,2048]{2,1,0:T(8,128)(2,1)}) custom-call(bf16[32,2,16,512]{3,2,1,0:T(8,128)(2,1)} %bitcast.85, bf16[32,2,16,512]{3,2,1,0:T(8,128)(2,1)} %bitcast.86), custom_call_target="tpu_custom_call" | custom-call | tf_op jit(solution)/shard_map/dispatch_rows/pallas_call | solution.py:861
  239.6 27.2 %run_experts.1 = (bf16[2,512,2048]{2,1,0:T(8,128)(2,1)}, bf16[2,512,2048]{2,1,0:T(8,128)(2,1)}, f32[2,2048,352]{2,1,0:T(8,128)}, f32[2,2048,352]{2,1,0:T(8,128)}, f32[2,352,2048]{2,1,0:T(8,128)}) custom-call(bf16[2,512,2048]{2,1,0:T(8,128)(2,1)} %get-tuple-element.74.rows, bf16[2,512,2048]{2,1,0:T(8,128)(2,1)} %get-tuple-element.75.grads, ...), custom_call_target="tpu_custom_call" | custom-call | tf_op jit(solution)/shard_map/run_experts/pallas_call | solution.py:1054
  266.8 62.3 %return_rows.1 = (bf16[32,2,16,512]{3,2,1,0:T(8,128)(2,1)}, bf16[32,2,16,512]{3,2,1,0:T(8,128)(2,1)}) custom-call(bf16[2,512,2048]{2,1,0:T(8,128)(2,1)} %get-tuple-element.76.refs_0_, bf16[2,512,2048]{2,1,0:T(8,128)(2,1)} %get-tuple-element.77.refs_1_), custom_call_target="tpu_custom_call" | custom-call | tf_op jit(solution)/shard_map/return_rows/pallas_call | solution.py:431
  329.1 1.7 fusion.84
  330.8 1.7 convolution_select_fusion
  332.5 1.0 fusion.14.refs_2_
  333.9 1.0 convolution_convert_fusion.7.refs_3_
  334.9 0.6 pad.14.refs_4_
  335.5 7.0 %fusion.82 = (bf16[2048,704]{1,0:T(8,128)(2,1)}, bf16[2048,704]{1,0:T(8,128)(2,1)}, bf16[2048,704]{1,0:T(8,128)(2,1)}) fusion(bf16[2048,2688]{1,0:T(8,128)(2,1)} %all-gather.2.cloned.1.call-done), kind=kLoop, calls=%fused_computation.134 | loop fusion | bytes 17301504 | tf_op jit(solution)/shard_map/split | solution.py:1090
  342.5 14.3 %run_shared.1 = (bf16[128,2048]{1,0:T(8,128)(2,1)}, bf16[128,2048]{1,0:T(8,128)(2,1)}, bf16[2048,704]{1,0:T(8,128)(2,1)}, bf16[2048,704]{1,0:T(8,128)(2,1)}, bf16[2048,704]{1,0:T(8,128)(2,1)}) custom-call(bf16[128,2048]{1,0:T(8,128)(2,1)} %copy-done.2, bf16[128,2048]{1,0:T(8,128)(2,1)} %g.1, bf16[2048,704]{1,0:T(8,128)(2,1)} %get-tuple-element.160.gate, ...), custom_call_target="tpu_custom_call" | custom-call | tf_op jit(solution)/shard_map/run_shared/pallas_call | solution.py:431
  356.8 22.2 %sum_mlp.1 = (bf16[128,2048]{1,0:T(8,128)(2,1)}, bf16[128,2048]{1,0:T(8,128)(2,1)}, f32[128,128]{1,0:T(8,128)}) custom-call(bf16[128,2048]{1,0:T(8,128)(2,1)} %get-tuple-element.72.refs_0_, bf16[128,2048]{1,0:T(8,128)(2,1)} %get-tuple-element.73.refs_1_, bf16[128,512]{1,0:T(8,128)(2,1)} %fusion.14.refs_2_, ...), custom_call_target="tpu_custom_call" | custom-call | tf_op jit(solution)/shard_map/sum_mlp/pallas_call | solution.py:431
  379.0 1.1 multiply_reduce_fusion.3
  380.1 1.2 convolution_convert_fusion.5
  381.3 2.3 multiply_reduce_fusion
  383.7 1.3 multiply_add_fusion
  385.0 2.0 convolution_convert_fusion
  387.1 2.7 fusion.11.x
  389.8 6.7 %tokens_to_heads.1.grad = bf16[4,128,128]{2,1,0:T(8,128)(2,1)} custom-call(bf16[128,512]{1,0:T(8,128)(2,1)} %fusion.11.x), custom_call_target="tpu_custom_call" | custom-call | tf_op jit(solution)/shard_map/tokens_to_heads/pallas_call | solution.py:431
  396.5 7.7 %attend_back.1 = (bf16[4,128,128]{2,1,0:T(8,128)(2,1)}, bf16[4096,128]{1,0:T(8,128)(2,1)}, bf16[4096,128]{1,0:T(8,128)(2,1)}) custom-call(bf16[4,128,128]{2,1,0:T(8,128)(2,1)} %get-tuple-element.68.q, bf16[4096,128]{1,0:T(8,128)(2,1)} %bitcast.82, bf16[4096,128]{1,0:T(8,128)(2,1)} %bitcast.84, bf16[10,128,1024]{2,1,0:T(8,128)(2,1)} %get-tuple-element.83.probs, ...), custom_call_target="tpu_custom_call" | custom-call | tf_op jit(solution)/shard_map/attend_back/pallas_call | solution.py:431
  404.2 26.8 %collect_heads.1 = (bf16[128,512]{1,0:T(8,128)(2,1)}, bf16[128,512]{1,0:T(8,128)(2,1)}, bf16[128,512]{1,0:T(8,128)(2,1)}) custom-call(bf16[4,128,128]{2,1,0:T(8,128)(2,1)} %get-tuple-element.85.dq, bf16[4,2,4,128,128]{4,3,2,1,0:T(8,128)(2,1)} %bitcast.93, bf16[4,2,4,128,128]{4,3,2,1,0:T(8,128)(2,1)} %bitcast.94), custom_call_target="tpu_custom_call" | custom-call | tf_op jit(solution)/shard_map/collect_heads/pallas_call | solution.py:431
  431.0 1.8 turn_back_heads.1
  432.8 2.5 fusion.85
  435.4 2.1 convolution_convert_fusion.3
  437.4 56.2 %reduce_mlp_grads.1 = (f32[64,704]{1,0:T(8,128)}, f32[64,704]{1,0:T(8,128)}, f32[64,704]{1,0:T(8,128)}) custom-call(bf16[4,2,4,64,704]{4,3,2,1,0:T(8,128)(2,1)} %bitcast.87, bf16[4,2,4,64,704]{4,3,2,1,0:T(8,128)(2,1)} %bitcast.88, bf16[4,2,4,64,704]{4,3,2,1,0:T(8,128)(2,1)} %bitcast.89), custom_call_target="tpu_custom_call" | custom-call | tf_op jit(solution)/shard_map/reduce_mlp_grads/pallas_call | solution.py:309
  493.6 2.0 convolution_convert_fusion.2
  495.7 0.8 convolution_add_fusion.1
  496.5 2.1 convolution_convert_fusion.1
  498.6 1.6 fusion.x
  500.2 21.6 %sum_normed_grad.1 = bf16[128,2048]{1,0:T(8,128)(2,1)} custom-call(bf16[128,2048]{1,0:T(8,128)(2,1)} %fusion.x), custom_call_target="tpu_custom_call" | custom-call | tf_op jit(solution)/shard_map/sum_normed_grad/pallas_call | solution.py:381
  521.8 1.5 fusion.21
  523.3 2.2 fusion.18
  525.9 0.9 pad.15.clone
  526.8 62.3 %reduce_attention_grads.1 = (f32[64,512]{1,0:T(8,128)}, f32[64,512]{1,0:T(8,128)}, f32[64,512]{1,0:T(8,128)}, f32[64,512]{1,0:T(8,128)}, f32[64,128]{1,0:T(8,128)}) custom-call(bf16[4,2,4,64,512]{4,3,2,1,0:T(8,128)(2,1)} %bitcast.72, bf16[4,2,4,64,512]{4,3,2,1,0:T(8,128)(2,1)} %bitcast.73, bf16[4,2,4,64,512]{4,3,2,1,0:T(8,128)(2,1)} %bitcast.74, ...), custom_call_target="tpu_custom_call" | custom-call | tf_op jit(solution)/shard_map/reduce_attention_grads/pallas_call | solution.py:309
  589.1 1.5 slice_reduce_fusion
  590.7 6.4 %copy.59 = f32[2,2048,352]{1,2,0:T(8,128)} copy(f32[2,2048,352]{2,1,0:T(8,128)} %get-tuple-element.149) | data formatting | bytes 11534336
  597.1 6.5 %copy.60 = f32[2,2048,352]{1,2,0:T(8,128)} copy(f32[2,2048,352]{2,1,0:T(8,128)} %get-tuple-element.150) | data formatting | bytes 11534336
  603.6 0.7 copy.81
  604.2 0.7 copy.82
  604.9 0.7 copy.83
  605.5 0.7 copy.84
  606.2 0.6 copy.85
  606.8 0.7 copy.86
  607.5 0.7 copy.87
  608.2 0.7 copy.88
  (79 shorter events, 4.4 us)
Async XLA Ops:
  7.2 144.9 %all-gather.2.cloned.1.call-start = ((), (), s32[]{:S(2)}) async-start(), calls=%async_computation | async-start | bytes 11354112 | tf_op jit(solution)/shard_map/all_gather | solution.py:1089
  9.1 5.6 copy-start.10
  17.5 72.0 %copy-start = (bf16[128,2048]{1,0:T(8,128)(2,1)S(1)}, bf16[128,2048]{1,0:T(8,128)(2,1)}, u32[]{:S(2)}) copy-start(bf16[128,2048]{1,0:T(8,128)(2,1)} %param.16) | copy-start | bytes 1572868
  90.7 60.4 %copy-start.25 = (s32[128,6]{0,1:T(8,128)S(1)}, s32[128,6]{0,1:T(8,128)}, u32[]{:S(2)}) copy-start(s32[128,6]{0,1:T(8,128)} %param.18) | copy-start | bytes 9220
  170.0 6.8 %copy-start.8 = (bf16[128,2048]{1,0:T(8,128)(2,1)S(1)}, bf16[128,2048]{1,0:T(8,128)(2,1)}, u32[]{:S(2)}) copy-start(bf16[128,2048]{1,0:T(8,128)(2,1)} %g.1) | copy-start | bytes 1572868
  172.6 4.6 copy-start.2
  329.1 3.4 copy-start.4
  329.1 4.8 copy-start.11
  342.5 37.6 %copy-start.3 = (bf16[128,2048]{1,0:T(8,128)(2,1)S(1)}, bf16[128,2048]{1,0:T(8,128)(2,1)}, u32[]{:S(2)}) copy-start(bf16[128,2048]{1,0:T(8,128)(2,1)} %copy-done.2) | copy-start | bytes 1572868
  342.5 38.8 %copy-start.7 = (bf16[128,2048]{1,0:T(8,128)(2,1)S(1)}, bf16[128,2048]{1,0:T(8,128)(2,1)}, u32[]{:S(2)}) copy-start(bf16[128,2048]{1,0:T(8,128)(2,1)} %sum_attention.1) | copy-start | bytes 1572868
  356.8 26.9 %copy-start.9 = (bf16[128,2048]{1,0:T(8,128)(2,1)S(1)}, bf16[128,2048]{1,0:T(8,128)(2,1)}, u32[]{:S(2)}) copy-start(bf16[128,2048]{1,0:T(8,128)(2,1)} %g.1) | copy-start | bytes 1572868
  379.0 4.7 copy-start.13
  383.7 1.4 copy-start.12
  404.2 31.2 %copy-start.1 = (bf16[128,2048]{1,0:T(8,128)(2,1)S(1)}, bf16[128,2048]{1,0:T(8,128)(2,1)}, u32[]{:S(2)}) copy-start(bf16[128,2048]{1,0:T(8,128)(2,1)} %fusion.19.normed) | copy-start | bytes 1572868
  432.8 2.5 copy-start.15
  437.4 56.2 %copy-start.14 = (bf16[128,512]{1,0:T(8,128)(2,1)S(1)}, bf16[128,512]{1,0:T(8,128)(2,1)}, u32[]{:S(2)}) copy-start(bf16[128,512]{1,0:T(8,128)(2,1)} %get-tuple-element.91) | copy-start | bytes 393220
  493.6 2.1 copy-start.6
  493.6 2.9 copy-start.16
  495.7 2.9 copy-start.5
  597.0 6.5 %copy-start.24 = (f32[64,512]{1,0:T(8,128)S(1)}, f32[64,512]{1,0:T(8,128)}, u32[]{:S(2)}) copy-start(f32[64,512]{1,0:T(8,128)} %get-tuple-element.199) | copy-start | bytes 393220
  597.0 7.2 %copy-start.23 = (f32[64,512]{1,0:T(8,128)S(1)}, f32[64,512]{1,0:T(8,128)}, u32[]{:S(2)}) copy-start(f32[64,512]{1,0:T(8,128)} %get-tuple-element.200) | copy-start | bytes 393220
  597.0 7.8 %copy-start.22 = (f32[64,512]{1,0:T(8,128)S(1)}, f32[64,512]{1,0:T(8,128)}, u32[]{:S(2)}) copy-start(f32[64,512]{1,0:T(8,128)} %get-tuple-element.201) | copy-start | bytes 393220
  597.0 8.5 %copy-start.21 = (f32[64,512]{1,0:T(8,128)S(1)}, f32[64,512]{1,0:T(8,128)}, u32[]{:S(2)}) copy-start(f32[64,512]{1,0:T(8,128)} %get-tuple-element.97) | copy-start | bytes 393220
  597.1 9.1 %copy-start.17 = (f32[64,128]{1,0:T(8,128)S(1)}, f32[64,128]{1,0:T(8,128)}, u32[]{:S(2)}) copy-start(f32[64,128]{1,0:T(8,128)} %get-tuple-element.93) | copy-start | bytes 98308
  597.1 9.7 %copy-start.20 = (f32[64,704]{1,0:T(8,128)S(1)}, f32[64,704]{1,0:T(8,128)}, u32[]{:S(2)}) copy-start(f32[64,704]{1,0:T(8,128)} %get-tuple-element.205) | copy-start | bytes 540676
  597.1 10.4 %copy-start.19 = (f32[64,704]{1,0:T(8,128)S(1)}, f32[64,704]{1,0:T(8,128)}, u32[]{:S(2)}) copy-start(f32[64,704]{1,0:T(8,128)} %get-tuple-element.206) | copy-start | bytes 540676
  597.1 11.1 %copy-start.18 = (f32[64,704]{1,0:T(8,128)S(1)}, f32[64,704]{1,0:T(8,128)}, u32[]{:S(2)}) copy-start(f32[64,704]{1,0:T(8,128)} %get-tuple-element.103) | copy-start | bytes 540676
Sparse Core Ops, SparseCore 0:
  11.6 140.3 all-gather.1

commit v3 on v2

--- a/solution.py
+++ b/solution.py
@@ -16,6 +16,8 @@
 ROPE_BASE = 10000.0
 MASKED = -1e30
 PRECISE = lax.Precision.HIGHEST
+
+
 MESH = pl.DeviceIdType.MESH
 VMEM_LIMIT = 60 * 1024 * 1024
 
@@ -45,13 +47,9 @@
     return {"ctx": 4 * (1 - xh) + y}
 
 
-def greet_cube():
-    barrier = pltpu.get_barrier_semaphore()
-    for axis in ("z", "y"):
-        for kind in ("A", "B"):
-            pl.semaphore_signal(barrier, inc=1, device_id=neighbour(axis, kind), device_id_type=MESH)
-    pl.semaphore_signal(barrier, inc=1, device_id=neighbour("x", "A"), device_id_type=MESH)
-    pl.semaphore_wait(barrier, 5)
+def cube_places():
+    rings = [neighbour(axis, kind) for axis in ("z", "y") for kind in ("A", "B")]
+    return rings + [neighbour("x", "A")]
 
 
 def pair_slots(i, kind):
@@ -69,29 +67,70 @@
 def slot_in_pair(i, kind):
     return i % 2 if kind == "A" else 0
 
-
-def gather_kernel(parts, count, *refs):
-    ins, outs = refs[:count], refs[count : 2 * count]
-    send_sem, recv_sem, local_sem = refs[2 * count :]
-    z, xh, y = own_place()
-    used = [0]
-    started = []
-
-    def start(src, dst, where):
-        k = used[0]
-        used[0] += 1
+def head_columns(h):
+    return pl.ds(pl.multiple_of(h * HD, HD), HD)
+
+
+class Copies:
+    def __init__(self, send_sem, recv_sem):
+        self.send_sem, self.recv_sem, self.started = send_sem, recv_sem, []
+
+    def start(self, src, dst, where):
+        k = len(self.started)
         copy = pltpu.make_async_remote_copy(
-            src_ref=src, dst_ref=dst, send_sem=send_sem.at[k], recv_sem=recv_sem.at[k],
-            device_id=where, device_id_type=MESH,
+            src_ref=src, dst_ref=dst, send_sem=self.send_sem.at[k],
+            recv_sem=self.recv_sem.at[k], device_id=where, device_id_type=MESH,
         )
         copy.start()
-        started.append(copy)
+        self.started.append(copy)
         return copy
+
+    def finish(self):
+        for copy in self.started:
+            copy.wait_send()
+
+
+def run(*programs):
+    programs = list(programs)
+    while programs:
+        programs = [program for program in programs if next(program, None) is not None]
+
+
+def greet(places):
+    barrier = pltpu.get_barrier_semaphore()
+    for place in places:
+        pl.semaphore_signal(barrier, inc=1, device_id=place, device_id_type=MESH)
+    pl.semaphore_wait(barrier, len(places))
+
+
+def along_z():
+    z = lax.axis_index("sp")
+    return [{"sp": (z + d) % 4} for d in (1, 2, 3)]
+
+
+def vmem_call(kernel, out_shape, operands, scratch, collective_id, name, **params):
+    return pl.pallas_call(
+        kernel,
+        out_shape=out_shape,
+        in_specs=[pl.BlockSpec(memory_space=pltpu.VMEM)] * len(operands),
+        out_specs=jax.tree.map(lambda _: pl.BlockSpec(memory_space=pltpu.VMEM), out_shape),
+        scratch_shapes=scratch,
+        compiler_params=pltpu.CompilerParams(
+            collective_id=collective_id,
+            has_side_effects=collective_id is not None,
+            vmem_limit_bytes=VMEM_LIMIT,
+        ),
+        name=name,
+        **params,
+    )(*operands)
+
+def gather_steps(parts, ins, outs, copies, local_sem):
+    z, xh, y = own_place()
+    count = len(ins)
 
     def step(lane, p, s):
         ring1, ring2 = ORDERS[p][0][0], ORDERS[p][2][0]
-        axis, kind = ORDERS[p][s]
-        where = neighbour(axis, kind)
+        where = neighbour(*ORDERS[p][s])
         xl = xh if lane == 0 else 1 - xh
         zs, ys = [pl.ds(z, 1)], [pl.ds(y, 1)]
         full = [pl.ds(0, 4)]
@@ -103,15 +142,14 @@
         if s == 3:
             other = [d for d, _ in pair_slots(z if ring2 == "z" else y, ORDERS[p][2][1])]
             zs, ys = (other, ys) if ring2 == "z" else (zs, other)
-        copies = []
+        started = []
         for a, rows, cols in parts[p]:
             for zd in zs:
                 for yd in ys:
                     place = outs[a].at[zd, pl.ds(xl, 1), yd, rows, cols]
-                    copies.append(start(place, place, where))
-        return copies
-
-    greet_cube()
+                    started.append(copies.start(place, place, where))
+        return started
+
     local = [
         pltpu.make_async_copy(ins[a], outs[a].at[z, xh, y], local_sem.at[a]) for a in range(count)
     ]
@@ -119,7 +157,9 @@
         copy.start()
     across = [
         [
-            start(ins[a].at[rows, cols], outs[a].at[z, xh, y, rows, cols], neighbour("x", "A"))
+            copies.start(
+                ins[a].at[rows, cols], outs[a].at[z, xh, y, rows, cols], neighbour("x", "A")
+            )
             for a, rows, cols in part
         ]
         for part in parts
@@ -127,29 +167,22 @@
     for copy in local:
         copy.wait()
     flying = {}
-
-    def advance(lane, s):
+    for lane, s in (
+        (0, 0), (0, 1), (1, 0), (0, 2), (1, 1), (0, 3), (1, 2), (1, 3), (0, 4), (1, 4)
+    ):
         for p in range(4):
-            if s == 0 and lane == 1:
-                for copy in across[p]:
-                    copy.wait_recv()
-            if s > 0:
-                for copy in flying[lane, p]:
-                    copy.wait_recv()
+            for copy in flying.get((lane, p), across[p] if lane == 1 else []):
+                copy.wait_recv()
             flying[lane, p] = step(lane, p, s) if s < 4 else []
-
-    advance(0, 0)
-    advance(0, 1)
-    advance(1, 0)
-    advance(0, 2)
-    advance(1, 1)
-    advance(0, 3)
-    advance(1, 2)
-    advance(1, 3)
-    advance(0, 4)
-    advance(1, 4)
-    for copy in started:
-        copy.wait_send()
+        yield True
+    copies.finish()
+
+
+def gather_kernel(parts, count, *refs):
+    ins, outs = refs[:count], refs[count : 2 * count]
+    send_sem, recv_sem, local_sem = refs[2 * count :]
+    greet(cube_places())
+    run(gather_steps(parts, ins, outs, Copies(send_sem, recv_sem), local_sem))
 
 
 def gather_cube(arrays, parts, collective_id, name):
@@ -170,27 +203,15 @@
     )(*arrays)
 
 
-def reduce_kernel(parts, count, *refs):
-    entries = [(p, *entry) for p in range(4) for entry in parts[p]]
-    size = 5 * len(entries)
-    ins, outs = refs[:count], refs[count : 2 * count]
-    bufs = refs[2 * count : 2 * count + size]
-    send_sem, recv_sem = refs[2 * count + size :]
+def entries_of(parts):
+    return [(p, *entry) for p in range(4) for entry in parts[p]]
+
+
+def reduce_steps(parts, ins, outs, bufs, copies):
+    entries = entries_of(parts)
     z, xh, y = own_place()
-    used = [0]
-    started = []
+    start = copies.start
     flying = {}
-
-    def start(src, dst, where):
-        k = used[0]
-        used[0] += 1
-        copy = pltpu.make_async_remote_copy(
-            src_ref=src, dst_ref=dst, send_sem=send_sem.at[k], recv_sem=recv_sem.at[k],
-            device_id=where, device_id_type=MESH,
-        )
-        copy.start()
-        started.append(copy)
-        return copy
 
     def first(lane, e):
         p, a, rows, cols = entries[e]
@@ -288,17 +309,23 @@
             )
             outs[a][rows, cols] = total.astype(outs[a].dtype)
 
-    greet_cube()
     for stage in (first, second, third, fourth, last):
         for lane in (1, 0):
             for e in range(len(entries)):
                 stage(lane, e)
-    for copy in started:
-        copy.wait_send()
-
-
-def reduce_cube(arrays, parts, collective_id, name, dtype=jnp.float32):
-    count = len(arrays)
+            yield True
+    copies.finish()
+
+
+def reduce_kernel(parts, count, *refs):
+    size = 5 * len(entries_of(parts))
+    ins, outs = refs[:count], refs[count : 2 * count]
+    bufs = refs[2 * count : 2 * count + size]
+    greet(cube_places())
+    run(reduce_steps(parts, ins, outs, bufs, Copies(*refs[2 * count + size :])))
+
+
+def reduce_scratch(arrays, parts):
     scratch = []
     for p in range(4):
         pair = (2, 4) if ORDERS[p][2][0] == "z" else (4, 2)
@@ -306,13 +333,18 @@
             for lead in ((2, *pair), (2, 4), (2, 2), (2,), ()):
                 scratch.append(pltpu.VMEM((*lead, rows.size, cols.size), arrays[a].dtype))
     copies = 13 * sum(len(part) for part in parts)
+    return scratch + [pltpu.SemaphoreType.DMA((copies,))] * 2
+
+
+def reduce_cube(arrays, parts, collective_id, name, dtype=jnp.float32):
+    count = len(arrays)
+    scratch = reduce_scratch(arrays, parts)
     return pl.pallas_call(
         functools.partial(reduce_kernel, parts, count),
         out_shape=[jax.ShapeDtypeStruct(a.shape[3:], dtype) for a in arrays],
         in_specs=[pl.BlockSpec(memory_space=pltpu.VMEM)] * count,
         out_specs=[pl.BlockSpec(memory_space=pltpu.VMEM)] * count,
-        scratch_shapes=scratch
-        + [pltpu.SemaphoreType.DMA((copies,)), pltpu.SemaphoreType.DMA((copies,))],
+        scratch_shapes=scratch,
         compiler_params=pltpu.CompilerParams(
             collective_id=collective_id, has_side_effects=True, vmem_limit_bytes=VMEM_LIMIT
         ),
@@ -343,37 +375,34 @@
     ]
 
 
-def sum_wa_kernel(x, out, half, got, far, send_sem, recv_sem):
+def wa_places():
     w = lax.axis_index("wa")
-    core = w % 2
-    beside = {"wa": w + 1 - 2 * core}
-    across = {"wa": (w + 2) % 4}
+    return [{"wa": w + 1 - 2 * (w % 2)}, {"wa": (w + 2) % 4}]
+
+
+def sum_wa_steps(x, out, half, got, far, copies):
+    core = lax.axis_index("wa") % 2
+    beside, across = wa_places()
     width = x.shape[1] // 2
-    barrier = pltpu.get_barrier_semaphore()
-    for place in (beside, across):
-        pl.semaphore_signal(barrier, inc=1, device_id=place, device_id_type=MESH)
-    pl.semaphore_wait(barrier, 2)
-
-    def send(src, dst, where, k):
-        copy = pltpu.make_async_remote_copy(
-            src_ref=src, dst_ref=dst, send_sem=send_sem.at[k], recv_sem=recv_sem.at[k],
-            device_id=where, device_id_type=MESH,
-        )
-        copy.start()
-        return copy
-
     mine = pl.ds(pl.multiple_of(core * width, width), width)
     theirs = pl.ds(pl.multiple_of((1 - core) * width, width), width)
-    one = send(x.at[:, theirs], got, beside, 0)
+    one = copies.start(x.at[:, theirs], got, beside)
+    yield True
     one.wait_recv()
     half[...] = x[:, mine] + got[...]
-    two = send(half, far, across, 1)
+    two = copies.start(half, far, across)
+    yield True
     two.wait_recv()
     out[:, mine] = half[...] + far[...]
-    three = send(out.at[:, mine], out.at[:, mine], beside, 2)
+    three = copies.start(out.at[:, mine], out.at[:, mine], beside)
+    yield True
     three.wait_recv()
-    for copy in (one, two, three):
-        copy.wait_send()
+    copies.finish()
+
+
+def sum_wa_kernel(x, out, half, got, far, send_sem, recv_sem):
+    greet(wa_places())
+    run(sum_wa_steps(x, out, half, got, far, Copies(send_sem, recv_sem)))
 
 
 def sum_wa(x, collective_id, name):
@@ -390,59 +419,6 @@
         ),
         name=name,
     )(x)
-
-
-def head_columns(h):
-    return pl.ds(pl.multiple_of(h * HD, HD), HD)
-
-
-class Copies:
-    def __init__(self, send_sem, recv_sem):
-        self.send_sem, self.recv_sem, self.started = send_sem, recv_sem, []
-
-    def start(self, src, dst, where):
-        k = len(self.started)
-        copy = pltpu.make_async_remote_copy(
-            src_ref=src, dst_ref=dst, send_sem=self.send_sem.at[k],
-            recv_sem=self.recv_sem.at[k], device_id=where, device_id_type=MESH,
-        )
-        copy.start()
-        self.started.append(copy)
-        return copy
-
-    def finish(self):
-        for copy in self.started:
-            copy.wait_send()
-
-
-def greet(places):
-    barrier = pltpu.get_barrier_semaphore()
-    for place in places:
-        pl.semaphore_signal(barrier, inc=1, device_id=place, device_id_type=MESH)
-    pl.semaphore_wait(barrier, len(places))
-
-
-def along_z():
-    z = lax.axis_index("sp")
-    return [{"sp": (z + d) % 4} for d in (1, 2, 3)]
-
-
-def vmem_call(kernel, out_shape, operands, scratch, collective_id, name, **params):
-    return pl.pallas_call(
-        kernel,
-        out_shape=out_shape,
-        in_specs=[pl.BlockSpec(memory_space=pltpu.VMEM)] * len(operands),
-        out_specs=jax.tree.map(lambda _: pl.BlockSpec(memory_space=pltpu.VMEM), out_shape),
-        scratch_shapes=scratch,
-        compiler_params=pltpu.CompilerParams(
-            collective_id=collective_id,
-            has_side_effects=collective_id is not None,
-            vmem_limit_bytes=VMEM_LIMIT,
-        ),
-        name=name,
-        **params,
-    )(*operands)
-
 
 def project_kernel(normed, wq, wk, wv, cosine, sine, q, k, v):
     for weight, out in ((wq, q), (wk, k)):
@@ -752,8 +728,9 @@
         attend_back_kernel, out_shape, (q, k, v, probs, grad, exact), scratch, None, "attend_back"
     )
 
-
 SLOTS = 16
+GROUP_ORDER = ((0, 1), (1, 0), (3, 0), (1, 1), (3, 1), (2, 0), (2, 1), (0, 0))
+SENT_AHEAD = 4
 
 
 def token_places():
@@ -770,7 +747,7 @@
     return where, there_z * 8 + there_x * 4 + there_y
 
 
-def greet_blocks():
+def greet_blocks(others):
     barrier = pltpu.get_barrier_semaphore()
 
     def one(i, carry):
@@ -779,11 +756,10 @@
         return carry
 
     lax.fori_loop(1, 32, one, 0)
-    w = lax.axis_index("wa")
-    core = w % 2
-    for place in (w + 1 - 2 * core, (w + 2) % 4):
-        pl.semaphore_signal(barrier, inc=1, device_id={"wa": place}, device_id_type=MESH)
-    pl.semaphore_wait(barrier, 33)
+    others = wa_places() + others
+    for place in others:
+        pl.semaphore_signal(barrier, inc=1, device_id=place, device_id_type=MESH)
+    pl.semaphore_wait(barrier, 31 + len(others))
 
 
 def quarter_columns(place, core):
@@ -791,62 +767,68 @@
     return pl.ds(pl.multiple_of(core * 2 * quarter + place * quarter, quarter), quarter)
 
 
-def dispatch_kernel(count, *refs):
-    ins, outs = refs[:count], refs[count : 2 * count]
-    out_sem, in_sem, own_sem, send_sem, recv_sem = refs[2 * count :]
+def dispatch_steps(ins, outs, out_sem, in_sem, own_sem, copies):
+    count = len(ins)
     z, xh, y, place, core = token_places()
-    w = lax.axis_index("wa")
-    beside, across = {"wa": w + 1 - 2 * core}, {"wa": (w + 2) % 4}
-    greet_blocks()
+    beside, across = wa_places()
     me = z * 8 + xh * 4 + y
     columns = quarter_columns(place, core)
     here = pl.ds(pl.multiple_of(me * SLOTS, SLOTS), SLOTS)
-    own = []
-    for a in range(count):
-        copy = pltpu.make_async_copy(ins[a].at[me], outs[a].at[:, here, columns], own_sem.at[a])
+    own = [
+        pltpu.make_async_copy(ins[a].at[me], outs[a].at[:, here, columns], own_sem.at[a])
+        for a in range(count)
+    ]
+    for copy in own:
         copy.start()
-        own.append(copy)
-
-        def one(i, carry):
-            where, block = block_device(i // 8, (i // 4) % 2, i % 4)
+    items = [(a, dz, dx) for a in range(count) for dz, dx in GROUP_ORDER]
+    passed, last = {}, []
+
+    def send(i):
+        a, dz, dx = items[i]
+
+        def one(dy, carry):
+            where, block = block_device(dz, dx, dy)
             pltpu.make_async_remote_copy(
                 src_ref=ins[a].at[block], dst_ref=outs[a].at[:, here, columns],
-                send_sem=out_sem.at[a], recv_sem=in_sem.at[a, i // 4],
+                send_sem=out_sem.at[a], recv_sem=in_sem.at[a, dz * 2 + dx],
                 device_id=where, device_id_type=MESH,
             ).start()
             return carry
 
-        lax.fori_loop(1, 32, one, 0)
-
-    copies = Copies(send_sem, recv_sem)
-    items = [(a, dz, dx) for a in range(count) for dz in range(4) for dx in range(2)]
-    items.sort(key=lambda item: (item[0], item[1] + item[2] == 0))
-    passed, last = {}, []
+        lax.fori_loop(1 if dz + dx == 0 else 0, 4, one, 0)
+
+    def rows_of(dz, dx):
+        first = ((z - dz + 4) % 4 * 8 + (xh + dx) % 2 * 4) * SLOTS
+        return pl.ds(pl.multiple_of(first, 4 * SLOTS), 4 * SLOTS)
 
     def arrived(i):
         a, dz, dx = items[i]
-        rows = pl.ds(pl.multiple_of(((z - dz + 4) % 4 * 8 + (xh + dx) % 2 * 4) * SLOTS, 4 * SLOTS), 4 * SLOTS)
         few = 3 if dz + dx == 0 else 4
         sample = outs[a].at[:, pl.ds(0, few * SLOTS), columns]
         pltpu.make_async_copy(sample, sample, in_sem.at[a, dz * 2 + dx]).wait()
         if dz + dx == 0:
             own[a].wait()
-        part = outs[a].at[:, rows, quarter_columns((place + dx) % 2, core)]
+        part = outs[a].at[:, rows_of(dz, dx), quarter_columns((place + dx) % 2, core)]
         passed[i] = copies.start(part, part, across)
         last.append(copies.start(part, part, beside))
 
     def from_across(i):
         a, dz, dx = items[i]
-        rows = pl.ds(pl.multiple_of(((z - dz + 4) % 4 * 8 + (xh + dx) % 2 * 4) * SLOTS, 4 * SLOTS), 4 * SLOTS)
         passed[i].wait_recv()
-        part = outs[a].at[:, rows, quarter_columns((place + dx + 1) % 2, core)]
+        part = outs[a].at[:, rows_of(dz, dx), quarter_columns((place + dx + 1) % 2, core)]
         last.append(copies.start(part, part, beside))
 
+    for i in range(SENT_AHEAD):
+        send(i)
+    yield True
     for i in range(len(items) + 2):
         if i < len(items):
             arrived(i)
+            if i + SENT_AHEAD < len(items):
+                send(i + SENT_AHEAD)
         if i >= 2:
             from_across(i - 2)
+        yield True
     for copy in last:
         copy.wait_recv()
     copies.finish()
@@ -855,42 +837,121 @@
         pltpu.make_async_copy(sample, sample, out_sem.at[a]).wait()
 
 
-def dispatch(arrays, collective_id):
-    count = len(arrays)
-    shape = jax.ShapeDtypeStruct((2, 32 * SLOTS, D), arrays[0].dtype)
+def shared_step(width):
+    return -(-width // HD) * HD
+
+
+def shared_steps(x, g, weights, whole, first, part, back, gate_grad, up_grad, down_grad, sem):
+    low = part.dtype
+    width = gate_grad.shape[1]
+    step = shared_step(width)
+    gate, up, down = (slice(k * step, k * step + width) for k in range(3))
+    load = pltpu.make_async_copy(whole.at[:, pl.ds(first, weights.shape[1])], weights, sem)
+    load.start()
+    yield True
+    load.wait()
+    pre = over(x[...], weights[:, gate], (1, 0))
+    yield True
+    lin = over(x[...], weights[:, up], (1, 0))
+    yield True
+    act, pre_grad, lin_grad = swish_parts(pre, lin, over(g[...], weights[:, down], (1, 0)))
+    act, pre_grad, lin_grad = act.astype(low), pre_grad.astype(low), lin_grad.astype(low)
+    yield True
+    for at in range(0, D, 512):
+        here = slice(at, at + 512)
+        part[:, here] = over(act, weights[here, down], (1, 1)).astype(low)
+        back[:, here] = (
+            over(pre_grad, weights[here, gate], (1, 1)) + over(lin_grad, weights[here, up], (1, 1))
+        ).astype(low)
+        yield True
+        down_grad[here] = over(g[:, here], act, (0, 0)).astype(low)
+        gate_grad[here] = over(x[:, here], pre_grad, (0, 0)).astype(low)
+        up_grad[here] = over(x[:, here], lin_grad, (0, 0)).astype(low)
+        yield True
+
+
+def dispatch_kernel(first, *refs):
+    ins, (x, g, whole), outs = refs[:2], refs[2:5], refs[5:7]
+    results, weights, load_sem = refs[7:12], refs[12], refs[13]
+    out_sem, in_sem, own_sem, *sems = refs[14:]
+    greet_blocks([])
+    moving = dispatch_steps(ins, outs, out_sem, in_sem, own_sem, Copies(*sems))
+    computing = shared_steps(x, g, weights, whole, first, *results, load_sem)
+    run(moving, computing)
+
+
+def dispatch(arrays, x, g, whole, first, width, collective_id):
+    low = x.dtype
+    rows = jax.ShapeDtypeStruct((2, 32 * SLOTS, D), low)
+    grad = jax.ShapeDtypeStruct((D, width), low)
+    anywhere, vmem = pl.BlockSpec(memory_space=pl.ANY), pl.BlockSpec(memory_space=pltpu.VMEM)
     return pl.pallas_call(
-        functools.partial(dispatch_kernel, count),
-        out_shape=[shape] * count,
-        in_specs=[pl.BlockSpec(memory_space=pl.ANY)] * count,
-        out_specs=[pl.BlockSpec(memory_space=pl.ANY)] * count,
+        functools.partial(dispatch_kernel, first),
+        out_shape=[rows] * 2 + [jax.ShapeDtypeStruct(x.shape, low)] * 2 + [grad] * 3,
+        in_specs=[anywhere] * 2 + [vmem] * 2 + [anywhere],
+        out_specs=[anywhere] * 2 + [vmem] * 5,
         scratch_shapes=[
-            pltpu.SemaphoreType.DMA((count,)),
-            pltpu.SemaphoreType.DMA((count, 8)),
-            pltpu.SemaphoreType.DMA((count,)),
-            pltpu.SemaphoreType.DMA((24 * count,)),
-            pltpu.SemaphoreType.DMA((24 * count,)),
+            pltpu.VMEM((D, 3 * shared_step(width)), low),
+            pltpu.SemaphoreType.DMA,
+            pltpu.SemaphoreType.DMA((2,)),
+            pltpu.SemaphoreType.DMA((2, 8)),
+            pltpu.SemaphoreType.DMA((2,)),
+            pltpu.SemaphoreType.DMA((48,)),
+            pltpu.SemaphoreType.DMA((48,)),
         ],
-        compiler_params=pltpu.CompilerParams(collective_id=collective_id, has_side_effects=True),
+        compiler_params=pltpu.CompilerParams(
+            collective_id=collective_id, has_side_effects=True, vmem_limit_bytes=VMEM_LIMIT
+        ),
         name="dispatch_rows",
-    )(*arrays)
-
-
-def return_kernel(count, *refs):
-    ins, outs = refs[:count], refs[count : 2 * count]
-    halves, quarters = refs[2 * count : 3 * count], refs[3 * count : 4 * count]
-    out_sem, in_sem, send_sem, recv_sem = refs[4 * count :]
+    )(*arrays, x, g, whole)
+
+
+def expert_steps(hbm, held, part, back, kept, load_sem, finished):
+    low = part.dtype
+    loads = [
+        [pltpu.make_async_copy(src.at[e], dst.at[e], load_sem.at[e, k]) for k, (src, dst) in enumerate(zip(hbm, held))]
+        for e in range(2)
+    ]
+    for load in loads[0] + loads[1]:
+        load.start()
+    yield True
+    rows, grads, gate, up, down = held
+    for e in range(2):
+        for load in loads[e]:
+            load.wait()
+        x, g = rows[e], grads[e]
+        pre = over(x, gate[e], (1, 1))
+        lin = over(x, up[e], (1, 1))
+        yield True
+        act, pre_grad, lin_grad = swish_parts(pre, lin, over(g, down[e], (1, 1)))
+        act, pre_grad, lin_grad = act.astype(low), pre_grad.astype(low), lin_grad.astype(low)
+        kept[0][e], kept[1][e], kept[2][e] = act, pre_grad, lin_grad
+        yield True
+        for at in range(0, D, 512):
+            here = slice(at, at + 512)
+            part[e, :, here] = over(act, down[e, :, here], (1, 0)).astype(low)
+            back[e, :, here] = (
+                over(pre_grad, gate[e, :, here], (1, 0)) + over(lin_grad, up[e, :, here], (1, 0))
+            ).astype(low)
+            if at + 512 == D:
+                finished(e)
+            yield True
+
+
+def return_steps(ins, outs, halves, quarters, out_sem, in_sem, copies):
     z, xh, y, place, core = token_places()
-    w = lax.axis_index("wa")
-    beside, across = {"wa": w + 1 - 2 * core}, {"wa": (w + 2) % 4}
-    greet_blocks()
+    beside, across = wa_places()
     me = z * 8 + xh * 4 + y
     quarter = D // 4
     group = 4 * SLOTS
     mine = pl.ds(pl.multiple_of(core * 2 * quarter, 2 * quarter), 2 * quarter)
     theirs = pl.ds(pl.multiple_of((1 - core) * 2 * quarter, 2 * quarter), 2 * quarter)
-    copies = Copies(send_sem, recv_sem)
-    items = [(a, dz, dx) for a in range(count) for dz in range(4) for dx in range(2)]
-    items.sort(key=lambda item: (item[0], item[1] + item[2] == 0))
+    items = [(e, a, dz, dx) for e in range(2) for a in range(2) for dz, dx in GROUP_ORDER]
+    paired_up, passed = {}, {}
+
+    def finished(e):
+        for a in range(2):
+            paired_up[e, a] = copies.start(ins[a].at[e, :, theirs], halves[a].at[e], beside)
 
     def rows_of(dz, dx):
         return pl.ds(pl.multiple_of(((z + dz) % 4 * 8 + (xh + dx) % 2 * 4) * SLOTS, group), group)
@@ -901,63 +962,98 @@
     def given(dx):
         return pl.ds(pl.multiple_of((place + dx + 1) % 2 * quarter, quarter), quarter)
 
-    paired_up = [
-        copies.start(ins[a].at[:, rows_of(dz, dx), theirs], halves[a].at[:, rows_of(dz, dx)], beside)
-        for a, dz, dx in items
-    ]
-    passed = {}
-
     def add_core(i):
-        a, dz, dx = items[i]
+        e, a, dz, dx = items[i]
         rows = rows_of(dz, dx)
-        paired_up[i].wait_recv()
-        for e in range(2):
-            halves[a][e, rows] = halves[a][e, rows] + ins[a][e, rows, mine]
+        if i % 8 == 0:
+            paired_up[e, a].wait_recv()
+        halves[a][e, rows] = halves[a][e, rows] + ins[a][e, rows, mine]
         passed[i] = copies.start(
-            halves[a].at[:, rows, given(dx)], quarters[a].at[:, rows], across
+            halves[a].at[e, rows, given(dx)], quarters[a].at[e, rows], across
         )
 
     def add_across(i):
-        a, dz, dx = items[i]
+        e, a, dz, dx = items[i]
         rows = rows_of(dz, dx)
         passed[i].wait_recv()
-        for e in range(2):
-            quarters[a][e, rows] = quarters[a][e, rows] + halves[a][e, rows, kept(dx)]
-        for dy in range(4):
+        quarters[a][e, rows] = quarters[a][e, rows] + halves[a][e, rows, kept(dx)]
+        if dz + dx == 0:
+            outs[a][me, e] = quarters[a][e, pl.ds(pl.multiple_of(me * SLOTS, SLOTS), SLOTS)]
+
+        def one(dy, carry):
             where, block = block_device(dz, dx, dy)
             part = pl.ds(pl.multiple_of(block * SLOTS, SLOTS), SLOTS)
-            if dz + dx + dy == 0:
-                outs[a][me] = quarters[a][:, part]
-            else:
-                pltpu.make_async_remote_copy(
-                    src_ref=quarters[a].at[:, part], dst_ref=outs[a].at[me],
-                    send_sem=out_sem.at[a], recv_sem=in_sem.at[a],
-                    device_id=where, device_id_type=MESH,
-                ).start()
-
-    for i in range(len(items) + 1):
-        if i < len(items):
-            add_core(i)
-        if i >= 1:
-            add_across(i - 1)
-    copies.finish()
-    for a in range(count):
-        sample = outs[a].at[pl.ds(0, 31)]
-        pltpu.make_async_copy(sample, sample, in_sem.at[a]).wait()
-        pltpu.make_async_copy(sample, sample, out_sem.at[a]).wait()
-
-
-def give_back(arrays, collective_id):
-    count = len(arrays)
-    shape = jax.ShapeDtypeStruct((32, 2, SLOTS, D // 4), arrays[0].dtype)
+            pltpu.make_async_remote_copy(
+                src_ref=quarters[a].at[e, part], dst_ref=outs[a].at[me, e],
+                send_sem=out_sem.at[a], recv_sem=in_sem.at[a],
+                device_id=where, device_id_type=MESH,
+            ).start()
+            return carry
+
+        lax.fori_loop(1 if dz + dx == 0 else 0, 4, one, 0)
+
+    def steps():
+        for i in range(len(items) + 1):
+            if i < len(items):
+                add_core(i)
+            if i >= 1:
+                add_across(i - 1)
+            yield True
+        copies.finish()
+        for a in range(2):
+            sample = outs[a].at[pl.ds(0, 31)]
+            pltpu.make_async_copy(sample, sample, in_sem.at[a]).wait()
+            pltpu.make_async_copy(sample, sample, out_sem.at[a]).wait()
+
+    return finished, steps()
+
+
+EXPERT_ORDER = "RRXXXXXXX" + "TXTTXTTXTTXTTXTTXTTXT" + "TTTRTTTRTTRTTRTTRTTRTTRT"
+
+
+def expert_kernel(parts, count, *refs):
+    hbm, summed, refs = refs[:5], refs[5 : 5 + count], refs[5 + count :]
+    outs, shares, kept, refs = refs[:2], refs[2 : 2 + count], refs[2 + count : 5 + count], refs[5 + count :]
+    held, (part, back), halves, quarters = refs[:5], refs[5:7], refs[7:9], refs[9:11]
+    load_sem, out_sem, in_sem, send_sem, recv_sem = refs[11:16]
+    bufs, more = refs[16:-2], refs[-2:]
+    greet_blocks([neighbour("x", "A")])
+    finished, returning = return_steps(
+        (part, back), outs, halves, quarters, out_sem, in_sem, Copies(send_sem, recv_sem)
+    )
+    computing = expert_steps(hbm, held, part, back, kept, load_sem, finished)
+    reducing = reduce_steps(parts, summed, shares, bufs, Copies(*more))
+    for turn in EXPERT_ORDER:
+        next({"R": reducing, "X": computing, "T": returning}[turn], None)
+    run(returning, reducing)
+
+
+def run_experts(operands, summed, collective_id):
     rows = 32 * SLOTS
-    scratch = [pltpu.VMEM((2, rows, D // 2), arrays[0].dtype)] * count
-    scratch += [pltpu.VMEM((2, rows, D // 4), arrays[0].dtype)] * count
-    scratch += [pltpu.SemaphoreType.DMA((count,))] * 2 + [pltpu.SemaphoreType.DMA((16 * count,))] * 2
-    return vmem_call(
-        functools.partial(return_kernel, count), [shape] * count, arrays, scratch, collective_id,
-        "return_rows",
-    )
+    low = operands[0].dtype
+    hidden = operands[2].shape[1]
+    parts = row_parts(summed)
+    out_shape = [jax.ShapeDtypeStruct((32, 2, SLOTS, D // 4), low)] * 2
+    out_shape += [jax.ShapeDtypeStruct(x.shape[3:], jnp.float32) for x in summed]
+    out_shape += [jax.ShapeDtypeStruct((2, rows, hidden), low)] * 3
+    scratch = [pltpu.VMEM(x.shape, low) for x in operands]
+    scratch += [pltpu.VMEM((2, rows, D), low)] * 2
+    scratch += [pltpu.VMEM((2, rows, D // 2), low)] * 2 + [pltpu.VMEM((2, rows, D // 4), low)] * 2
+    scratch += [pltpu.SemaphoreType.DMA((2, 5))] + [pltpu.SemaphoreType.DMA((2,))] * 2
+    scratch += [pltpu.SemaphoreType.DMA((36,))] * 2
+    scratch += reduce_scratch(summed, parts)
+    anywhere, vmem = pl.BlockSpec(memory_space=pl.ANY), pl.BlockSpec(memory_space=pltpu.VMEM)
+    return pl.pallas_call(
+        functools.partial(expert_kernel, parts, len(summed)),
+        out_shape=out_shape,
+        in_specs=[anywhere] * 5 + [vmem] * len(summed),
+        out_specs=[vmem] * len(out_shape),
+        scratch_shapes=scratch,
+        compiler_params=pltpu.CompilerParams(
+            collective_id=collective_id, has_side_effects=True, vmem_limit_bytes=VMEM_LIMIT
+        ),
+        name="run_experts",
+    )(*operands, *summed)
 
 
 def sum_more_kernel(parts, *refs):
@@ -1012,6 +1108,42 @@
     )
 
 
+def tail_kernel(parts, count, *refs):
+    ins, x = refs[:count], refs[count]
+    outs, total = refs[count + 1 : 2 * count + 1], refs[2 * count + 1]
+    half, got, far, small_got, small_far = refs[2 * count + 2 : 2 * count + 7]
+    bufs, more = refs[2 * count + 7 : -6], refs[-6:]
+    greet(cube_places() + wa_places())
+    run(
+        reduce_steps(parts, ins, outs, bufs, Copies(*more[:2])),
+        sum_wa_steps(x, total, half, got, far, Copies(*more[2:4])),
+    )
+    beside, across = wa_places()
+    copies = Copies(*more[4:])
+    small = outs[count - 1]
+    copies.start(small, small_got, beside).wait()
+    small[...] = small[...] + small_got[...]
+    copies.start(small, small_far, across).wait()
+    small[...] = small[...] + small_far[...]
+
+
+def reduce_and_sum(arrays, parts, x, collective_id):
+    count = len(arrays)
+    rows, columns = x.shape
+    out_shape = [jax.ShapeDtypeStruct(a.shape[3:], jnp.float32) for a in arrays]
+    scratch = [pltpu.VMEM((rows, columns // 2), x.dtype)] * 3
+    scratch += [pltpu.VMEM(arrays[-1].shape[3:], jnp.float32)] * 2
+    scratch += reduce_scratch(arrays, parts)
+    scratch += [pltpu.SemaphoreType.DMA((3,))] * 2 + [pltpu.SemaphoreType.DMA((2,))] * 2
+    return vmem_call(
+        functools.partial(tail_kernel, parts, count),
+        [*out_shape, jax.ShapeDtypeStruct(x.shape, x.dtype)],
+        (*arrays, x),
+        scratch,
+        collective_id,
+        "reduce_attention_grads",
+    )
+
 def over(left, right, dims):
     return lax.dot_general(
         left, right, ((dims[:1], dims[1:]), ((), ())), preferred_element_type=jnp.float32
@@ -1025,63 +1157,29 @@
     return swish * lin, act_grads * lin * slope, act_grads * swish
 
 
-def expert_kernel(rows, grads, gate, up, down, part, back, gate_grad, up_grad, down_grad):
-    low = part.dtype
-    x, g = rows[0], grads[0]
-    pre = over(x, gate[0], (1, 0))
-    lin = over(x, up[0], (1, 0))
-    act, pre_grad, lin_grad = swish_parts(pre, lin, over(g, down[0], (1, 1)))
-    act, pre_grad, lin_grad = act.astype(low), pre_grad.astype(low), lin_grad.astype(low)
+def expert_grads_kernel(rows, grads, act, pre_grad, lin_grad, gate_grad, up_grad, down_grad):
     for at in range(0, D, 512):
         here = slice(at, at + 512)
-        part[0, :, here] = over(act, down[0, :, here], (1, 0)).astype(low)
-        back[0, :, here] = (
-            over(pre_grad, gate[0, here], (1, 1)) + over(lin_grad, up[0, here], (1, 1))
-        ).astype(low)
-        down_grad[0, :, here] = over(act, g[:, here], (0, 0))
-        gate_grad[0, here] = over(x[:, here], pre_grad, (0, 0))
-        up_grad[0, here] = over(x[:, here], lin_grad, (0, 0))
-
-
-def run_experts(rows, grads, gate, up, down):
-    operands = (rows, grads, gate, up, down)
-    out_shape = [jax.ShapeDtypeStruct(rows.shape, rows.dtype)] * 2
-    out_shape += [jax.ShapeDtypeStruct(x.shape, jnp.float32) for x in (gate, up, down)]
+        down_grad[0, :, here] = over(act[0], grads[0, :, here], (0, 0))
+        gate_grad[0, :, here] = over(pre_grad[0], rows[0, :, here], (0, 0))
+        up_grad[0, :, here] = over(lin_grad[0], rows[0, :, here], (0, 0))
+
+
+def expert_grads(*operands):
+    shape = jax.ShapeDtypeStruct((2, operands[2].shape[2], D), jnp.float32)
 
     def spec(x):
         return pl.BlockSpec((1, *x.shape[1:]), lambda e: (e, 0, 0))
 
     return pl.pallas_call(
-        expert_kernel,
-        grid=(rows.shape[0],),
-        out_shape=out_shape,
+        expert_grads_kernel,
+        grid=(2,),
+        out_shape=[shape] * 3,
         in_specs=[spec(x) for x in operands],
-        out_specs=[spec(x) for x in out_shape],
+        out_specs=[spec(shape)] * 3,
         compiler_params=pltpu.CompilerParams(vmem_limit_bytes=VMEM_LIMIT),
-        name="run_experts",
+        name="expert_grads",
     )(*operands)
-
-
-def shared_kernel(x, g, gate, up, down, part, back, gate_grad, up_grad, down_grad):
-    low = part.dtype
-    pre = over(x[...], gate[...], (1, 0))
-    lin = over(x[...], up[...], (1, 0))
-    act, pre_grad, lin_grad = swish_parts(pre, lin, over(g[...], down[...], (1, 0)))
-    act, pre_grad, lin_grad = act.astype(low), pre_grad.astype(low), lin_grad.astype(low)
-    for at in range(0, D, 512):
-        here = slice(at, at + 512)
-        part[:, here] = over(act, down[here], (1, 1)).astype(low)
-        back[:, here] = (
-            over(pre_grad, gate[here], (1, 1)) + over(lin_grad, up[here], (1, 1))
-        ).astype(low)
-        down_grad[here] = over(g[:, here], act, (0, 0)).astype(low)
-        gate_grad[here] = over(x[:, here], pre_grad, (0, 0)).astype(low)
-        up_grad[here] = over(x[:, here], lin_grad, (0, 0)).astype(low)
-
-
-def run_shared(x, g, gate, up, down):
-    out_shape = [jax.ShapeDtypeStruct(a.shape, a.dtype) for a in (x, x, gate, up, down)]
-    return vmem_call(shared_kernel, out_shape, (x, g, gate, up, down), [], None, "run_shared")
 
 
 def turned_gather(arrays, axis):
@@ -1135,25 +1233,24 @@
         return lax.dynamic_slice_in_dim(x, quarter_at, D // 4, 1)
 
     heads = (query_weight, key_weight, value_weight)
-    gains = jnp.pad(jnp.stack([attn_gain, mlp_gain], axis=1), ((0, 0), (0, HD - 2)))
+    gain_rows = attn_gain.shape[0]
+    gains = jnp.pad(jnp.stack([attn_gain, mlp_gain]), ((0, 14), (0, HD - gain_rows)))
     parts = row_parts(heads)
-    parts[0].append((3, pl.ds(0, gains.shape[0]), pl.ds(0, HD)))
-    full_query, full_key, full_value, full_gains = (
-        whole.reshape(D, -1)
-        for whole in gather_cube((*heads, gains), parts, 1, "gather_head_weights")
-    )
-    turned, full_sgate, full_sup, turned_sdown, full_router = turned_gather(
-        (
-            output_weight.T,
-            shared_gate,
-            shared_up,
-            shared_down.T,
-            router_weight,
-        ),
-        groups,
-    )
-    gain_one = full_gains[:, 0].astype(jnp.float32)
-    gain_two = full_gains[:, 1].astype(jnp.float32)
+    parts[0].append((3, pl.ds(0, 16), pl.ds(0, HD)))
+    *wholes, full_gains = gather_cube((*heads, gains), parts, 1, "gather_head_weights")
+    full_query, full_key, full_value = (whole.reshape(D, head_cols) for whole in wholes)
+    hidden_cols = shared_gate.shape[1]
+    padded = [
+        jnp.pad(x, ((0, 0), (0, -x.shape[1] % HD)))
+        for x in (output_weight.T, router_weight, shared_gate, shared_up, shared_down.T)
+    ]
+    whole = lax.all_gather(jnp.concatenate(padded, axis=1), groups, axis=0, tiled=True)
+    turned = whole[:, :head_cols]
+    full_router = whole[:, head_cols : head_cols + experts_all]
+    shared_first = head_cols + HD
+    gain_one, gain_two = (
+        full_gains[..., k, :gain_rows].reshape(D).astype(jnp.float32) for k in range(2)
+    )
     tokens_f = tokens.astype(jnp.float32)
     inv_one = lax.rsqrt(jnp.mean(tokens_f * tokens_f, axis=-1, keepdims=True) + EPSILON)
     unit_one = tokens_f * inv_one
@@ -1197,22 +1294,32 @@
     send_grads = (
         dot(gate_high, grad_quarter, (0, 0)) + dot(gate_rest, grad_quarter, (0, 0))
     ).astype(low)
-    shared_part, shared_in_part, *mlp_grads = run_shared(
-        mlp_in, cotangent, full_sgate, full_sup, turned_sdown
+    by_owner = (32, 2, SLOTS, D // 4)
+    rows_in, grads_in, shared_part, shared_in_part, *mlp_grads = dispatch(
+        (send_rows.reshape(by_owner), send_grads.reshape(by_owner)),
+        mlp_in,
+        cotangent,
+        whole,
+        shared_first,
+        hidden_cols,
+        5,
     )
     mlp_grads = [x.reshape(4, 2, 4, x.shape[0] // 32, x.shape[1]) for x in mlp_grads]
-    gate_share, up_share, down_share = reduce_cube(
-        mlp_grads, row_parts(mlp_grads), 11, "reduce_mlp_grads"
-    )
-    by_owner = (32, 2, SLOTS, D // 4)
-    rows_in, grads_in = dispatch((send_rows.reshape(by_owner), send_grads.reshape(by_owner)), 5)
-
-    expert_part, rows_part, expert_gate_grad, expert_up_grad, expert_down_grad = run_experts(
-        rows_in, grads_in, expert_gate, expert_up, expert_down
-    )
-    returned, rows_back = (
-        x.reshape(-1, D // 4) for x in give_back((expert_part, rows_part), 6)
-    )
+
+    returned, rows_back, gate_share, up_share, down_share, *kept = run_experts(
+        (
+            rows_in,
+            grads_in,
+            expert_gate.transpose(0, 2, 1),
+            expert_up.transpose(0, 2, 1),
+            expert_down,
+        ),
+        mlp_grads,
+        6,
+    )
+    gate_grad_turned, up_grad_turned, expert_down_grad = expert_grads(rows_in, grads_in, *kept)
+    returned, rows_back = returned.reshape(-1, D // 4), rows_back.reshape(-1, D // 4)
+
     routed = (dot(gate_high, returned, (1, 0)) + dot(gate_rest, returned, (1, 0))).astype(low)
     routed_in = dot(pick, rows_back, (1, 0)).astype(low)
     slot_grads = jnp.where(taken, dot(grad_quarter, returned, (1, 1)), 0.0)
@@ -1251,19 +1358,11 @@
         + dot(key_in, full_key, (1, 1))
         + dot(value_in, full_value, (1, 1))
     ).astype(low)
-    normed_grad = sum_wa(normed_part, 10, "sum_normed_grad").astype(jnp.float32)
-    gain_one_grad = jnp.sum(normed_grad * unit_one, axis=0)
-    scaled_one = normed_grad * gain_one
-    tokens_grad = (
-        hidden_grad
-        + inv_one
-        * (scaled_one - unit_one * jnp.mean(scaled_one * unit_one, axis=-1, keepdims=True))
-    ).astype(low)
-
-    gain_grads = jnp.stack([gain_one_grad, gain_two_grad], axis=1)
-    small_grads = jnp.pad(
-        jnp.concatenate([router_grad, gain_grads], axis=1), ((0, 0), (0, HD - 2 - experts_all))
-    )
+    gain_one_part = jnp.sum(normed_part.astype(jnp.float32) * unit_one, axis=0)
+    small_grads = jnp.concatenate(
+        [0.25 * router_grad, gain_one_part[:, None], 0.25 * gain_two_grad[:, None]], axis=1
+    )
+    small_grads = jnp.pad(small_grads, ((0, 0), (0, HD - small_grads.shape[1])))
 
     def by_shard(x):
         return x.astype(low).reshape(4, 2, 4, x.shape[0] // 32, x.shape[1])
@@ -1279,10 +1378,18 @@
     ]
     parts = whole_parts(attention_grads)
     attention_grads.append(by_shard(small_grads))
-    parts[0].append((4, pl.ds(0, attention_grads[4].shape[3]), pl.ds(0, HD)))
-    query_share, key_share, value_share, output_share, small_share = reduce_cube(
-        attention_grads, parts, 12, "reduce_attention_grads"
-    )
+    for part, (_, rows, columns) in zip(parts, sum(row_parts(attention_grads[4:]), [])):
+        part.append((4, rows, columns))
+    query_share, key_share, value_share, output_share, small_share, normed_sum = reduce_and_sum(
+        attention_grads, parts, normed_part, 12
+    )
+    normed_grad = normed_sum.astype(jnp.float32)
+    scaled_one = normed_grad * gain_one
+    tokens_grad = (
+        hidden_grad
+        + inv_one
+        * (scaled_one - unit_one * jnp.mean(scaled_one * unit_one, axis=-1, keepdims=True))
+    ).astype(low)
     return (
         block_out,
         tokens_grad,
@@ -1296,8 +1403,8 @@
         gate_share,
         up_share,
         down_share.T,
-        expert_gate_grad,
-        expert_up_grad,
+        gate_grad_turned.transpose(0, 2, 1),
+        up_grad_turned.transpose(0, 2, 1),
         expert_down_grad,
     )
 

time: 627 us -> 554 us (0.88)
  Pallas kernels: 513 us -> 457 us
  local copies, waits for them, and re-layouts: 39.4 us -> 13.3 us
  waiting for transfers between devices: 0.5 us -> 13.3 us
    pallas_call x4 -> x3, Pallas kernels: 207 us -> 177 us  [the longest x1 99.1 us: run_experts(): pl.pallas_call(functools.partial(expert_kernel, parts, len(summed)), out_...]
    pallas_call x2 -> x1, Pallas kernels: 36.2 us -> 12.9 us  [sum_wa(): pl.pallas_call(sum_wa_kernel, out_shape=jax.ShapeDtypeStruct(x.shape, x.d...]
    unnamed x67 -> x65, local copies, waits for them, and re-layouts: 26.6 us -> 9.92 us
    all_gather x1, waiting for transfers between devices: 0.48 us -> 13.2 us  [shards(): lax.all_gather(jnp.concatenate(padded, axis=1), groups, axis=0, tiled=True)]
    split x1 -> x0, local copies, waits for them, and re-layouts: 6.99 us -> none  [turned_gather(): jnp.split(whole, [sum(widths[:k]) for k in range(1, len(widths))], axis=1)]
    pallas_call x11 -> x10, Pallas kernels: 202 us -> 198 us  [vmem_call(): pl.pallas_call(kernel, out_shape=out_shape, in_specs=[pl.BlockSpec(memory...]
  transfers between devices with their start and end apart: 1 -> 1, of which waited for: 1 -> 1; matrix products, arithmetic and copies ran while one was open for 2% -> 1% of each run, Pallas kernels for 21% -> 24%
where the time goes in v3:
time: 554 us; the launch traced here: 545 us
  Pallas kernels  457 us (82%)
  matrix products  33.1 us (6%)
  between operations  15 us (3%)
  local copies, waits for them, and re-layouts  13.3 us (2%)
  waiting for transfers between devices  13.3 us (2%)
  other arithmetic  13.3 us (2%)
    pallas_call x10, Pallas kernels, vmem_call(): pl.pallas_call(kernel, out_shape=out_shape, in_specs=[pl.BlockSpec(memory...  198 us
    pallas_call x1, Pallas kernels, run_experts(): pl.pallas_call(functools.partial(expert_kernel, parts, len(summed)), out_...  99.1 us
    pallas_call x1, Pallas kernels, gather_cube(): pl.pallas_call(functools.partial(gather_kernel, parts, count), out_shape=...  69.3 us
    pallas_call x1, Pallas kernels, dispatch(): pl.pallas_call(functools.partial(dispatch_kernel, first), out_shape=[rows...  67 us
    dot_general x23, matrix products, dot(): lax.dot_general(left, right, ((over[:1], over[1:]), ((), ())), preferred_...  33.1 us
    all_gather x1, waiting for transfers between devices, shards(): lax.all_gather(jnp.concatenate(padded, axis=1), groups, axis=0, tiled=True)  13.2 us
    pallas_call x1, Pallas kernels, sum_wa(): pl.pallas_call(sum_wa_kernel, out_shape=jax.ShapeDtypeStruct(x.shape, x.d...  12.9 us
  transfers between devices with their start and end apart: 1, of which 1 were waited for; matrix products, arithmetic and copies ran while one was open for 1% of the time, Pallas kernels for 24%

profile of v3, /device:TPU:1, one launch (start us, length us, event | category | flops | bytes accessed | tf_op | source)
XLA Modules:
  0.0 545.1 jit_solution(4876107347278677536)
XLA Ops:
  7.2 0.9 bitcast_dynamic-update-slice_fusion
  8.1 0.7 pad_dynamic-update-slice_fusion.3
  8.9 0.9 pad_dynamic-update-slice_fusion.2
  9.8 0.9 pad_dynamic-update-slice_fusion.1
  10.7 0.9 pad_dynamic-update-slice_fusion
  11.6 0.7 copy-done.16
  12.4 1.3 fusion.77.refs_3_
  13.7 69.3 %gather_head_weights.1 = (bf16[4,2,4,64,512]{4,3,2,1,0:T(8,128)(2,1)}, bf16[4,2,4,64,512]{4,3,2,1,0:T(8,128)(2,1)}, bf16[4,2,4,64,512]{4,3,2,1,0:T(8,128)(2,1)}, bf16[4,2,4,16,128]{4,3,2,1,0:T(8,128)(2,1)}) custom-call(bf16[64,512]{1,0:T(8,128)(2,1)} %refs_0_.1, bf16[64,512]{1,0:T(8,128)(2,1)} %refs_1_.1, bf16[64,512]{1,0:T(8,128)(2,1)} %refs_2_.1, ...), custom_call_target="tpu_custom_call" | custom-call | tf_op jit(solution)/shard_map/gather_head_weights/pallas_call | solution.py:191
  82.9 1.0 convert_reduce_fusion
  84.4 0.8 pad_maximum_fusion.1
  85.4 1.0 fusion.16.normed
  86.4 4.7 project_heads.1
  91.1 41.1 %spread_heads.1 = (bf16[4,128,128]{2,1,0:T(8,128)(2,1)}, bf16[4,2,4,128,128]{4,3,2,1,0:T(8,128)(2,1)}, bf16[4,2,4,128,128]{4,3,2,1,0:T(8,128)(2,1)}) custom-call(bf16[128,512]{1,0:T(8,128)(2,1)} %get-tuple-element.67.q, bf16[128,512]{1,0:T(8,128)(2,1)} %get-tuple-element.68.k, bf16[128,512]{1,0:T(8,128)(2,1)} %get-tuple-element.69.v), custom_call_target="tpu_custom_call" | custom-call | tf_op jit(solution)/shard_map/spread_heads/pallas_call | solution.py:112
  132.1 6.8 %attend.1 = (bf16[4,128,128]{2,1,0:T(8,128)(2,1)}, f32[4,128,128]{2,1,0:T(8,128)}, bf16[10,128,1024]{2,1,0:T(8,128)(2,1)}) custom-call(bf16[4,128,128]{2,1,0:T(8,128)(2,1)} %get-tuple-element.70.q, bf16[4096,128]{1,0:T(8,128)(2,1)} %bitcast.83, bf16[4096,128]{1,0:T(8,128)(2,1)} %bitcast.85), custom_call_target="tpu_custom_call" | custom-call | tf_op jit(solution)/shard_map/attend/pallas_call | solution.py:112
  138.9 6.3 %heads_to_tokens.1 = bf16[128,512]{1,0:T(8,128)(2,1)} custom-call(bf16[4,128,128]{2,1,0:T(8,128)(2,1)} %get-tuple-element.73.x), custom_call_target="tpu_custom_call" | custom-call | tf_op jit(solution)/shard_map/heads_to_tokens/pallas_call | solution.py:112
  145.3 0.5 convolution_compare_fusion
  145.8 13.2 %all-gather.2.cloned.1.call-done.refs_4_ = bf16[2048,2944]{1,0:T(8,128)(2,1)} async-done(((bf16[64,2944]{1,0:T(8,128)(2,1)}), bf16[2048,2944]{1,0:T(8,128)(2,1)}) %all-gather.2.cloned.1.call-update) | async-done | bytes 12058640 | tf_op jit(solution)/shard_map/all_gather | solution.py:1247
  159.1 3.3 convolution_convert_fusion.4.x
  162.3 12.9 %sum_attention.1 = bf16[128,2048]{1,0:T(8,128)(2,1)} custom-call(bf16[128,2048]{1,0:T(8,128)(2,1)} %convolution_convert_fusion.4.x), custom_call_target="tpu_custom_call" | custom-call | tf_op jit(solution)/shard_map/sum_attention/pallas_call | solution.py:410
  175.2 1.3 multiply_reduce_fusion.2
  176.5 1.3 multiply_convert_fusion.refs_2_
  177.8 1.6 fusion.89
  180.3 1.5 convolution_convert_fusion.5
  181.8 0.4 fusion.38
  182.2 1.4 add_convert_fusion
  183.7 67.0 %dispatch_rows.1 = (bf16[2,512,2048]{2,1,0:T(8,128)(2,1)}, bf16[2,512,2048]{2,1,0:T(8,128)(2,1)}, bf16[128,2048]{1,0:T(8,128)(2,1)}, bf16[128,2048]{1,0:T(8,128)...) custom-call(bf16[32,2,16,512]{3,2,1,0:T(8,128)(2,1)} %bitcast.87, ...), custom_call_target="tpu_custom_call" | custom-call | tf_op jit(solution)/shard_map/dispatch_rows/pallas_call | solution.py:888
  250.7 99.1 %run_experts.1 = (bf16[32,2,16,512]{3,2,1,0:T(8,128)(2,1)}, bf16[32,2,16,512]{3,2,1,0:T(8,128)(2,1)}, f32[64,704]{1,0:T(8,128)}, f32[64,704]{1,0:T(8,128)}, f32[...) custom-call(bf16[2,512,2048]{2,1,0:T(8,128)(2,1)} %get-tuple-element., ...), custom_call_target="tpu_custom_call" | custom-call | tf_op jit(solution)/shard_map/run_experts/pallas_call | solution.py:1046
  349.8 1.6 fusion.90
  351.4 0.5 convolution_select_fusion
  351.9 1.0 fusion.14.refs_2_
  352.9 0.4 fusion.30
  353.3 1.0 convolution_convert_fusion.6.refs_3_
  354.3 0.6 pad.32.refs_4_
  354.9 28.1 %sum_mlp.1 = (bf16[128,2048]{1,0:T(8,128)(2,1)}, bf16[128,2048]{1,0:T(8,128)(2,1)}, f32[128,128]{1,0:T(8,128)}) custom-call(bf16[128,2048]{1,0:T(8,128)(2,1)} %get-tuple-element.74.refs_0_, bf16[128,2048]{1,0:T(8,128)(2,1)} %get-tuple-element.75.refs_1_, bf16[128,512]{1,0:T(8,128)(2,1)} %fusion.14.refs_2_, ...), custom_call_target="tpu_custom_call" | custom-call | tf_op jit(solution)/shard_map/sum_mlp/pallas_call | solution.py:112
  383.0 1.0 multiply_reduce_fusion.3
  384.1 1.3 fusion.1
  385.3 2.3 multiply_reduce_fusion
  387.7 1.3 multiply_add_fusion
  389.0 2.7 fusion.11.x
  391.7 6.2 %tokens_to_heads.1.grad = bf16[4,128,128]{2,1,0:T(8,128)(2,1)} custom-call(bf16[128,512]{1,0:T(8,128)(2,1)} %fusion.11.x), custom_call_target="tpu_custom_call" | custom-call | tf_op jit(solution)/shard_map/tokens_to_heads/pallas_call | solution.py:112
  397.9 7.5 %attend_back.1 = (bf16[4,128,128]{2,1,0:T(8,128)(2,1)}, bf16[4096,128]{1,0:T(8,128)(2,1)}, bf16[4096,128]{1,0:T(8,128)(2,1)}) custom-call(bf16[4,128,128]{2,1,0:T(8,128)(2,1)} %get-tuple-element.70.q, bf16[4096,128]{1,0:T(8,128)(2,1)} %bitcast.84, bf16[4096,128]{1,0:T(8,128)(2,1)} %bitcast.86, bf16[10,128,1024]{2,1,0:T(8,128)(2,1)} %get-tuple-element.86.probs, ...), custom_call_target="tpu_custom_call" | custom-call | tf_op jit(solution)/shard_map/attend_back/pallas_call | solution.py:112
  405.4 28.1 %collect_heads.1 = (bf16[128,512]{1,0:T(8,128)(2,1)}, bf16[128,512]{1,0:T(8,128)(2,1)}, bf16[128,512]{1,0:T(8,128)(2,1)}) custom-call(bf16[4,128,128]{2,1,0:T(8,128)(2,1)} %get-tuple-element.88.dq, bf16[4,2,4,128,128]{4,3,2,1,0:T(8,128)(2,1)} %bitcast.96, bf16[4,2,4,128,128]{4,3,2,1,0:T(8,128)(2,1)} %bitcast.97), custom_call_target="tpu_custom_call" | custom-call | tf_op jit(solution)/shard_map/collect_heads/pallas_call | solution.py:112
  433.5 1.9 turn_back_heads.1
  435.4 2.5 fusion.91
  437.9 2.0 convolution_convert_fusion.3
  440.0 2.1 convolution_convert_fusion
  442.1 2.1 convolution_convert_fusion.2
  444.1 0.8 convolution_add_fusion.1
  445.0 2.0 convolution_convert_fusion.1
  447.1 1.6 fusion.17
  449.1 0.9 pad.33.clone
  450.0 67.3 %reduce_attention_grads.1 = (f32[64,512]{1,0:T(8,128)}, f32[64,512]{1,0:T(8,128)}, f32[64,512]{1,0:T(8,128)}, f32[64,512]{1,0:T(8,128)}, f32[64,128]{1,0:T(8,128)}, /*index=5*/bf16[128,2048]{1,0:T(8,128)(2,1)}) custom-call(bf16[4,2,4,64,512]{4,3,2,1,0:T(8,128)(2,1)} %bitcast.79, bf16[4,2,4,64,512]{4,3,2,1,0:T(8,128)(2,1)} %bitcast.81, ...), custom_call_target="tpu_custom_call" | custom-call | tf_op jit(solution)/shard_map/reduce_attention_grads/pallas_call | solution.py:112
  517.3 1.4 fusion.18
  518.6 2.2 fusion.22
  520.9 0.7 slice_reduce_fusion
  521.6 10.9 %expert_grads.1 = (f32[2,352,2048]{2,1,0:T(8,128)}, f32[2,352,2048]{2,1,0:T(8,128)}, f32[2,352,2048]{2,1,0:T(8,128)}) custom-call(bf16[2,512,2048]{2,1,0:T(8,128)(2,1)} %get-tuple-element.76.refs_0_.rows, bf16[2,512,2048]{2,1,0:T(8,128)(2,1)} %get-tuple-element.77.refs_1_.grads, bf16[2,512,352]{2,1,0:T(8,128)(2,1)} %get-tuple-element.105.act, ...), custom_call_target="tpu_custom_call" | custom-call | tf_op jit(solution)/shard_map/expert_grads/pallas_call | solution.py:1174
  532.5 0.7 copy.57
  533.2 0.7 copy.58
  533.8 0.7 copy.59
  534.5 0.7 copy.60
  535.2 0.6 copy.61
  535.8 0.7 copy.62
  536.5 0.7 copy.63
  537.1 0.7 copy.64
  (74 shorter events, 2.2 us)
Async XLA Ops:
  7.2 78.0 %copy-start = (bf16[128,2048]{1,0:T(8,128)(2,1)S(1)}, bf16[128,2048]{1,0:T(8,128)(2,1)}, u32[]{:S(2)}) copy-start(bf16[128,2048]{1,0:T(8,128)(2,1)} %param.16) | copy-start | bytes 1572868
  7.2 151.9 %all-gather.2.cloned.1.call-start = ((), (), s32[]{:S(2)}) async-start(), calls=%async_computation | async-start | bytes 12435456 | tf_op jit(solution)/shard_map/all_gather | solution.py:1247
  11.6 0.7 copy-start.16
  91.1 54.2 %copy-start.25 = (s32[128,6]{0,1:T(8,128)S(1)}, s32[128,6]{0,1:T(8,128)}, u32[]{:S(2)}) copy-start(s32[128,6]{0,1:T(8,128)} %param.18) | copy-start | bytes 9220
  177.8 4.4 copy-start.2
  177.8 3.9 copy-start.8
  250.7 100.8 %copy-start.9 = (bf16[128,2048]{1,0:T(8,128)(2,1)S(1)}, bf16[128,2048]{1,0:T(8,128)(2,1)}, u32[]{:S(2)}) copy-start(bf16[128,2048]{1,0:T(8,128)(2,1)} %refs_3_.1) | copy-start | bytes 1572868
  349.8 1.6 copy-start.4
  351.4 1.9 copy-start.10
  352.9 31.2 %copy-start.3 = (bf16[128,2048]{1,0:T(8,128)(2,1)S(1)}, bf16[128,2048]{1,0:T(8,128)(2,1)}, u32[]{:S(2)}) copy-start(bf16[128,2048]{1,0:T(8,128)(2,1)} %copy-done.2) | copy-start | bytes 1572868
  352.9 32.4 %copy-start.7 = (bf16[128,2048]{1,0:T(8,128)(2,1)S(1)}, bf16[128,2048]{1,0:T(8,128)(2,1)}, u32[]{:S(2)}) copy-start(bf16[128,2048]{1,0:T(8,128)(2,1)} %sum_attention.1) | copy-start | bytes 1572868
  384.1 3.6 copy-start.12
  433.5 4.4 copy-start.1
  435.4 2.5 copy-start.14
  437.9 2.1 copy-start.11
  440.0 2.1 copy-start.13
  442.0 2.1 copy-start.6
  444.1 0.9 copy-start.15
  444.9 2.1 copy-start.5
  517.2 3.6 copy-start.17
  521.6 11.0 %copy-start.24 = (f32[64,512]{1,0:T(8,128)S(1)}, f32[64,512]{1,0:T(8,128)}, u32[]{:S(2)}) copy-start(f32[64,512]{1,0:T(8,128)} %get-tuple-element.155) | copy-start | bytes 393220
  521.6 11.6 %copy-start.23 = (f32[64,512]{1,0:T(8,128)S(1)}, f32[64,512]{1,0:T(8,128)}, u32[]{:S(2)}) copy-start(f32[64,512]{1,0:T(8,128)} %get-tuple-element.156) | copy-start | bytes 393220
  521.6 12.3 %copy-start.22 = (f32[64,512]{1,0:T(8,128)S(1)}, f32[64,512]{1,0:T(8,128)}, u32[]{:S(2)}) copy-start(f32[64,512]{1,0:T(8,128)} %get-tuple-element.157) | copy-start | bytes 393220
  521.6 12.9 %copy-start.21 = (f32[64,512]{1,0:T(8,128)S(1)}, f32[64,512]{1,0:T(8,128)}, u32[]{:S(2)}) copy-start(f32[64,512]{1,0:T(8,128)} %get-tuple-element.101) | copy-start | bytes 393220
  521.6 14.2 %copy-start.20 = (f32[64,704]{1,0:T(8,128)S(1)}, f32[64,704]{1,0:T(8,128)}, u32[]{:S(2)}) copy-start(f32[64,704]{1,0:T(8,128)} %get-tuple-element.161) | copy-start | bytes 540676
  521.6 14.9 %copy-start.19 = (f32[64,704]{1,0:T(8,128)S(1)}, f32[64,704]{1,0:T(8,128)}, u32[]{:S(2)}) copy-start(f32[64,704]{1,0:T(8,128)} %get-tuple-element.162) | copy-start | bytes 540676
  521.6 15.5 %copy-start.18 = (f32[64,704]{1,0:T(8,128)S(1)}, f32[64,704]{1,0:T(8,128)}, u32[]{:S(2)}) copy-start(f32[64,704]{1,0:T(8,128)} %get-tuple-element.104) | copy-start | bytes 540676
Sparse Core Ops, SparseCore 0:
  12.5 146.5 all-gather.1

commit v4 on v3

--- a/solution.py
+++ b/solution.py
@@ -66,6 +66,12 @@
 
 def slot_in_pair(i, kind):
     return i % 2 if kind == "A" else 0
+
+def over(left, right, dims):
+    return lax.dot_general(
+        left, right, ((dims[:1], dims[1:]), ((), ())), preferred_element_type=jnp.float32
+    )
+
 
 def head_columns(h):
     return pl.ds(pl.multiple_of(h * HD, HD), HD)
@@ -94,6 +100,11 @@
     programs = list(programs)
     while programs:
         programs = [program for program in programs if next(program, None) is not None]
+
+
+def in_turn(order, programs):
+    for letter in order:
+        next(programs[letter], None)
 
 
 def greet(places):
@@ -207,6 +218,9 @@
     return [(p, *entry) for p in range(4) for entry in parts[p]]
 
 
+CUBE_ORDER = tuple((stage, lane) for stage in range(5) for lane in (1, 0))
+
+
 def reduce_steps(parts, ins, outs, bufs, copies):
     entries = entries_of(parts)
     z, xh, y = own_place()
@@ -309,11 +323,11 @@
             )
             outs[a][rows, cols] = total.astype(outs[a].dtype)
 
-    for stage in (first, second, third, fourth, last):
-        for lane in (1, 0):
-            for e in range(len(entries)):
-                stage(lane, e)
-            yield True
+    stages = (first, second, third, fourth, last)
+    for at, lane in CUBE_ORDER:
+        for e in range(len(entries)):
+            stages[at](lane, e)
+        yield True
     copies.finish()
 
 
@@ -420,142 +434,76 @@
         name=name,
     )(x)
 
-def project_kernel(normed, wq, wk, wv, cosine, sine, q, k, v):
-    for weight, out in ((wq, q), (wk, k)):
-        raw = jnp.dot(normed[...], weight[...], preferred_element_type=jnp.float32)
-        for h in range(out.shape[1] // HD):
-            one = raw[:, h * HD : (h + 1) * HD]
-            turned = one * cosine[...] + pltpu.roll(one, HD // 2, 1) * sine[...]
-            out[:, h * HD : (h + 1) * HD] = turned.astype(out.dtype)
-    raw = jnp.dot(normed[...], wv[...], preferred_element_type=jnp.float32)
-    v[...] = raw.astype(v.dtype)
-
-
-def project(normed, weights, cosine, sine):
-    shape = jax.ShapeDtypeStruct((normed.shape[0], weights[0].shape[1]), jnp.bfloat16)
-    return vmem_call(
-        project_kernel, [shape] * 3, (normed, *weights, cosine, sine), [], None, "project_heads"
-    )
-
-
-def turn_back_kernel(q, k, cosine, sine, q_in, k_in):
-    for src, out in ((q, q_in), (k, k_in)):
-        for h in range(out.shape[1] // HD):
-            one = src[:, h * HD : (h + 1) * HD].astype(jnp.float32)
-            turned = one * cosine[...] - pltpu.roll(one, HD // 2, 1) * sine[...]
-            out[:, h * HD : (h + 1) * HD] = turned.astype(out.dtype)
-
-
-def turn_back(q, k, cosine, sine):
-    shape = jax.ShapeDtypeStruct(q.shape, jnp.bfloat16)
-    return vmem_call(
-        turn_back_kernel, [shape] * 2, (q, k, cosine, sine), [], None, "turn_back_heads"
-    )
-
-
-def spread_kernel(q, k, v, q_out, k_out, v_out, send_sem, recv_sem):
+def ctx_gather_steps(parts, copies):
     z, xh, y = own_place()
-    places = along_z() + [neighbour("y", "A"), neighbour("y", "B"), neighbour("x", "A")]
-    greet(places)
-    copies = Copies(send_sem, recv_sem)
-    arriving = []
-    for d in (1, 2, 3):
-        there = (z + d) % 4
-        cols = head_columns(there)
-        for src, dst in (
-            (k, k_out.at[z, xh, y]), (v, v_out.at[z, xh, y]), (q, q_out.at[z])
-        ):
-            arriving.append(copies.start(src.at[:, cols], dst, {"sp": there}))
-    k_out[z, xh, y] = k[:, head_columns(z)]
-    v_out[z, xh, y] = v[:, head_columns(z)]
-    q_out[z] = q[:, head_columns(z)]
-    for copy in arriving:
-        copy.wait_recv()
-
-    def block(out, xl, place):
-        return out.at[:, xl, place]
-
-    def send(out, xl, place, axis, kind):
-        where = neighbour(axis, kind)
-        return copies.start(block(out, xl, place), block(out, xl, place), where)
-
-    first, across = {}, []
-    for out, kind in ((k_out, "A"), (v_out, "B")):
-        first[0, kind] = send(out, xh, y, "y", kind)
-        across.append(send(out, xh, y, "x", "A"))
-    last = []
-
-    def onward(lane, xl):
-        first[lane, "A"].wait_recv()
-        for place, _ in pair_slots(y, "A"):
-            last.append(send(k_out, xl, place, "y", "B"))
-        first[lane, "B"].wait_recv()
-        for place, _ in pair_slots(y, "B"):
-            last.append(send(v_out, xl, place, "y", "A"))
-
-    onward(0, xh)
-    for copy in across:
-        copy.wait_recv()
-    for out, kind in ((k_out, "A"), (v_out, "B")):
-        first[1, kind] = send(out, 1 - xh, y, "y", kind)
-    onward(1, 1 - xh)
+
+    def send(part, xl, place, axis, kind):
+        ref, rows = part
+        block = ref.at[:, xl, place, rows]
+        return copies.start(block, block, neighbour(axis, kind))
+
+    near, far = ("A", "B"), ("B", "A")
+    first, across, last = {}, [], []
+    for a in range(2):
+        first[0, a] = send(parts[a], xh, y, "y", near[a])
+        across.append(send(parts[a], xh, y, "x", "A"))
+    yield True
+    for lane in range(2):
+        xl = xh if lane == 0 else 1 - xh
+        if lane == 1:
+            for a in range(2):
+                across[a].wait_recv()
+                first[1, a] = send(parts[a], xl, y, "y", near[a])
+            yield True
+        for a in range(2):
+            first[lane, a].wait_recv()
+            for place, _ in pair_slots(y, near[a]):
+                last.append(send(parts[a], xl, place, "y", far[a]))
+        yield True
     for copy in last:
         copy.wait_recv()
     copies.finish()
 
 
-def spread_heads(q, k, v, collective_id):
-    rows = q.shape[0]
-    own = jax.ShapeDtypeStruct((4, rows, HD), q.dtype)
-    every = jax.ShapeDtypeStruct((4, 2, 4, rows, HD), q.dtype)
-    sems = [pltpu.SemaphoreType.DMA((21,))] * 2
-    return vmem_call(
-        spread_kernel, [own, every, every], (q, k, v), sems, collective_id, "spread_heads"
-    )
-
-
-def collect_kernel(dq, dk, dv, q_out, k_out, v_out, *refs):
-    bufs, sums, cross = refs[0:2], refs[2:4], refs[4:6]
-    own, (send_sem, recv_sem) = refs[6:8], refs[8:]
+CTX_ORDER = ((0, 1), (1, 1), (0, 0), (2, 1), (1, 0), (2, 0))
+
+
+def ctx_reduce_steps(parts, bufs, sums, cross, own, copies):
     z, xh, y = own_place()
-    greet(along_z() + [neighbour("y", "A"), neighbour("y", "B"), neighbour("x", "A")])
-    copies = Copies(send_sem, recv_sem)
-    ins, near, far = (dk, dv), ("A", "B"), ("B", "A")
+    near, far = ("A", "B"), ("B", "A")
     flying = {}
-    for lane in (1, 0):
+
+    def first(lane):
         xl = xh if lane == 0 else 1 - xh
-        for a in range(2):
-            theirs = paired(y, far[a])
+        for a, (ref, rows) in enumerate(parts):
             flying[lane, a] = [
-                copies.start(ins[a].at[:, xl, src], bufs[a].at[lane, :, dst], neighbour("y", far[a]))
-                for src, dst in pair_slots(theirs, near[a])
+                copies.start(
+                    ref.at[:, xl, src, rows], bufs[a].at[lane, :, dst], neighbour("y", far[a])
+                )
+                for src, dst in pair_slots(paired(y, far[a]), near[a])
             ]
-    arriving = []
-    for d in (1, 2, 3):
-        there = (z + d) % 4
-        arriving.append(copies.start(dq.at[there], q_out.at[:, head_columns(z)], {"sp": there}))
-    q_out[:, head_columns(z)] = dq[z]
-    for lane in (1, 0):
+
+    def second(lane):
         xl = xh if lane == 0 else 1 - xh
-        for a in range(2):
+        for a, (ref, rows) in enumerate(parts):
             for copy in flying[lane, a]:
                 copy.wait_recv()
             slot = slot_in_pair(y, near[a])
-            there = paired(y, near[a])
 
             def add(j, place):
                 def one(i, carry):
-                    bufs[a][lane, i, j] = bufs[a][lane, i, j] + ins[a][i, xl, place]
+                    bufs[a][lane, i, j] = bufs[a][lane, i, j] + ref[i, xl, place, rows]
                     return carry
 
                 lax.fori_loop(0, 4, one, 0)
 
-            add(1 - slot, there)
+            add(1 - slot, paired(y, near[a]))
             flying[lane, a] = copies.start(
                 bufs[a].at[lane, :, 1 - slot], sums[a].at[lane], neighbour("y", near[a])
             )
             add(slot, y)
-    for lane in (1, 0):
+
+    def third(lane):
         for a in range(2):
             flying[lane, a].wait_recv()
             slot = slot_in_pair(y, near[a])
@@ -567,7 +515,11 @@
             lax.fori_loop(0, 4, more, 0)
             if lane == 1:
                 flying["x", a] = copies.start(sums[a].at[1], cross[a], neighbour("x", "A"))
-    for a, out in ((0, k_out), (1, v_out)):
+
+    for stage, lane in CTX_ORDER:
+        (first, second, third)[stage](lane)
+        yield True
+    for a in range(2):
         flying["x", a].wait_recv()
 
         def total(i, carry):
@@ -575,78 +527,133 @@
             return carry
 
         lax.fori_loop(0, 4, total, 0)
-        for d in (1, 2, 3):
-            there = (z + d) % 4
-            arriving.append(copies.start(own[a].at[there], out.at[:, head_columns(z)], {"sp": there}))
-        out[:, head_columns(z)] = own[a][z]
-    for copy in arriving:
+    yield True
+    copies.finish()
+
+
+def ctx_scratch(shapes, dtype):
+    scratch = [
+        pltpu.VMEM((*lead, *shape), dtype) for lead in ((2, 4, 2), (2, 4), (4,), (4,)) for shape in shapes
+    ]
+    return scratch + [pltpu.SemaphoreType.DMA((12,))] * 2
+
+
+def column_halves(width):
+    return [pl.ds(0, width // 2), pl.ds(width // 2, width // 2)]
+
+
+def rows_gather_steps(x, out, copies):
+    z = lax.axis_index("sp")
+    near, far = ("A", "B"), ("B", "A")
+    halves = column_halves(x.shape[1])
+    first = [
+        copies.start(x.at[:, halves[a]], out.at[z, :, halves[a]], neighbour("z", near[a]))
+        for a in range(2)
+    ]
+    out[z] = x[...]
+    yield True
+    last = []
+    for a in range(2):
+        first[a].wait_recv()
+        for place, _ in pair_slots(z, near[a]):
+            block = out.at[place, :, halves[a]]
+            last.append(copies.start(block, block, neighbour("z", far[a])))
+    yield True
+    for copy in last:
         copy.wait_recv()
     copies.finish()
 
 
-def collect_heads(dq, dk, dv, collective_id):
-    rows = dq.shape[1]
-    block = (rows, HD)
-    shape = jax.ShapeDtypeStruct((rows, 4 * HD), dq.dtype)
-    scratch = [
-        pltpu.VMEM((*lead, *block), dq.dtype) for lead in ((2, 4, 2), (2, 4), (4,), (4,)) for _ in range(2)
+def rows_reduce_steps(x, out, bufs, sums, copies):
+    z = lax.axis_index("sp")
+    near, far = ("A", "B"), ("B", "A")
+    halves = column_halves(x.shape[2])
+    flying = [
+        [
+            copies.start(x.at[src, :, halves[a]], bufs[a].at[dst], neighbour("z", far[a]))
+            for src, dst in pair_slots(paired(z, far[a]), near[a])
+        ]
+        for a in range(2)
     ]
-    sems = [pltpu.SemaphoreType.DMA((21,))] * 2
-    return vmem_call(
-        collect_kernel, [shape] * 3, (dq, dk, dv), scratch + sems, collective_id, "collect_heads"
-    )
-
-
-def heads_out_kernel(x, out, send_sem, recv_sem):
-    z = lax.axis_index("sp")
-    greet(along_z())
-    copies = Copies(send_sem, recv_sem)
+    yield True
+    second = []
+    for a in range(2):
+        for copy in flying[a]:
+            copy.wait_recv()
+        slot = slot_in_pair(z, near[a])
+        bufs[a][1 - slot] = bufs[a][1 - slot] + x[paired(z, near[a]), :, halves[a]]
+        second.append(copies.start(bufs[a].at[1 - slot], sums[a], neighbour("z", near[a])))
+        bufs[a][slot] = bufs[a][slot] + x[z, :, halves[a]]
+    yield True
+    for a in range(2):
+        second[a].wait_recv()
+        slot = slot_in_pair(z, near[a])
+        out[:, halves[a]] = bufs[a][slot] + sums[a][...]
+    yield True
+    copies.finish()
+
+
+def gather_head_kernel(x, w, rows_out, weights_out, *sems):
+    z, xh, y = own_place()
+    greet(along_z() + [neighbour("y", "A"), neighbour("y", "B"), neighbour("x", "A")])
+    turns = Copies(*sems[:2])
+    heads = w.shape[1] // HD // 4
+
+    def columns(k, h):
+        return pl.ds(pl.multiple_of(k * 4 * HD + h * HD, HD), HD)
+
     for d in (1, 2, 3):
         there = (z + d) % 4
-        copies.start(x.at[there], out.at[:, head_columns(z)], {"sp": there})
-    out[:, head_columns(z)] = x[z]
-    for copy in copies.started:
+        for k in range(heads):
+            place = weights_out.at[z, xh, y, :, pl.ds(k * HD, HD)]
+            turns.start(w.at[:, columns(k, there)], place, {"sp": there})
+    rows = rows_gather_steps(x, rows_out, Copies(*sems[2:4]))
+    next(rows)
+    for k in range(heads):
+        weights_out[z, xh, y, :, k * HD : (k + 1) * HD] = w[:, columns(k, z)]
+    for copy in turns.started:
         copy.wait_recv()
-    copies.finish()
-
-
-def heads_in_kernel(x, out, send_sem, recv_sem):
-    z = lax.axis_index("sp")
-    greet(along_z())
-    copies = Copies(send_sem, recv_sem)
-    for d in (1, 2, 3):
-        there = (z + d) % 4
-        copies.start(x.at[:, head_columns(there)], out.at[z], {"sp": there})
-    out[z] = x[:, head_columns(z)]
-    for copy in copies.started:
-        copy.wait_recv()
-    copies.finish()
-
-
-def heads_out(x, collective_id):
-    shape = jax.ShapeDtypeStruct((x.shape[1], 4 * HD), x.dtype)
-    sems = [pltpu.SemaphoreType.DMA((3,))] * 2
-    return vmem_call(heads_out_kernel, shape, (x,), sems, collective_id, "heads_to_tokens")
-
-
-def heads_in(x, collective_id):
-    shape = jax.ShapeDtypeStruct((4, x.shape[0], HD), x.dtype)
-    sems = [pltpu.SemaphoreType.DMA((3,))] * 2
-    return vmem_call(heads_in_kernel, shape, (x,), sems, collective_id, "tokens_to_heads")
-
-
-def attend_kernel(q, k, v, attended, exact, probs, scores):
+    half = w.shape[0] // 2
+    parts = [(weights_out, pl.ds(a * half, half)) for a in range(2)]
+    run(ctx_gather_steps(parts, Copies(*sems[4:6])), rows)
+    turns.finish()
+
+
+def gather_head(x, w, collective_id):
+    out_shape = [
+        jax.ShapeDtypeStruct((4, *x.shape), x.dtype),
+        jax.ShapeDtypeStruct((4, 2, 4, w.shape[0], w.shape[1] // 4), w.dtype),
+    ]
+    sems = [pltpu.SemaphoreType.DMA((n,)) for n in (9, 9, 5, 5, 12, 12)]
+    return vmem_call(gather_head_kernel, out_shape, (x, w), sems, collective_id, "gather_head")
+
+
+def project_kernel(x, w, cosine, sine, q, k, v):
+    raw = jnp.dot(x[...], w[...], preferred_element_type=jnp.float32)
+    for at, out in enumerate((q, k)):
+        one = raw[:, at * HD : (at + 1) * HD]
+        out[...] = (one * cosine[...] + pltpu.roll(one, HD // 2, 1) * sine[...]).astype(out.dtype)
+    v[...] = raw[:, 2 * HD :].astype(v.dtype)
+
+
+def project(x, w, cosine, sine):
+    shape = jax.ShapeDtypeStruct((x.shape[0], HD), x.dtype)
+    return vmem_call(project_kernel, [shape] * 3, (x, w, cosine, sine), [], None, "project_head")
+
+
+def attend_steps(q, k, v, blocks, exact, probs, scores):
     rows = q.shape[1]
     span = 8 * rows
     first = lax.axis_index("ctx") * rows
     scale = HD ** (-0.5)
-    contract = (((1,), (1,)), ((), ()))
     at = 0
+
+    def chunk(ref, c):
+        return ref[c].reshape(span, HD)
+
     for block in range(4):
         for c in range(block + 1):
-            part = lax.dot_general(
-                q[block], k[c * span : (c + 1) * span], contract, preferred_element_type=jnp.float32
-            ) * scale
+            part = over(q[block], chunk(k, c), (1, 1)) * scale
             if c == block:
                 row = lax.broadcasted_iota(jnp.int32, part.shape, 0)
                 col = lax.broadcasted_iota(jnp.int32, part.shape, 1)
@@ -664,69 +671,225 @@
         for c in range(block + 1):
             low = (scores[:, c * span : (c + 1) * span] * scaled).astype(probs.dtype)
             probs[at] = low
-            result = result + jnp.dot(
-                low, v[c * span : (c + 1) * span], preferred_element_type=jnp.float32
-            )
+            result = result + over(low, chunk(v, c), (1, 0))
             at += 1
         exact[block] = result
-        attended[block] = result.astype(attended.dtype)
-
-
-def attend(q, k, v):
-    rows = q.shape[1]
+        blocks[block] = result.astype(blocks.dtype)
+        yield True
+
+
+ATTEND_ORDER = "KGGKGKGKGK" + "AGAGAGA"
+
+
+def attention_kernel(parts, q, k, v, own, total, attended, keys, values, probs, exact, whole, *refs):
+    scores, blocks, part, *wa_bufs = refs[:6]
+    sems = refs[6:]
+    z, xh, y = own_place()
+    places = along_z() + [neighbour("y", "A"), neighbour("y", "B"), neighbour("x", "A")]
+    greet(places + wa_places())
+    keys[:, xh, y] = k[...]
+    values[:, xh, y] = v[...]
+    rows = pl.ds(0, k.shape[1])
+    programs = {
+        "K": ctx_gather_steps([(keys, rows), (values, rows)], Copies(*sems[0:2])),
+        "G": gather_steps(parts, [own], [whole], Copies(*sems[2:4]), sems[4]),
+        "A": attend_steps(q, keys, values, blocks, exact, probs, scores),
+    }
+    in_turn(ATTEND_ORDER, programs)
+    turns = Copies(*sems[5:7])
+    for d in (1, 2, 3):
+        there = (z + d) % 4
+        turns.start(blocks.at[there], attended.at[:, head_columns(z)], {"sp": there})
+    attended[:, head_columns(z)] = blocks[z]
+    run(programs["G"])
+    for copy in turns.started:
+        copy.wait_recv()
+    turns.finish()
+    width = attended.shape[1]
+    step = D // 4
+    for i in range(4):
+        weights = whole[i].reshape(step, -1)[:, :width]
+        part[:, i * step : (i + 1) * step] = over(attended[...], weights, (1, 1)).astype(part.dtype)
+    run(sum_wa_steps(part, total, *wa_bufs, Copies(*sems[7:9])))
+
+
+def attention(q, k, v, own, collective_id):
+    rows, low = q.shape[1], q.dtype
+    every = jax.ShapeDtypeStruct((4, 2, 4, rows, HD), low)
     out_shape = [
-        jax.ShapeDtypeStruct(q.shape, q.dtype),
+        jax.ShapeDtypeStruct((rows, D), low),
+        jax.ShapeDtypeStruct((rows, 4 * HD), low),
+        every,
+        every,
+        jax.ShapeDtypeStruct((10, rows, 8 * rows), low),
         jax.ShapeDtypeStruct(q.shape, jnp.float32),
-        jax.ShapeDtypeStruct((10, rows, 8 * rows), q.dtype),
+        jax.ShapeDtypeStruct((4, 2, 4, *own.shape), low),
     ]
-    scratch = [pltpu.VMEM((rows, 32 * rows), jnp.float32)]
-    return vmem_call(attend_kernel, out_shape, (q, k, v), scratch, None, "attend")
-
-
-def attend_back_kernel(q, k, v, probs, grad, exact, dq, dk, dv, dk_sum, dv_sum):
+    scratch = [pltpu.VMEM((rows, 32 * rows), jnp.float32), pltpu.VMEM(q.shape, low)]
+    scratch += [pltpu.VMEM((rows, D), low)] + [pltpu.VMEM((rows, D // 2), low)] * 3
+    scratch += [pltpu.SemaphoreType.DMA((n,)) for n in (12, 12, 44, 44, 1, 3, 3, 3, 3)]
+    return vmem_call(
+        functools.partial(attention_kernel, row_parts([own])), out_shape, (q, k, v, own), scratch,
+        collective_id, "attention",
+    )
+
+
+def attend_back_steps(q, k, v, probs, grad, exact, dq, dk, dv, dk_sum, dv_sum):
     rows = q.shape[1]
     span = 8 * rows
     scale = HD ** (-0.5)
     at = 0
+
+    def chunk(ref, c):
+        return ref[c].reshape(span, HD)
+
     for block in range(4):
         low_grad = grad[block]
         delta = jnp.sum(low_grad.astype(jnp.float32) * exact[block], axis=1, keepdims=True)
         total = jnp.zeros((rows, HD), jnp.float32)
         for c in range(block + 1):
-            here = slice(c * span, (c + 1) * span)
             low = probs[at]
-            back = lax.dot_general(
-                low_grad, v[here], (((1,), (1,)), ((), ())), preferred_element_type=jnp.float32
-            )
+            back = over(low_grad, chunk(v, c), (1, 1))
             terms = (low.astype(jnp.float32) * (back - delta)).astype(q.dtype)
-            total = total + jnp.dot(terms, k[here], preferred_element_type=jnp.float32)
-            over_rows = (((0,), (0,)), ((), ()))
-            key_terms = lax.dot_general(
-                terms, q[block], over_rows, preferred_element_type=jnp.float32
-            )
-            value_terms = lax.dot_general(
-                low, low_grad, over_rows, preferred_element_type=jnp.float32
-            )
+            total = total + over(terms, chunk(k, c), (1, 0))
+            key_terms = over(terms, q[block], (0, 0))
+            value_terms = over(low, low_grad, (0, 0))
             if c == block:
-                dk_sum[here] = key_terms
-                dv_sum[here] = value_terms
+                dk_sum[c] = key_terms
+                dv_sum[c] = value_terms
             else:
-                dk_sum[here] = dk_sum[here] + key_terms
-                dv_sum[here] = dv_sum[here] + value_terms
+                dk_sum[c] = dk_sum[c] + key_terms
+                dv_sum[c] = dv_sum[c] + value_terms
             at += 1
         dq[block] = (total * scale).astype(dq.dtype)
+        yield True
     for c in range(4):
-        here = slice(c * span, (c + 1) * span)
-        dk[here] = (dk_sum[here] * scale).astype(dk.dtype)
-        dv[here] = dv_sum[here].astype(dv.dtype)
-
-
-def attend_back(q, k, v, probs, grad, exact):
-    out_shape = [jax.ShapeDtypeStruct(x.shape, x.dtype) for x in (q, k, v)]
-    scratch = [pltpu.VMEM(k.shape, jnp.float32)] * 2
+        dk[c] = (dk_sum[c] * scale).astype(dk.dtype).reshape(dk.shape[1:])
+        dv[c] = dv_sum[c].astype(dv.dtype).reshape(dv.shape[1:])
+    yield True
+
+
+def project_back_steps(dq, dk, dv, cosine, sine, x, w, back, grad):
+    low = back.dtype
+    rows = dq.shape[1]
+    terms = []
+    for src in (dq, dk):
+        one = src[...].reshape(4 * rows, HD).astype(jnp.float32)
+        terms.append((one * cosine[...] - pltpu.roll(one, HD // 2, 1) * sine[...]).astype(low))
+    terms = jnp.concatenate([*terms, dv[...].reshape(4 * rows, HD)], axis=1)
+    step = D // 4
+    for i in range(4):
+        here = slice(i * step, (i + 1) * step)
+        back[:, :, here] = over(terms, w[here], (1, 1)).astype(low).reshape(4, rows, step)
+        grad[i] = over(x[:, here], terms, (0, 0)).astype(low).reshape(grad.shape[1:])
+        yield True
+
+
+BACK_ORDER = "RRAAAAA" + "CRRCCRRCCRRRRCRRCC"
+
+
+def attention_back_kernel(parts, count, *refs):
+    attended_grad, q, keys, values, probs, exact, cosine, sine, x, w, heads, *refs = refs
+    summed, refs = refs[:count], refs[count:]
+    total, grad_out, gain_out, *refs = refs
+    shares, refs = refs[:count], refs[count:]
+    head_grad, dq, dk, dv, dk_sum, dv_sum, back, grad, mixed, *refs = refs
+    z_bufs, z_sums, wa_bufs, gain_bufs = refs[0:2], refs[2:4], refs[4:7], refs[7:9]
+    refs = refs[9:]
+    (kv_bufs, kv_sums, kv_cross, kv_own), refs = (refs[2 * i : 2 * i + 2] for i in range(4)), refs[8:]
+    kv_sems, refs = refs[:2], refs[2:]
+    (bufs, sums, cross, own), refs = (refs[2 * i : 2 * i + 2] for i in range(4)), refs[8:]
+    head_sems, refs = refs[:2], refs[2:]
+    sems, refs = refs[:10], refs[10:]
+    cube_bufs, cube_sems = refs[:-2], refs[-2:]
+    z = lax.axis_index("sp")
+    places = along_z() + [neighbour("y", "A"), neighbour("y", "B"), neighbour("x", "A")]
+    greet(places + wa_places())
+    turns = Copies(*sems[0:2])
+    for d in (1, 2, 3):
+        there = (z + d) % 4
+        turns.start(attended_grad.at[:, head_columns(there)], head_grad.at[z], {"sp": there})
+    head_grad[z] = attended_grad[:, head_columns(z)]
+    rows = pl.ds(0, dq.shape[1])
+    programs = {
+        "R": reduce_steps(parts, summed, shares, cube_bufs, Copies(*cube_sems)),
+        "A": attend_back_steps(
+            q, keys, values, probs, head_grad, exact, dq, dk, dv, dk_sum, dv_sum
+        ),
+        "C": ctx_reduce_steps(
+            [(dk, rows), (dv, rows)], kv_bufs, kv_sums, kv_cross, kv_own, Copies(*kv_sems)
+        ),
+    }
+    in_turn("RR", programs)
+    for copy in turns.started:
+        copy.wait_recv()
+    turns.finish()
+    in_turn(BACK_ORDER, programs)
+    run(programs["C"])
+    run(project_back_steps(dq, *kv_own, cosine, sine, x, w, back, grad))
+    half = grad.shape[3] // 2
+    grad_parts = [(grad, pl.ds(a * half, half)) for a in range(2)]
+
+    def sums_of_rows():
+        yield from rows_reduce_steps(back, mixed, z_bufs, z_sums, Copies(*sems[2:4]))
+        yield from sum_wa_steps(mixed, total, *wa_bufs, Copies(*sems[4:6]))
+
+    def grads():
+        yield from ctx_reduce_steps(grad_parts, bufs, sums, cross, own, Copies(*head_sems))
+        turns = Copies(*sems[6:8])
+        for d in (1, 2, 3):
+            there = (z + d) % 4
+            for a in range(2):
+                turns.start(own[a].at[there], grad_out.at[z, grad_parts[a][1]], {"sp": there})
+        for a in range(2):
+            grad_out[z, a * half : (a + 1) * half] = own[a][z]
+        yield True
+        for copy in turns.started:
+            copy.wait_recv()
+        turns.finish()
+        products = jnp.zeros(gain_out.shape, jnp.float32)
+        for h in range(4):
+            for k in range(grad_out.shape[2] // HD):
+                ours = heads[:, (4 * k + h) * HD : (4 * k + h + 1) * HD].astype(jnp.float32)
+                theirs = grad_out[h, :, k * HD : (k + 1) * HD].astype(jnp.float32)
+                products = products + ours * theirs
+        gain_out[...] = products
+        copies = Copies(*sems[8:10])
+        for place, buf in zip(wa_places(), gain_bufs):
+            copy = copies.start(gain_out, buf, place)
+            yield True
+            copy.wait()
+            gain_out[...] = gain_out[...] + buf[...]
+
+    run(grads(), sums_of_rows(), programs["R"])
+
+
+def attention_back(operands, summed, collective_id):
+    attended_grad, q, keys, _, _, _, _, _, x, w, heads = operands
+    rows, low = q.shape[1], q.dtype
+    shard = heads.shape[0]
+    parts = row_parts(summed)
+    out_shape = [
+        jax.ShapeDtypeStruct((rows, D), low),
+        jax.ShapeDtypeStruct((4, shard, w.shape[1]), low),
+        jax.ShapeDtypeStruct((shard, HD), jnp.float32),
+    ]
+    out_shape += [jax.ShapeDtypeStruct(a.shape[3:], jnp.float32) for a in summed]
+    wide = (rows, D // 2)
+    sums = pltpu.VMEM((4, 8 * rows, HD), jnp.float32)
+    scratch = [pltpu.VMEM(a.shape, low) for a in (q, q, keys, keys)] + [sums, sums]
+    scratch += [pltpu.VMEM((4, rows, D), low), pltpu.VMEM((4, 2, 4, shard, w.shape[1]), low)]
+    scratch += [pltpu.VMEM((rows, D), low)]
+    scratch += [pltpu.VMEM((2, *wide), low)] * 2 + [pltpu.VMEM(wide, low)] * 5
+    scratch += [pltpu.VMEM((shard, HD), jnp.float32)] * 2
+    scratch += ctx_scratch([(rows, HD)] * 2, low) + ctx_scratch([(shard // 2, w.shape[1])] * 2, low)
+    scratch += [pltpu.SemaphoreType.DMA((n,)) for n in (3, 3, 5, 5, 3, 3, 6, 6, 2, 2)]
+    scratch += reduce_scratch(summed, parts)
     return vmem_call(
-        attend_back_kernel, out_shape, (q, k, v, probs, grad, exact), scratch, None, "attend_back"
-    )
+        functools.partial(attention_back_kernel, parts, len(summed)), out_shape,
+        (*operands, *summed), scratch, collective_id, "attention_back",
+    )
+
 
 SLOTS = 16
 GROUP_ORDER = ((0, 1), (1, 0), (3, 0), (1, 1), (3, 1), (2, 0), (2, 1), (0, 0))
@@ -1108,48 +1271,6 @@
     )
 
 
-def tail_kernel(parts, count, *refs):
-    ins, x = refs[:count], refs[count]
-    outs, total = refs[count + 1 : 2 * count + 1], refs[2 * count + 1]
-    half, got, far, small_got, small_far = refs[2 * count + 2 : 2 * count + 7]
-    bufs, more = refs[2 * count + 7 : -6], refs[-6:]
-    greet(cube_places() + wa_places())
-    run(
-        reduce_steps(parts, ins, outs, bufs, Copies(*more[:2])),
-        sum_wa_steps(x, total, half, got, far, Copies(*more[2:4])),
-    )
-    beside, across = wa_places()
-    copies = Copies(*more[4:])
-    small = outs[count - 1]
-    copies.start(small, small_got, beside).wait()
-    small[...] = small[...] + small_got[...]
-    copies.start(small, small_far, across).wait()
-    small[...] = small[...] + small_far[...]
-
-
-def reduce_and_sum(arrays, parts, x, collective_id):
-    count = len(arrays)
-    rows, columns = x.shape
-    out_shape = [jax.ShapeDtypeStruct(a.shape[3:], jnp.float32) for a in arrays]
-    scratch = [pltpu.VMEM((rows, columns // 2), x.dtype)] * 3
-    scratch += [pltpu.VMEM(arrays[-1].shape[3:], jnp.float32)] * 2
-    scratch += reduce_scratch(arrays, parts)
-    scratch += [pltpu.SemaphoreType.DMA((3,))] * 2 + [pltpu.SemaphoreType.DMA((2,))] * 2
-    return vmem_call(
-        functools.partial(tail_kernel, parts, count),
-        [*out_shape, jax.ShapeDtypeStruct(x.shape, x.dtype)],
-        (*arrays, x),
-        scratch,
-        collective_id,
-        "reduce_attention_grads",
-    )
-
-def over(left, right, dims):
-    return lax.dot_general(
-        left, right, ((dims[:1], dims[1:]), ((), ())), preferred_element_type=jnp.float32
-    )
-
-
 def swish_parts(pre, lin, act_grads):
     sig = jax.nn.sigmoid(pre)
     swish = pre * sig
@@ -1225,46 +1346,45 @@
     head_cols = query_weight.shape[1]
     experts_all = router_weight.shape[1]
     groups = ("sp", "ctx")
-    device_pos = lax.axis_index("sp") * lax.axis_size("ctx") + lax.axis_index("ctx")
     place, core = lax.axis_index("wa") // 2, lax.axis_index("wa") % 2
     quarter_at = core * (D // 2) + place * (D // 4)
 
     def quarter(x):
         return lax.dynamic_slice_in_dim(x, quarter_at, D // 4, 1)
 
-    heads = (query_weight, key_weight, value_weight)
-    gain_rows = attn_gain.shape[0]
-    gains = jnp.pad(jnp.stack([attn_gain, mlp_gain]), ((0, 14), (0, HD - gain_rows)))
-    parts = row_parts(heads)
-    parts[0].append((3, pl.ds(0, 16), pl.ds(0, HD)))
-    *wholes, full_gains = gather_cube((*heads, gains), parts, 1, "gather_head_weights")
-    full_query, full_key, full_value = (whole.reshape(D, head_cols) for whole in wholes)
     hidden_cols = shared_gate.shape[1]
-    padded = [
-        jnp.pad(x, ((0, 0), (0, -x.shape[1] % HD)))
-        for x in (output_weight.T, router_weight, shared_gate, shared_up, shared_down.T)
-    ]
-    whole = lax.all_gather(jnp.concatenate(padded, axis=1), groups, axis=0, tiled=True)
-    turned = whole[:, :head_cols]
-    full_router = whole[:, head_cols : head_cols + experts_all]
-    shared_first = head_cols + HD
-    gain_one, gain_two = (
-        full_gains[..., k, :gain_rows].reshape(D).astype(jnp.float32) for k in range(2)
-    )
+    def beside(arrays):
+        return jnp.concatenate(
+            [jnp.pad(x, ((0, 0), (0, -x.shape[1] % HD))) for x in arrays], axis=1
+        )
+
+    shared_whole = lax.all_gather(
+        beside((shared_gate, shared_up, shared_down.T)), groups, axis=0, tiled=True
+    )
+    router_own = jnp.concatenate([router_weight, mlp_gain[:, None]], axis=1)
     tokens_f = tokens.astype(jnp.float32)
     inv_one = lax.rsqrt(jnp.mean(tokens_f * tokens_f, axis=-1, keepdims=True) + EPSILON)
     unit_one = tokens_f * inv_one
-    normed = (unit_one * gain_one).astype(low)
-    query_pos = device_pos * local_tokens + jnp.arange(local_tokens, dtype=jnp.int32)
-    cosine, sine = rope_tables(query_pos.astype(jnp.float32))
-    queries, keys, values = project(normed, (full_query, full_key, full_value), cosine, sine)
-    head_queries, head_keys, head_values = spread_heads(queries, keys, values, 2)
-    head_keys = head_keys.reshape(-1, HD)
-    head_values = head_values.reshape(-1, HD)
-    head_attended, exact, probs = attend(head_queries, head_keys, head_values)
-    attended = heads_out(head_attended, 3)
-    attn_part = dot(attended, turned, (1, 1)).astype(low)
-    attn_out = sum_wa(attn_part, 4, "sum_attention").astype(jnp.float32)
+    gain_one = attn_gain.astype(jnp.float32)[:, None]
+    heads = jnp.concatenate([query_weight, key_weight, value_weight], axis=1)
+    scaled = (gain_one * heads.astype(jnp.float32)).astype(low)
+    head_rows, head_weights = gather_head(unit_one.astype(low), scaled, 1)
+    head_rows, head_weights = head_rows.reshape(-1, D), head_weights.reshape(D, -1)
+    blocks = jnp.arange(4, dtype=jnp.int32)[:, None] * 8 + lax.axis_index("ctx")
+    positions = blocks * local_tokens + jnp.arange(local_tokens, dtype=jnp.int32)[None, :]
+    cosine, sine = rope_tables(positions.reshape(-1).astype(jnp.float32))
+    by_head = (4, local_tokens, HD)
+    head_queries, own_keys, own_values = (
+        x.reshape(by_head) for x in project(head_rows, head_weights, cosine, sine)
+    )
+    attn_out, attended, head_keys, head_values, probs, exact, whole = attention(
+        head_queries, own_keys, own_values, beside((output_weight.T, router_own)), 2
+    )
+    attn_out = attn_out.astype(jnp.float32)
+    whole = whole.reshape(D, -1)
+    turned = whole[:, :head_cols]
+    full_router = whole[:, head_cols : head_cols + experts_all]
+    gain_two = whole[:, head_cols + experts_all].astype(jnp.float32)
     hidden_state = tokens_f + attn_out
     inv_two = lax.rsqrt(jnp.mean(hidden_state * hidden_state, axis=-1, keepdims=True) + EPSILON)
     unit_two = hidden_state * inv_two
@@ -1299,8 +1419,8 @@
         (send_rows.reshape(by_owner), send_grads.reshape(by_owner)),
         mlp_in,
         cotangent,
-        whole,
-        shared_first,
+        shared_whole,
+        0,
         hidden_cols,
         5,
     )
@@ -1346,59 +1466,49 @@
     router_grad = dot(mlp_in, logit_grads.astype(low), (0, 0))
 
     attended_grad = dot(out_grad, turned, (1, 0)).astype(low)
-    head_grad = heads_in(attended_grad, 8)
-    dq, dk, dv = attend_back(head_queries, head_keys, head_values, probs, head_grad, exact)
-    by_block = (4, 2, 4, local_tokens, HD)
-    query_grads, key_grads, value_in = collect_heads(
-        dq, dk.reshape(by_block), dv.reshape(by_block), 9
-    )
-    query_in, key_in = turn_back(query_grads, key_grads, cosine, sine)
-    normed_part = (
-        dot(query_in, full_query, (1, 1))
-        + dot(key_in, full_key, (1, 1))
-        + dot(value_in, full_value, (1, 1))
-    ).astype(low)
-    gain_one_part = jnp.sum(normed_part.astype(jnp.float32) * unit_one, axis=0)
-    small_grads = jnp.concatenate(
-        [0.25 * router_grad, gain_one_part[:, None], 0.25 * gain_two_grad[:, None]], axis=1
-    )
-    small_grads = jnp.pad(small_grads, ((0, 0), (0, HD - small_grads.shape[1])))
-
     def by_shard(x):
         return x.astype(low).reshape(4, 2, 4, x.shape[0] // 32, x.shape[1])
 
-    attention_grads = [
-        by_shard(dot(left, right, (0, 0)))
-        for left, right in (
-            (normed, query_in),
-            (normed, key_in),
-            (normed, value_in),
-            (out_grad, attended),
-        )
-    ]
-    parts = whole_parts(attention_grads)
-    attention_grads.append(by_shard(small_grads))
-    for part, (_, rows, columns) in zip(parts, sum(row_parts(attention_grads[4:]), [])):
-        part.append((4, rows, columns))
-    query_share, key_share, value_share, output_share, small_share, normed_sum = reduce_and_sum(
-        attention_grads, parts, normed_part, 12
-    )
-    normed_grad = normed_sum.astype(jnp.float32)
-    scaled_one = normed_grad * gain_one
+    small_grads = jnp.concatenate([router_grad, gain_two_grad[:, None]], axis=1)
+    small_grads = jnp.pad(small_grads, ((0, 0), (0, HD - small_grads.shape[1])))
+    summed = [by_shard(dot(out_grad, attended, (0, 0))), by_shard(small_grads)]
+    scaled_one, head_shares, gain_terms, output_share, small_share = attention_back(
+        (
+            attended_grad,
+            head_queries,
+            head_keys,
+            head_values,
+            probs,
+            exact,
+            cosine,
+            sine,
+            head_rows,
+            head_weights,
+            heads,
+        ),
+        summed,
+        9,
+    )
+    scaled_one = scaled_one.astype(jnp.float32)
     tokens_grad = (
         hidden_grad
         + inv_one
         * (scaled_one - unit_one * jnp.mean(scaled_one * unit_one, axis=-1, keepdims=True))
     ).astype(low)
+    head_shares = head_shares.astype(jnp.float32) * gain_one
+    query_share, key_share, value_share = (
+        head_shares[..., k * HD : (k + 1) * HD].swapaxes(0, 1).reshape(-1, head_cols)
+        for k in range(3)
+    )
     return (
         block_out,
         tokens_grad,
-        small_share[:, experts_all],
+        jnp.sum(gain_terms, axis=1),
         query_share,
         key_share,
         value_share,
         output_share.T,
-        small_share[:, experts_all + 1],
+        small_share[:, experts_all],
         small_share[:, :experts_all],
         gate_share,
         up_share,

time: 554 us -> 484 us (0.87)
  Pallas kernels: 457 us -> 417 us
  matrix products: 33.1 us -> 18.4 us
  waiting for transfers between devices: 13.3 us -> 0.02 us
    pallas_call x2 -> x0, Pallas kernels: 82.1 us -> none  [the longest x1 69.3 us: gather_cube(): pl.pallas_call(functools.partial(gather_kernel, parts, count), out_shape=...]
    pallas_call x10 -> x5, Pallas kernels: 198 us -> 241 us  [vmem_call(): pl.pallas_call(kernel, out_shape=out_shape, in_specs=[pl.BlockSpec(memory...]
    dot_general x23 -> x16, matrix products: 33.1 us -> 18.4 us  [dot(): lax.dot_general(left, right, ((over[:1], over[1:]), ((), ())), preferred_...]
    all_gather x1, waiting for transfers between devices: 13.2 us -> 0.01 us  [shards(): lax.all_gather(beside((shared_gate, shared_up, shared_down.T)), groups, a...]
  transfers between devices with their start and end apart: 1 -> 1, of which waited for: 1 -> 0; matrix products, arithmetic and copies ran while one was open for 1% -> 4% of each run, Pallas kernels for 24% -> 26%
where the time goes in v4:
time: 484 us; the launch traced here: 480 us
  Pallas kernels  417 us (86%)
  matrix products  18.4 us (4%)
  other arithmetic  17.8 us (4%)
  between operations  14.7 us (3%)
  local copies, waits for them, and re-layouts  12.3 us (3%)
    pallas_call x5, Pallas kernels, vmem_call(): pl.pallas_call(kernel, out_shape=out_shape, in_specs=[pl.BlockSpec(memory...  241 us
    pallas_call x1, Pallas kernels, run_experts(): pl.pallas_call(functools.partial(expert_kernel, parts, len(summed)), out_...  101 us
    pallas_call x1, Pallas kernels, dispatch(): pl.pallas_call(functools.partial(dispatch_kernel, first), out_shape=[rows...  64.7 us
    dot_general x16, matrix products, dot(): lax.dot_general(left, right, ((over[:1], over[1:]), ((), ())), preferred_...  18.4 us
    pallas_call x1, Pallas kernels, expert_grads(): pl.pallas_call(expert_grads_kernel, grid=(2,), out_shape=[shape] * 3, in_...  10.9 us
  transfers between devices with their start and end apart: 1, of which 0 were waited for; matrix products, arithmetic and copies ran while one was open for 4% of the time, Pallas kernels for 26%

profile of v4, /device:TPU:1, one launch (start us, length us, event | category | flops | bytes accessed | tf_op | source)
XLA Modules:
  0.0 480.4 jit_solution(18007106297408349629)
XLA Ops:
  7.2 0.0 all-gather.2.cloned.1.call-start
  7.2 1.8 fusion.26
  9.1 0.7 convert_element_type.130
  9.7 0.8 copy.35
  10.5 0.8 constant_dynamic-update-slice_fusion.2
  11.3 0.8 constant_dynamic-update-slice_fusion.1
  12.2 0.8 constant_dynamic-update-slice_fusion.refs_10_
  13.0 1.3 fusion.16
  14.3 0.8 multiply_convert_fusion.1.w
  15.1 0.9 fusion.4.x
  16.1 44.3 %gather_head.1 = (bf16[4,128,2048]{2,1,0:T(8,128)(2,1)}, bf16[4,2,4,64,384]{4,3,2,1,0:T(8,128)(2,1)}) custom-call(bf16[128,2048]{1,0:T(8,128)(2,1)} %fusion.4.x, bf16[64,1536]{1,0:T(8,128)(2,1)} %multiply_convert_fusion.1.w), custom_call_target="tpu_custom_call" | custom-call | tf_op jit(solution)/shard_map/gather_head/pallas_call | solution.py:123
  60.4 0.1 convert_bitcast_fusion
  60.5 1.0 fusion.39
  61.5 1.0 pad_maximum_fusion.1
  62.5 4.2 project_head.1
  66.7 0.1 fusion.65
  66.8 0.6 pad_maximum_fusion.3.own
  67.4 75.3 %attention.1 = (bf16[128,2048]{1,0:T(8,128)(2,1)}, bf16[128,512]{1,0:T(8,128)(2,1)}, bf16[4,2,4,128,128]{4,3,2,1,0:T(8,128)(2,1)}, bf16[4,2,4,128,128]{4,3,2,1,0...) custom-call(bf16[4,128,128]{2,1,0:T(8,128)(2,1)} %bitcast.93, ...), custom_call_target="tpu_custom_call" | custom-call | tf_op jit(solution)/shard_map/attention/pallas_call | solution.py:123
  142.8 1.3 slice_convert_fusion
  144.1 0.3 copy.49
  144.4 0.3 multiply_reduce_fusion.2
  144.7 0.2 multiply_convert_fusion.refs_2_
  145.0 1.6 fusion.85
  146.6 0.1 copy.37
  146.7 0.2 fusion.48
  146.9 0.5 convolution_compare_fusion
  147.4 1.5 convolution_convert_fusion.2
  148.9 0.3 fusion.6
  149.2 0.3 fusion.5
  149.5 0.5 fusion.37
  149.9 1.4 add_convert_fusion
  151.4 64.7 %dispatch_rows.1 = (bf16[2,512,2048]{2,1,0:T(8,128)(2,1)}, bf16[2,512,2048]{2,1,0:T(8,128)(2,1)}, bf16[128,2048]{1,0:T(8,128)(2,1)}, bf16[128,2048]{1,0:T(8,128)...) custom-call(bf16[32,2,16,512]{3,2,1,0:T(8,128)(2,1)} %bitcast.80, ...), custom_call_target="tpu_custom_call" | custom-call | tf_op jit(solution)/shard_map/dispatch_rows/pallas_call | solution.py:1051
  216.1 100.8 %run_experts.1 = (bf16[32,2,16,512]{3,2,1,0:T(8,128)(2,1)}, bf16[32,2,16,512]{3,2,1,0:T(8,128)(2,1)}, f32[64,704]{1,0:T(8,128)}, f32[64,704]{1,0:T(8,128)}, f32[...) custom-call(bf16[2,512,2048]{2,1,0:T(8,128)(2,1)} %get-tuple-element., ...), custom_call_target="tpu_custom_call" | custom-call | tf_op jit(solution)/shard_map/run_experts/pallas_call | solution.py:1209
  316.9 1.7 fusion.86
  318.6 1.7 convolution_select_fusion
  320.4 1.0 fusion.10.refs_2_
  321.3 0.4 fusion.29
  321.8 1.0 convolution_convert_fusion.3.refs_3_
  322.7 0.6 pad.27.refs_4_
  323.4 27.8 %sum_mlp.1 = (bf16[128,2048]{1,0:T(8,128)(2,1)}, bf16[128,2048]{1,0:T(8,128)(2,1)}, f32[128,128]{1,0:T(8,128)}) custom-call(bf16[128,2048]{1,0:T(8,128)(2,1)} %get-tuple-element.60.refs_0_, bf16[128,2048]{1,0:T(8,128)(2,1)} %get-tuple-element.61.refs_1_, bf16[128,512]{1,0:T(8,128)(2,1)} %fusion.10.refs_2_, ...), custom_call_target="tpu_custom_call" | custom-call | tf_op jit(solution)/shard_map/sum_mlp/pallas_call | solution.py:123
  351.2 1.1 multiply_reduce_fusion.3
  352.3 1.2 convolution_convert_fusion.1
  353.5 2.3 multiply_reduce_fusion
  355.8 1.3 multiply_add_fusion
  357.1 0.6 copy-done.7
  357.7 1.1 fusion.7.refs_0_
  358.9 0.3 copy.45
  359.2 2.1 convolution_convert_fusion
  361.2 0.9 pad.28.clone
  362.1 89.1 %attention_back.1 = (bf16[128,2048]{1,0:T(8,128)(2,1)}, bf16[4,64,384]{2,1,0:T(8,128)(2,1)}, f32[64,128]{1,0:T(8,128)}, f32[64,512]{1,0:T(8,128)}, f32[64,128]{1,0:T(8,128)}) custom-call(bf16[128,512]{1,0:T(8,128)(2,1)} %fusion.7.refs_0_, bf16[4,128,128]{2,1,0:T(8,128)(2,1)} %bitcast.94, bf16[4,2,4,128,128]{4,3,2,1,0:T(8,128)(2,1)} %get-tuple-element.72.refs_2_, ...), custom_call_target="tpu_custom_call" | custom-call | tf_op jit(solution)/shard_map/attention_back/pallas_call | solution.py:123
  451.2 1.4 reduce_sum.79
  452.6 1.4 fusion.15
  454.0 2.2 fusion.14
  456.2 0.7 slice_reduce_fusion
  456.9 0.1 convert_multiply_fusion.2
  457.1 0.7 copy.53
  457.7 0.7 copy.54
  458.4 0.7 copy.55
  459.1 10.9 %expert_grads.1 = (f32[2,352,2048]{2,1,0:T(8,128)}, f32[2,352,2048]{2,1,0:T(8,128)}, f32[2,352,2048]{2,1,0:T(8,128)}) custom-call(bf16[2,512,2048]{2,1,0:T(8,128)(2,1)} %get-tuple-element.62.refs_0_.rows, bf16[2,512,2048]{2,1,0:T(8,128)(2,1)} %get-tuple-element.63.refs_1_.grads, bf16[2,512,352]{2,1,0:T(8,128)(2,1)} %get-tuple-element.85.act, ...), custom_call_target="tpu_custom_call" | custom-call | tf_op jit(solution)/shard_map/expert_grads/pallas_call | solution.py:1295
  470.0 0.7 copy.69
  470.6 0.6 copy.70
  471.3 0.7 copy.71
  471.9 0.7 copy.72
  472.6 0.7 copy.73
  (54 shorter events, 0.2 us)
Async XLA Ops:
  7.2 7.9 %copy-start = (bf16[128,2048]{1,0:T(8,128)(2,1)S(1)}, bf16[128,2048]{1,0:T(8,128)(2,1)}, u32[]{:S(2)}) copy-start(bf16[128,2048]{1,0:T(8,128)(2,1)} %param.16) | copy-start | bytes 1572868
  7.2 144.2 %all-gather.2.cloned.1.call-start = ((), (), s32[]{:S(2)}) async-start(), calls=%async_computation | async-start | bytes 9732096 | tf_op jit(solution)/shard_map/all_gather | solution.py:1361
  13.0 53.7 %copy-start.8 = (bf16[64,1536]{1,0:T(8,128)(2,1)}, bf16[64,1536]{1,0:T(8,128)(2,1)S(1)}, u32[]{:S(2)}) copy-start(bf16[64,1536]{1,0:T(8,128)(2,1)S(1)} %constant_dynamic-update-slice_fusion.refs_10_) | copy-start | bytes 589828
  61.5 5.3 %copy-start.19 = (bf16[64,64]{1,0:T(8,128)(2,1)S(1)}, bf16[64,64]{1,0:T(8,128)(2,1)}, u32[]{:S(2)}) copy-start(bf16[64,64]{1,0:T(8,128)(2,1)} %param.25) | copy-start | bytes 24580
  61.5 5.3 %copy-start.18 = (bf16[512,64]{0,1:T(8,128)(2,1)S(1)}, bf16[512,64]{0,1:T(8,128)(2,1)}, u32[]{:S(2)}) copy-start(bf16[512,64]{0,1:T(8,128)(2,1)} %param.23) | copy-start | bytes 196612
  142.8 1.7 copy-start.4
  144.1 2.8 copy-start.20
  145.0 4.5 copy-start.1
  145.0 4.5 copy-start.5
  216.1 102.5 %copy-start.6 = (bf16[128,2048]{1,0:T(8,128)(2,1)S(1)}, bf16[128,2048]{1,0:T(8,128)(2,1)}, u32[]{:S(2)}) copy-start(bf16[128,2048]{1,0:T(8,128)(2,1)} %refs_3_.1) | copy-start | bytes 1572868
  316.9 3.4 copy-start.3
  316.9 4.8 %copy-start.9 = (bf16[32,2,16,512]{3,2,1,0:T(8,128)(2,1)S(1)}, bf16[32,2,16,512]{3,2,1,0:T(8,128)(2,1)}, u32[]{:S(2)}) copy-start(bf16[32,2,16,512]{3,2,1,0:T(8,128)(2,1)} %get-tuple-element.68) | copy-start | bytes 3145732
  320.4 31.9 %copy-start.2 = (bf16[128,2048]{1,0:T(8,128)(2,1)S(1)}, bf16[128,2048]{1,0:T(8,128)(2,1)}, u32[]{:S(2)}) copy-start(bf16[128,2048]{1,0:T(8,128)(2,1)} %copy-done.1) | copy-start | bytes 1572868
  351.2 4.6 copy-start.10
  355.8 1.9 copy-start.7
  357.1 2.0 copy-start.15
  451.2 5.0 %copy-start.17 = (f32[64,128]{1,0:T(8,128)S(1)}, f32[64,128]{1,0:T(8,128)}, u32[]{:S(2)}) copy-start(f32[64,128]{1,0:T(8,128)} %get-tuple-element.81) | copy-start | bytes 98308
  451.2 5.7 %copy-start.14 = (bf16[4,64,384]{2,1,0:T(8,128)(2,1)S(1)}, bf16[4,64,384]{2,1,0:T(8,128)(2,1)}, u32[]{:S(2)}) copy-start(bf16[4,64,384]{2,1,0:T(8,128)(2,1)} %get-tuple-element.79) | copy-start | bytes 589828
  459.1 10.9 %copy-start.16 = (f32[64,512]{1,0:T(8,128)S(1)}, f32[64,512]{1,0:T(8,128)}, u32[]{:S(2)}) copy-start(f32[64,512]{1,0:T(8,128)} %get-tuple-element.80) | copy-start | bytes 393220
  459.1 12.2 %copy-start.13 = (f32[64,704]{1,0:T(8,128)S(1)}, f32[64,704]{1,0:T(8,128)}, u32[]{:S(2)}) copy-start(f32[64,704]{1,0:T(8,128)} %get-tuple-element.138) | copy-start | bytes 540676
  459.1 12.9 %copy-start.12 = (f32[64,704]{1,0:T(8,128)S(1)}, f32[64,704]{1,0:T(8,128)}, u32[]{:S(2)}) copy-start(f32[64,704]{1,0:T(8,128)} %get-tuple-element.139) | copy-start | bytes 540676
  459.1 13.6 %copy-start.11 = (f32[64,704]{1,0:T(8,128)S(1)}, f32[64,704]{1,0:T(8,128)}, u32[]{:S(2)}) copy-start(f32[64,704]{1,0:T(8,128)} %get-tuple-element.84) | copy-start | bytes 540676
Sparse Core Ops, SparseCore 0:
  11.6 120.4 all-gather.1

commit v5 on v4

--- a/solution.py
+++ b/solution.py
@@ -19,7 +19,7 @@
 
 
 MESH = pl.DeviceIdType.MESH
-VMEM_LIMIT = 60 * 1024 * 1024
+VMEM_LIMIT = 63 * 1024 * 1024
 
 ORDERS = (
     (("z", "A"), ("z", "B"), ("y", "A"), ("y", "B")),
@@ -785,7 +785,7 @@
         yield True
 
 
-BACK_ORDER = "RRAAAAA" + "CRRCCRRCCRRRRCRRCC"
+BACK_ORDER = "AAAAACCCCCCC"
 
 
 def attention_back_kernel(parts, count, *refs):
@@ -894,6 +894,8 @@
 SLOTS = 16
 GROUP_ORDER = ((0, 1), (1, 0), (3, 0), (1, 1), (3, 1), (2, 0), (2, 1), (0, 0))
 SENT_AHEAD = 4
+PASSED_BEHIND = 2
+FIRST_COMPLETE = 11
 
 
 def token_places():
@@ -945,6 +947,11 @@
         copy.start()
     items = [(a, dz, dx) for a in range(count) for dz, dx in GROUP_ORDER]
     passed, last = {}, []
+    firsts = len(GROUP_ORDER)
+
+    def forward(part, i):
+        copy = copies.start(part, part, beside)
+        last.append((i // firsts, copy))
 
     def send(i):
         a, dz, dx = items[i]
@@ -973,31 +980,37 @@
             own[a].wait()
         part = outs[a].at[:, rows_of(dz, dx), quarter_columns((place + dx) % 2, core)]
         passed[i] = copies.start(part, part, across)
-        last.append(copies.start(part, part, beside))
+        forward(part, i)
 
     def from_across(i):
         a, dz, dx = items[i]
         passed[i].wait_recv()
         part = outs[a].at[:, rows_of(dz, dx), quarter_columns((place + dx + 1) % 2, core)]
-        last.append(copies.start(part, part, beside))
+        forward(part, i)
 
     for i in range(SENT_AHEAD):
         send(i)
     yield True
-    for i in range(len(items) + 2):
+    for i in range(len(items) + PASSED_BEHIND):
         if i < len(items):
             arrived(i)
             if i + SENT_AHEAD < len(items):
                 send(i + SENT_AHEAD)
-        if i >= 2:
-            from_across(i - 2)
+        if i >= PASSED_BEHIND:
+            from_across(i - PASSED_BEHIND)
+        if i == FIRST_COMPLETE:
+            for a, copy in last:
+                if a == 0:
+                    copy.wait_recv()
         yield True
-    for copy in last:
-        copy.wait_recv()
+    for a, copy in last:
+        if a > 0:
+            copy.wait_recv()
     copies.finish()
     for a in range(count):
         sample = ins[a].at[pl.ds(0, 31)]
         pltpu.make_async_copy(sample, sample, out_sem.at[a]).wait()
+    yield True
 
 
 def shared_step(width):
@@ -1009,7 +1022,7 @@
     width = gate_grad.shape[1]
     step = shared_step(width)
     gate, up, down = (slice(k * step, k * step + width) for k in range(3))
-    load = pltpu.make_async_copy(whole.at[:, pl.ds(first, weights.shape[1])], weights, sem)
+    load = pltpu.make_async_copy(whole.at[:, pl.ds(first, weights.shape[1])], weights, sem.at[0])
     load.start()
     yield True
     load.wait()
@@ -1033,75 +1046,50 @@
         yield True
 
 
-def dispatch_kernel(first, *refs):
-    ins, (x, g, whole), outs = refs[:2], refs[2:5], refs[5:7]
-    results, weights, load_sem = refs[7:12], refs[12], refs[13]
-    out_sem, in_sem, own_sem, *sems = refs[14:]
-    greet_blocks([])
-    moving = dispatch_steps(ins, outs, out_sem, in_sem, own_sem, Copies(*sems))
-    computing = shared_steps(x, g, weights, whole, first, *results, load_sem)
-    run(moving, computing)
-
-
-def dispatch(arrays, x, g, whole, first, width, collective_id):
-    low = x.dtype
-    rows = jax.ShapeDtypeStruct((2, 32 * SLOTS, D), low)
-    grad = jax.ShapeDtypeStruct((D, width), low)
-    anywhere, vmem = pl.BlockSpec(memory_space=pl.ANY), pl.BlockSpec(memory_space=pltpu.VMEM)
-    return pl.pallas_call(
-        functools.partial(dispatch_kernel, first),
-        out_shape=[rows] * 2 + [jax.ShapeDtypeStruct(x.shape, low)] * 2 + [grad] * 3,
-        in_specs=[anywhere] * 2 + [vmem] * 2 + [anywhere],
-        out_specs=[anywhere] * 2 + [vmem] * 5,
-        scratch_shapes=[
-            pltpu.VMEM((D, 3 * shared_step(width)), low),
-            pltpu.SemaphoreType.DMA,
-            pltpu.SemaphoreType.DMA((2,)),
-            pltpu.SemaphoreType.DMA((2, 8)),
-            pltpu.SemaphoreType.DMA((2,)),
-            pltpu.SemaphoreType.DMA((48,)),
-            pltpu.SemaphoreType.DMA((48,)),
-        ],
-        compiler_params=pltpu.CompilerParams(
-            collective_id=collective_id, has_side_effects=True, vmem_limit_bytes=VMEM_LIMIT
-        ),
-        name="dispatch_rows",
-    )(*arrays, x, g, whole)
-
-
-def expert_steps(hbm, held, part, back, kept, load_sem, finished):
-    low = part.dtype
+def expert_steps(rows, grads, hbm, held, part, back, kept, load_sem, finished):
+    low = rows.dtype
+    hidden = hbm[0].shape[1]
     loads = [
-        [pltpu.make_async_copy(src.at[e], dst.at[e], load_sem.at[e, k]) for k, (src, dst) in enumerate(zip(hbm, held))]
-        for e in range(2)
+        pltpu.make_async_copy(src, dst, load_sem.at[k]) for k, (src, dst) in enumerate(zip(hbm, held))
     ]
-    for load in loads[0] + loads[1]:
+    for load in loads:
         load.start()
     yield True
-    rows, grads, gate, up, down = held
+    for load in loads:
+        load.wait()
+    gate, up, down = held
+    chunks = [slice(at, at + 512) for at in range(0, D, 512)]
+    found = []
     for e in range(2):
-        for load in loads[e]:
-            load.wait()
-        x, g = rows[e], grads[e]
-        pre = over(x, gate[e], (1, 1))
-        lin = over(x, up[e], (1, 1))
+        pre = over(rows[e], gate[e], (1, 1))
         yield True
-        act, pre_grad, lin_grad = swish_parts(pre, lin, over(g, down[e], (1, 1)))
-        act, pre_grad, lin_grad = act.astype(low), pre_grad.astype(low), lin_grad.astype(low)
-        kept[0][e], kept[1][e], kept[2][e] = act, pre_grad, lin_grad
+        lin = over(rows[e], up[e], (1, 1))
+        found.append((pre, lin))
+        act = (pre * jax.nn.sigmoid(pre) * lin).astype(low)
+        kept[0][e] = act
         yield True
-        for at in range(0, D, 512):
-            here = slice(at, at + 512)
-            part[e, :, here] = over(act, down[e, :, here], (1, 0)).astype(low)
-            back[e, :, here] = (
+        for here in chunks:
+            ref, place = part(e, here)
+            ref[place] = over(act, down[e, :, here], (1, 0)).astype(low)
+            if here is chunks[-1]:
+                finished(e, 0)
+            yield True
+    for e in range(2):
+        _, pre_grad, lin_grad = swish_parts(*found[e], over(grads[e], down[e], (1, 1)))
+        pre_grad, lin_grad = pre_grad.astype(low), lin_grad.astype(low)
+        kept[1][e], kept[2][e] = pre_grad, lin_grad
+        yield True
+        for here in chunks:
+            ref, place = back(e, here)
+            ref[place] = (
                 over(pre_grad, gate[e, :, here], (1, 0)) + over(lin_grad, up[e, :, here], (1, 0))
             ).astype(low)
-            if at + 512 == D:
-                finished(e)
+            if here is chunks[-1]:
+                finished(e, 1)
             yield True
 
 
-def return_steps(ins, outs, halves, quarters, out_sem, in_sem, copies):
+def return_steps(held, outs, halves, quarters, out_sem, in_sem, copies):
     z, xh, y, place, core = token_places()
     beside, across = wa_places()
     me = z * 8 + xh * 4 + y
@@ -1109,12 +1097,13 @@
     group = 4 * SLOTS
     mine = pl.ds(pl.multiple_of(core * 2 * quarter, 2 * quarter), 2 * quarter)
     theirs = pl.ds(pl.multiple_of((1 - core) * 2 * quarter, 2 * quarter), 2 * quarter)
-    items = [(e, a, dz, dx) for e in range(2) for a in range(2) for dz, dx in GROUP_ORDER]
+    rows_each = halves[0].shape[1]
+    items = [(e, a, dz, dx) for a in range(2) for e in range(2) for dz, dx in GROUP_ORDER]
     paired_up, passed = {}, {}
 
-    def finished(e):
-        for a in range(2):
-            paired_up[e, a] = copies.start(ins[a].at[e, :, theirs], halves[a].at[e], beside)
+    def finished(e, a):
+        rows = pl.ds((2 * a + e) * rows_each, rows_each)
+        paired_up[e, a] = copies.start(held.at[rows, theirs], halves[a].at[e], beside)
 
     def rows_of(dz, dx):
         return pl.ds(pl.multiple_of(((z + dz) % 4 * 8 + (xh + dx) % 2 * 4) * SLOTS, group), group)
@@ -1130,7 +1119,9 @@
         rows = rows_of(dz, dx)
         if i % 8 == 0:
             paired_up[e, a].wait_recv()
-        halves[a][e, rows] = halves[a][e, rows] + ins[a][e, rows, mine]
+        first = (2 * a + e) * rows_each
+        ours = held[pl.ds(pl.multiple_of(first + rows.start, group), group), mine]
+        halves[a][e, rows] = halves[a][e, rows] + ours
         passed[i] = copies.start(
             halves[a].at[e, rows, given(dx)], quarters[a].at[e, rows], across
         )
@@ -1156,11 +1147,11 @@
         lax.fori_loop(1 if dz + dx == 0 else 0, 4, one, 0)
 
     def steps():
-        for i in range(len(items) + 1):
+        for i in range(len(items) + BEHIND):
             if i < len(items):
                 add_core(i)
-            if i >= 1:
-                add_across(i - 1)
+            if i >= BEHIND:
+                add_across(i - BEHIND)
             yield True
         copies.finish()
         for a in range(2):
@@ -1171,52 +1162,87 @@
     return finished, steps()
 
 
-EXPERT_ORDER = "RRXXXXXXX" + "TXTTXTTXTTXTTXTTXTTXT" + "TTTRTTTRTTRTTRTTRTTRTTRT"
-
-
-def expert_kernel(parts, count, *refs):
-    hbm, summed, refs = refs[:5], refs[5 : 5 + count], refs[5 + count :]
-    outs, shares, kept, refs = refs[:2], refs[2 : 2 + count], refs[2 + count : 5 + count], refs[5 + count :]
-    held, (part, back), halves, quarters = refs[:5], refs[5:7], refs[7:9], refs[9:11]
-    load_sem, out_sem, in_sem, send_sem, recv_sem = refs[11:16]
-    bufs, more = refs[16:-2], refs[-2:]
+BEHIND = 12
+MLP_ORDER = (
+    "XD" + "SD" * 12 + "RR" + "XD" * 6 + "XTXTXTXTXTXTD"
+    + "XTXTXTTXTXT" + "XTTXTTXRTTXRTTXRTT" + "TTRTTRTTRTTRTTRTTTTRR"
+)
+
+
+def mlp_kernel(count, *refs):
+    ins, (x, g, whole), hbm, refs = refs[:2], refs[2:5], refs[5:8], refs[8:]
+    arrived, back_rows, (shared_part, shared_back), refs = refs[:2], refs[2:4], refs[4:6], refs[6:]
+    shares, kept, refs = refs[:count], refs[count : count + 3], refs[count + 3 :]
+    weights, shared_grads, refs = refs[0], refs[1 : 1 + count], refs[1 + count :]
+    held, halves, quarters, refs = refs[:3], refs[3:5], refs[5:7], refs[7:]
+    shared_sem, load_sem, out_sem, in_sem, own_sem, *refs = refs
+    pass_sems, back_out_sem, back_in_sem, back_sems, refs = refs[:2], refs[2], refs[3], refs[4:6], refs[6:]
+    bufs, cube_sems = refs[:-2], refs[-2:]
     greet_blocks([neighbour("x", "A")])
+    rows = arrived[0].shape[1]
+    results = weights.at[:, pl.ds(0, D)]
+
+    def place_of(a):
+        def place(e, here):
+            first = (2 * a + e) * rows
+            return weights, (slice(first, first + rows), here)
+
+        return place
+
     finished, returning = return_steps(
-        (part, back), outs, halves, quarters, out_sem, in_sem, Copies(send_sem, recv_sem)
-    )
-    computing = expert_steps(hbm, held, part, back, kept, load_sem, finished)
-    reducing = reduce_steps(parts, summed, shares, bufs, Copies(*more))
-    for turn in EXPERT_ORDER:
-        next({"R": reducing, "X": computing, "T": returning}[turn], None)
-    run(returning, reducing)
-
-
-def run_experts(operands, summed, collective_id):
-    rows = 32 * SLOTS
-    low = operands[0].dtype
-    hidden = operands[2].shape[1]
-    parts = row_parts(summed)
-    out_shape = [jax.ShapeDtypeStruct((32, 2, SLOTS, D // 4), low)] * 2
-    out_shape += [jax.ShapeDtypeStruct(x.shape[3:], jnp.float32) for x in summed]
+        results, back_rows, halves, quarters, back_out_sem, back_in_sem, Copies(*back_sems)
+    )
+    shards = [grad.shape[0] // 32 for grad in shared_grads]
+    cubes = [
+        grad.reshape(4, 2, 4, shard, grad.shape[1]) for grad, shard in zip(shared_grads, shards)
+    ]
+    parts = row_parts(cubes)
+    programs = {
+        "D": dispatch_steps(ins, arrived, out_sem, in_sem, own_sem, Copies(*pass_sems)),
+        "S": shared_steps(
+            x, g, weights, whole, 0, shared_part, shared_back, *shared_grads, shared_sem
+        ),
+        "X": expert_steps(
+            *arrived, hbm, held, place_of(0), place_of(1), kept, load_sem, finished
+        ),
+        "T": returning,
+        "R": reduce_steps(parts, cubes, shares, bufs, Copies(*cube_sems)),
+    }
+    in_turn(MLP_ORDER, programs)
+    run(programs["T"], programs["R"])
+
+
+def mlp(arrays, x, g, whole, width, expert_weights, collective_id):
+    low = x.dtype
+    rows, count = 32 * SLOTS, 3
+    hidden = expert_weights[0].shape[1]
+    at_experts = jax.ShapeDtypeStruct((2, rows, D), low)
+    grad = jax.ShapeDtypeStruct((D, width), low)
+    cube = jax.ShapeDtypeStruct((4, 2, 4, D // 32, width), low)
+    out_shape = [at_experts] * 2
+    out_shape += [jax.ShapeDtypeStruct((32, 2, SLOTS, D // 4), low)] * 2
+    out_shape += [jax.ShapeDtypeStruct(x.shape, low)] * 2
+    out_shape += [jax.ShapeDtypeStruct((D // 32, width), jnp.float32)] * count
     out_shape += [jax.ShapeDtypeStruct((2, rows, hidden), low)] * 3
-    scratch = [pltpu.VMEM(x.shape, low) for x in operands]
-    scratch += [pltpu.VMEM((2, rows, D), low)] * 2
+    scratch = [pltpu.VMEM((D, 3 * shared_step(width)), low)]
+    scratch += [pltpu.VMEM(grad.shape, low)] * count
+    scratch += [pltpu.VMEM(a.shape, low) for a in expert_weights]
     scratch += [pltpu.VMEM((2, rows, D // 2), low)] * 2 + [pltpu.VMEM((2, rows, D // 4), low)] * 2
-    scratch += [pltpu.SemaphoreType.DMA((2, 5))] + [pltpu.SemaphoreType.DMA((2,))] * 2
-    scratch += [pltpu.SemaphoreType.DMA((36,))] * 2
-    scratch += reduce_scratch(summed, parts)
+    sems = [(1,), (3,), (2,), (2, 8), (2,), (48,), (48,), (2,), (2,), (36,), (36,)]
+    scratch += [pltpu.SemaphoreType.DMA(n) for n in sems]
+    scratch += reduce_scratch([cube] * count, row_parts([cube] * count))
     anywhere, vmem = pl.BlockSpec(memory_space=pl.ANY), pl.BlockSpec(memory_space=pltpu.VMEM)
     return pl.pallas_call(
-        functools.partial(expert_kernel, parts, len(summed)),
+        functools.partial(mlp_kernel, count),
         out_shape=out_shape,
-        in_specs=[anywhere] * 5 + [vmem] * len(summed),
+        in_specs=[anywhere] * 2 + [vmem] * 2 + [anywhere] * 4,
         out_specs=[vmem] * len(out_shape),
         scratch_shapes=scratch,
         compiler_params=pltpu.CompilerParams(
             collective_id=collective_id, has_side_effects=True, vmem_limit_bytes=VMEM_LIMIT
         ),
-        name="run_experts",
-    )(*operands, *summed)
+        name="mlp",
+    )(*arrays, x, g, whole, *expert_weights)
 
 
 def sum_more_kernel(parts, *refs):
@@ -1415,27 +1441,26 @@
         dot(gate_high, grad_quarter, (0, 0)) + dot(gate_rest, grad_quarter, (0, 0))
     ).astype(low)
     by_owner = (32, 2, SLOTS, D // 4)
-    rows_in, grads_in, shared_part, shared_in_part, *mlp_grads = dispatch(
+    expert_weights = (expert_gate.transpose(0, 2, 1), expert_up.transpose(0, 2, 1), expert_down)
+    (
+        rows_in,
+        grads_in,
+        returned,
+        rows_back,
+        shared_part,
+        shared_in_part,
+        gate_share,
+        up_share,
+        down_share,
+        *kept,
+    ) = mlp(
         (send_rows.reshape(by_owner), send_grads.reshape(by_owner)),
         mlp_in,
         cotangent,
         shared_whole,
-        0,
         hidden_cols,
+        expert_weights,
         5,
-    )
-    mlp_grads = [x.reshape(4, 2, 4, x.shape[0] // 32, x.shape[1]) for x in mlp_grads]
-
-    returned, rows_back, gate_share, up_share, down_share, *kept = run_experts(
-        (
-            rows_in,
-            grads_in,
-            expert_gate.transpose(0, 2, 1),
-            expert_up.transpose(0, 2, 1),
-            expert_down,
-        ),
-        mlp_grads,
-        6,
     )
     gate_grad_turned, up_grad_turned, expert_down_grad = expert_grads(rows_in, grads_in, *kept)
     returned, rows_back = returned.reshape(-1, D // 4), rows_back.reshape(-1, D // 4)

time: 484 us -> 443 us (0.915)
  Pallas kernels: 417 us -> 375 us
    pallas_call x2 -> x1, Pallas kernels: 166 us -> 135 us  [mlp(): pl.pallas_call(functools.partial(mlp_kernel, count), out_shape=out_shape,...]
    pallas_call x5, Pallas kernels: 241 us -> 229 us  [vmem_call(): pl.pallas_call(kernel, out_shape=out_shape, in_specs=[pl.BlockSpec(memory...]
  transfers between devices with their start and end apart: 1 -> 1, of which waited for: 0 -> 0; matrix products, arithmetic and copies ran while one was open for 4% -> 4% of each run, Pallas kernels for 26% -> 28%
where the time goes in v5:
time: 443 us; the launch traced here: 439 us
  Pallas kernels  375 us (85%)
  matrix products  18.9 us (4%)
  other arithmetic  18.1 us (4%)
  between operations  14.8 us (3%)
  local copies, waits for them, and re-layouts  12.3 us (3%)
    pallas_call x5, Pallas kernels, vmem_call(): pl.pallas_call(kernel, out_shape=out_shape, in_specs=[pl.BlockSpec(memory...  229 us
    pallas_call x1, Pallas kernels, mlp(): pl.pallas_call(functools.partial(mlp_kernel, count), out_shape=out_shape,...  135 us
    dot_general x16, matrix products, dot(): lax.dot_general(left, right, ((over[:1], over[1:]), ((), ())), preferred_...  18.9 us
    pallas_call x1, Pallas kernels, expert_grads(): pl.pallas_call(expert_grads_kernel, grid=(2,), out_shape=[shape] * 3, in_...  10.9 us
  transfers between devices with their start and end apart: 1, of which 0 were waited for; matrix products, arithmetic and copies ran while one was open for 4% of the time, Pallas kernels for 28%

profile of v5, /device:TPU:1, one launch (start us, length us, event | category | flops | bytes accessed | tf_op | source)
XLA Modules:
  0.0 439.3 jit_solution(8533359802640869667)
XLA Ops:
  7.2 0.0 all-gather.2.cloned.1.call-start
  7.2 1.8 fusion.26
  9.0 0.0 all-gather.2.cloned.1.call-update
  9.1 0.7 convert_element_type.130
  9.7 0.8 copy.35
  10.5 0.8 constant_dynamic-update-slice_fusion.2
  11.3 0.8 constant_dynamic-update-slice_fusion.1
  12.2 0.8 constant_dynamic-update-slice_fusion.refs_10_
  13.0 1.3 fusion.16
  14.3 0.8 multiply_convert_fusion.1.w
  15.1 0.9 fusion.4.x
  16.1 44.3 %gather_head.1 = (bf16[4,128,2048]{2,1,0:T(8,128)(2,1)}, bf16[4,2,4,64,384]{4,3,2,1,0:T(8,128)(2,1)}) custom-call(bf16[128,2048]{1,0:T(8,128)(2,1)} %fusion.4.x, bf16[64,1536]{1,0:T(8,128)(2,1)} %multiply_convert_fusion.1.w), custom_call_target="tpu_custom_call" | custom-call | tf_op jit(solution)/shard_map/gather_head/pallas_call | solution.py:123
  60.4 0.1 convert_bitcast_fusion
  60.5 1.0 fusion.39
  61.5 1.0 pad_maximum_fusion.1
  62.5 4.2 project_head.1
  66.8 0.1 fusion.65
  66.8 0.6 pad_maximum_fusion.3.own
  67.5 75.2 %attention.1 = (bf16[128,2048]{1,0:T(8,128)(2,1)}, bf16[128,512]{1,0:T(8,128)(2,1)}, bf16[4,2,4,128,128]{4,3,2,1,0:T(8,128)(2,1)}, bf16[4,2,4,128,128]{4,3,2,1,0...) custom-call(bf16[4,128,128]{2,1,0:T(8,128)(2,1)} %bitcast.87, ...), custom_call_target="tpu_custom_call" | custom-call | tf_op jit(solution)/shard_map/attention/pallas_call | solution.py:123
  142.7 1.3 slice_convert_fusion
  144.0 0.3 copy.49
  144.4 0.3 multiply_reduce_fusion.2
  144.7 0.2 multiply_convert_fusion.refs_2_
  144.9 1.6 fusion.85
  146.5 0.1 copy.37
  146.6 0.2 fusion.48
  146.9 0.5 convolution_compare_fusion
  147.4 1.5 convolution_convert_fusion.2
  148.9 0.3 fusion.6
  149.1 0.3 fusion.5
  149.4 0.5 fusion.37
  149.9 1.4 add_convert_fusion
  151.4 134.8 %mlp.1 = (bf16[2,512,2048]{2,1,0:T(8,128)(2,1)}, bf16[2,512,2048]{2,1,0:T(8,128)(2,1)}, bf16[32,2,16,512]{3,2,1,0:T(8,128)(2,1)}, bf16[32,2,16,512]{3,2,1,0:T(8,...) custom-call(bf16[32,2,16,512]{3,2,1,0:T(8,128)(2,1)} %bitcast.77, ...), custom_call_target="tpu_custom_call" | custom-call | tf_op jit(solution)/shard_map/mlp/pallas_call | solution.py:1235
  286.2 1.8 fusion.86
  288.0 1.8 convolution_select_fusion
  289.8 1.0 fusion.10.refs_2_
  290.8 1.0 convolution_convert_fusion.3.refs_3_
  291.8 0.4 fusion.29
  292.2 0.6 pad.27.refs_4_
  292.8 21.8 %sum_mlp.1 = (bf16[128,2048]{1,0:T(8,128)(2,1)}, bf16[128,2048]{1,0:T(8,128)(2,1)}, f32[128,128]{1,0:T(8,128)}) custom-call(bf16[128,2048]{1,0:T(8,128)(2,1)} %get-tuple-element.57.refs_0_, bf16[128,2048]{1,0:T(8,128)(2,1)} %get-tuple-element.58.refs_1_, bf16[128,512]{1,0:T(8,128)(2,1)} %fusion.10.refs_2_, ...), custom_call_target="tpu_custom_call" | custom-call | tf_op jit(solution)/shard_map/sum_mlp/pallas_call | solution.py:123
  314.7 1.1 multiply_reduce_fusion.3
  315.8 1.4 convolution_convert_fusion.1
  317.3 2.4 multiply_reduce_fusion
  319.7 1.3 multiply_add_fusion
  321.0 0.6 copy-done.8
  321.6 1.1 fusion.7.refs_0_
  322.8 0.3 copy.45
  323.1 2.0 convolution_convert_fusion
  325.1 0.9 pad.28.clone
  326.0 83.8 %attention_back.1 = (bf16[128,2048]{1,0:T(8,128)(2,1)}, bf16[4,64,384]{2,1,0:T(8,128)(2,1)}, f32[64,128]{1,0:T(8,128)}, f32[64,512]{1,0:T(8,128)}, f32[64,128]{1,0:T(8,128)}) custom-call(bf16[128,512]{1,0:T(8,128)(2,1)} %fusion.7.refs_0_, bf16[4,128,128]{2,1,0:T(8,128)(2,1)} %bitcast.88, bf16[4,2,4,128,128]{4,3,2,1,0:T(8,128)(2,1)} %get-tuple-element.64.refs_2_, ...), custom_call_target="tpu_custom_call" | custom-call | tf_op jit(solution)/shard_map/attention_back/pallas_call | solution.py:123
  409.8 1.4 reduce_sum.79
  411.2 1.4 fusion.15
  412.6 2.5 fusion.14
  415.2 0.7 slice_reduce_fusion
  415.9 0.1 convert_multiply_fusion.2
  416.0 0.7 copy.53
  416.7 0.7 copy.54
  417.3 0.7 copy.55
  418.0 10.9 %expert_grads.1 = (f32[2,352,2048]{2,1,0:T(8,128)}, f32[2,352,2048]{2,1,0:T(8,128)}, f32[2,352,2048]{2,1,0:T(8,128)}) custom-call(bf16[2,512,2048]{2,1,0:T(8,128)(2,1)} %get-tuple-element.77.rows, bf16[2,512,2048]{2,1,0:T(8,128)(2,1)} %get-tuple-element.78.grads, bf16[2,512,352]{2,1,0:T(8,128)(2,1)} %get-tuple-element.79.act, ...), custom_call_target="tpu_custom_call" | custom-call | tf_op jit(solution)/shard_map/expert_grads/pallas_call | solution.py:1321
  428.9 0.7 copy.69
  429.6 0.6 copy.70
  430.2 0.7 copy.71
  430.9 0.7 copy.72
  431.5 0.7 copy.73
  (85 shorter events, 0.3 us)
Async XLA Ops:
  7.2 7.9 %copy-start = (bf16[128,2048]{1,0:T(8,128)(2,1)S(1)}, bf16[128,2048]{1,0:T(8,128)(2,1)}, u32[]{:S(2)}) copy-start(bf16[128,2048]{1,0:T(8,128)(2,1)} %param.16) | copy-start | bytes 1572868
  7.2 144.2 %all-gather.2.cloned.1.call-start = ((), (), s32[]{:S(2)}) async-start(), calls=%async_computation | async-start | bytes 9732096 | tf_op jit(solution)/shard_map/all_gather | solution.py:1387
  9.7 51.8 %copy-start.33 = (f32[64]{0:T(128)}, f32[64]{0:T(128)S(1)}, u32[]{:S(2)}) copy-start(f32[64]{0:T(128)S(1)} %convert_element_type.130) | copy-start | bytes 772
  13.0 53.7 %copy-start.9 = (bf16[64,1536]{1,0:T(8,128)(2,1)}, bf16[64,1536]{1,0:T(8,128)(2,1)S(1)}, u32[]{:S(2)}) copy-start(bf16[64,1536]{1,0:T(8,128)(2,1)S(1)} %constant_dynamic-update-slice_fusion.refs_10_) | copy-start | bytes 589828
  14.3 46.1 %copy-start.28 = (f32[128]{0:T(128)}, f32[128]{0:T(128)S(1)}, u32[]{:S(2)}) copy-start(f32[128]{0:T(128)S(1)} %add_rsqrt_fusion.1) | copy-start | bytes 1540
  61.5 5.3 %copy-start.25 = (bf16[64,64]{1,0:T(8,128)(2,1)S(1)}, bf16[64,64]{1,0:T(8,128)(2,1)}, u32[]{:S(2)}) copy-start(bf16[64,64]{1,0:T(8,128)(2,1)} %param.25) | copy-start | bytes 24580
  61.5 5.3 %copy-start.22 = (bf16[512,64]{0,1:T(8,128)(2,1)S(1)}, bf16[512,64]{0,1:T(8,128)(2,1)}, u32[]{:S(2)}) copy-start(bf16[512,64]{0,1:T(8,128)(2,1)} %param.23) | copy-start | bytes 196612
  142.7 1.7 copy-start.4
  144.0 2.8 copy-start.32
  144.4 3.0 copy-start.20
  144.7 2.0 copy-start.35
  144.9 4.5 %copy-start.2 = (bf16[128,2048]{1,0:T(8,128)(2,1)}, bf16[128,2048]{1,0:T(8,128)(2,1)S(1)}, u32[]{:S(2)}) copy-start(bf16[128,2048]{1,0:T(8,128)(2,1)S(1)} %multiply_convert_fusion.refs_2_) | copy-start | bytes 1572868
  144.9 4.5 %copy-start.6 = (bf16[128,2048]{1,0:T(8,128)(2,1)S(1)}, bf16[128,2048]{1,0:T(8,128)(2,1)}, u32[]{:S(2)}) copy-start(bf16[128,2048]{1,0:T(8,128)(2,1)} %refs_3_.1) | copy-start | bytes 1572868
  146.5 3.4 copy-start.26
  146.6 3.3 copy-start.23
  146.8 3.1 copy-start.30
  149.4 1.9 copy-start.11
  286.2 3.6 copy-start.3
  286.2 4.6 %copy-start.10 = (bf16[32,2,16,512]{3,2,1,0:T(8,128)(2,1)S(1)}, bf16[32,2,16,512]{3,2,1,0:T(8,128)(2,1)}, u32[]{:S(2)}) copy-start(bf16[32,2,16,512]{3,2,1,0:T(8,128)(2,1)} %get-tuple-element.60) | copy-start | bytes 3145732
  288.0 3.8 copy-start.24
  290.8 23.9 %copy-start.27 = (f32[128]{0:T(128)S(1)}, f32[128]{0:T(128)}, u32[]{:S(2)}) copy-start(f32[128]{0:T(128)} %copy-done.26) | copy-start | bytes 1540
  290.8 23.9 %copy-start.31 = (f32[128]{0:T(128)S(1)}, f32[128]{0:T(128)}, u32[]{:S(2)}) copy-start(f32[128]{0:T(128)} %copy-done.30) | copy-start | bytes 1540
  290.8 26.4 %copy-start.21 = (f32[2048,1]{0,1:T(1,128)S(1)}, f32[2048,1]{0,1:T(1,128)}, u32[]{:S(2)}) copy-start(f32[2048,1]{0,1:T(1,128)} %copy-done.20) | copy-start | bytes 24580
  290.8 26.5 %copy-start.36 = (f32[128]{0:T(128)S(1)}, f32[128]{0:T(128)}, u32[]{:S(2)}) copy-start(f32[128]{0:T(128)} %copy-done.35) | copy-start | bytes 1540
  314.6 5.1 %copy-start.5 = (bf16[128,2048]{1,0:T(8,128)(2,1)S(1)}, bf16[128,2048]{1,0:T(8,128)(2,1)}, u32[]{:S(2)}) copy-start(bf16[128,2048]{1,0:T(8,128)(2,1)} %get-tuple-element.55) | copy-start | bytes 1572868
  314.6 5.1 %copy-start.7 = (bf16[128,2048]{1,0:T(8,128)(2,1)S(1)}, bf16[128,2048]{1,0:T(8,128)(2,1)}, u32[]{:S(2)}) copy-start(bf16[128,2048]{1,0:T(8,128)(2,1)} %refs_3_.1) | copy-start | bytes 1572868
  314.7 5.1 %copy-start.12 = (bf16[128,2048]{1,0:T(8,128)(2,1)S(1)}, bf16[128,2048]{1,0:T(8,128)(2,1)}, u32[]{:S(2)}) copy-start(bf16[128,2048]{1,0:T(8,128)(2,1)} %get-tuple-element.61) | copy-start | bytes 1572868
  319.7 1.9 copy-start.8
  321.0 4.1 copy-start.1
  321.0 2.0 copy-start.17
  326.0 85.2 %copy-start.29 = (f32[128]{0:T(128)S(1)}, f32[128]{0:T(128)}, u32[]{:S(2)}) copy-start(f32[128]{0:T(128)} %copy-done.28) | copy-start | bytes 1540
  409.8 5.4 %copy-start.19 = (f32[64,128]{1,0:T(8,128)S(1)}, f32[64,128]{1,0:T(8,128)}, u32[]{:S(2)}) copy-start(f32[64,128]{1,0:T(8,128)} %get-tuple-element.73) | copy-start | bytes 98308
  409.8 6.0 %copy-start.16 = (bf16[4,64,384]{2,1,0:T(8,128)(2,1)S(1)}, bf16[4,64,384]{2,1,0:T(8,128)(2,1)}, u32[]{:S(2)}) copy-start(bf16[4,64,384]{2,1,0:T(8,128)(2,1)} %get-tuple-element.71) | copy-start | bytes 589828
  409.8 6.0 %copy-start.34 = (f32[64]{0:T(128)S(1)}, f32[64]{0:T(128)}, u32[]{:S(2)}) copy-start(f32[64]{0:T(128)} %copy-done.33) | copy-start | bytes 772
  418.0 10.9 %copy-start.18 = (f32[64,512]{1,0:T(8,128)S(1)}, f32[64,512]{1,0:T(8,128)}, u32[]{:S(2)}) copy-start(f32[64,512]{1,0:T(8,128)} %get-tuple-element.72) | copy-start | bytes 393220
  418.0 12.2 %copy-start.15 = (f32[64,704]{1,0:T(8,128)S(1)}, f32[64,704]{1,0:T(8,128)}, u32[]{:S(2)}) copy-start(f32[64,704]{1,0:T(8,128)} %get-tuple-element.132) | copy-start | bytes 540676
  418.0 12.9 %copy-start.14 = (f32[64,704]{1,0:T(8,128)S(1)}, f32[64,704]{1,0:T(8,128)}, u32[]{:S(2)}) copy-start(f32[64,704]{1,0:T(8,128)} %get-tuple-element.133) | copy-start | bytes 540676
  418.0 13.6 %copy-start.13 = (f32[64,704]{1,0:T(8,128)S(1)}, f32[64,704]{1,0:T(8,128)}, u32[]{:S(2)}) copy-start(f32[64,704]{1,0:T(8,128)} %get-tuple-element.76) | copy-start | bytes 540676
Sparse Core Ops, SparseCore 0:
  11.6 120.4 all-gather.1

commit v6 on v5

--- a/solution.py
+++ b/solution.py
@@ -1089,7 +1089,7 @@
             yield True
 
 
-def return_steps(held, outs, halves, quarters, out_sem, in_sem, copies):
+def return_steps(held, outs, halves, quarters, out_sem, in_sem, own_sem, copies):
     z, xh, y, place, core = token_places()
     beside, across = wa_places()
     me = z * 8 + xh * 4 + y
@@ -1099,7 +1099,7 @@
     theirs = pl.ds(pl.multiple_of((1 - core) * 2 * quarter, 2 * quarter), 2 * quarter)
     rows_each = halves[0].shape[1]
     items = [(e, a, dz, dx) for a in range(2) for e in range(2) for dz, dx in GROUP_ORDER]
-    paired_up, passed = {}, {}
+    paired_up, passed, own = {}, {}, []
 
     def finished(e, a):
         rows = pl.ds((2 * a + e) * rows_each, rows_each)
@@ -1132,7 +1132,12 @@
         passed[i].wait_recv()
         quarters[a][e, rows] = quarters[a][e, rows] + halves[a][e, rows, kept(dx)]
         if dz + dx == 0:
-            outs[a][me, e] = quarters[a][e, pl.ds(pl.multiple_of(me * SLOTS, SLOTS), SLOTS)]
+            part = pl.ds(pl.multiple_of(me * SLOTS, SLOTS), SLOTS)
+            copy = pltpu.make_async_copy(
+                quarters[a].at[e, part], outs[a].at[me, e], own_sem.at[2 * a + e]
+            )
+            copy.start()
+            own.append(copy)
 
         def one(dy, carry):
             where, block = block_device(dz, dx, dy)
@@ -1154,6 +1159,8 @@
                 add_across(i - BEHIND)
             yield True
         copies.finish()
+        for copy in own:
+            copy.wait()
         for a in range(2):
             sample = outs[a].at[pl.ds(0, 31)]
             pltpu.make_async_copy(sample, sample, in_sem.at[a]).wait()
@@ -1162,20 +1169,46 @@
     return finished, steps()
 
 
+def quarter_sum_steps(ins, outs, got, far, copies):
+    w = lax.axis_index("wa")
+    core, place = w % 2, w // 2
+    beside, across = wa_places()
+    half, quarter = D // 2, D // 4
+    mine = pl.ds(pl.multiple_of(core * half, half), half)
+    theirs = pl.ds(pl.multiple_of((1 - core) * half, half), half)
+    kept = pl.ds(pl.multiple_of(place * quarter, quarter), quarter)
+    given = pl.ds(pl.multiple_of((1 - place) * quarter, quarter), quarter)
+    one = [copies.start(x.at[:, theirs], buf, beside) for x, buf in zip(ins, got)]
+    yield True
+    two = []
+    for a, x in enumerate(ins):
+        one[a].wait_recv()
+        got[a][...] = got[a][...] + x[:, mine]
+        two.append(copies.start(got[a].at[:, given], far[a], across))
+    yield True
+    for a, out in enumerate(outs):
+        two[a].wait_recv()
+        out[...] = got[a][:, kept] + far[a][...]
+    copies.finish()
+    yield True
+
+
 BEHIND = 12
 MLP_ORDER = (
-    "XD" + "SD" * 12 + "RR" + "XD" * 6 + "XTXTXTXTXTXTD"
+    "XD" + "SD" * 12 + "RRW" + "XD" * 3 + "W" + "XD" * 3 + "WXTXTXTXTXTXTD"
     + "XTXTXTTXTXT" + "XTTXTTXRTTXRTTXRTT" + "TTRTTRTTRTTRTTRTTTTRR"
 )
 
 
 def mlp_kernel(count, *refs):
     ins, (x, g, whole), hbm, refs = refs[:2], refs[2:5], refs[5:8], refs[8:]
-    arrived, back_rows, (shared_part, shared_back), refs = refs[:2], refs[2:4], refs[4:6], refs[6:]
+    arrived, back_rows, shared_sums, refs = refs[:2], refs[2:4], refs[4:6], refs[6:]
     shares, kept, refs = refs[:count], refs[count : count + 3], refs[count + 3 :]
     weights, shared_grads, refs = refs[0], refs[1 : 1 + count], refs[1 + count :]
     held, halves, quarters, refs = refs[:3], refs[3:5], refs[5:7], refs[7:]
-    shared_sem, load_sem, out_sem, in_sem, own_sem, *refs = refs
+    shared_parts, shared_got, shared_far, refs = refs[:2], refs[2:4], refs[4:6], refs[6:]
+    shared_sem, load_sem, out_sem, in_sem, own_sem, own_back_sem, *refs = refs
+    sum_sems, refs = refs[:2], refs[2:]
     pass_sems, back_out_sem, back_in_sem, back_sems, refs = refs[:2], refs[2], refs[3], refs[4:6], refs[6:]
     bufs, cube_sems = refs[:-2], refs[-2:]
     greet_blocks([neighbour("x", "A")])
@@ -1190,7 +1223,8 @@
         return place
 
     finished, returning = return_steps(
-        results, back_rows, halves, quarters, back_out_sem, back_in_sem, Copies(*back_sems)
+        results, back_rows, halves, quarters, back_out_sem, back_in_sem, own_back_sem,
+        Copies(*back_sems),
     )
     shards = [grad.shape[0] // 32 for grad in shared_grads]
     cubes = [
@@ -1200,7 +1234,10 @@
     programs = {
         "D": dispatch_steps(ins, arrived, out_sem, in_sem, own_sem, Copies(*pass_sems)),
         "S": shared_steps(
-            x, g, weights, whole, 0, shared_part, shared_back, *shared_grads, shared_sem
+            x, g, weights, whole, 0, *shared_parts, *shared_grads, shared_sem
+        ),
+        "W": quarter_sum_steps(
+            shared_parts, shared_sums, shared_got, shared_far, Copies(*sum_sems)
         ),
         "X": expert_steps(
             *arrived, hbm, held, place_of(0), place_of(1), kept, load_sem, finished
@@ -1221,14 +1258,15 @@
     cube = jax.ShapeDtypeStruct((4, 2, 4, D // 32, width), low)
     out_shape = [at_experts] * 2
     out_shape += [jax.ShapeDtypeStruct((32, 2, SLOTS, D // 4), low)] * 2
-    out_shape += [jax.ShapeDtypeStruct(x.shape, low)] * 2
+    out_shape += [jax.ShapeDtypeStruct((x.shape[0], D // 4), low)] * 2
     out_shape += [jax.ShapeDtypeStruct((D // 32, width), jnp.float32)] * count
     out_shape += [jax.ShapeDtypeStruct((2, rows, hidden), low)] * 3
     scratch = [pltpu.VMEM((D, 3 * shared_step(width)), low)]
     scratch += [pltpu.VMEM(grad.shape, low)] * count
     scratch += [pltpu.VMEM(a.shape, low) for a in expert_weights]
     scratch += [pltpu.VMEM((2, rows, D // 2), low)] * 2 + [pltpu.VMEM((2, rows, D // 4), low)] * 2
-    sems = [(1,), (3,), (2,), (2, 8), (2,), (48,), (48,), (2,), (2,), (36,), (36,)]
+    scratch += [pltpu.VMEM((x.shape[0], D // n), low) for n in (1, 1, 2, 2, 4, 4)]
+    sems = [(1,), (3,), (2,), (2, 8), (2,), (4,), (4,), (4,), (48,), (48,), (2,), (2,), (36,), (36,)]
     scratch += [pltpu.SemaphoreType.DMA(n) for n in sems]
     scratch += reduce_scratch([cube] * count, row_parts([cube] * count))
     anywhere, vmem = pl.BlockSpec(memory_space=pl.ANY), pl.BlockSpec(memory_space=pltpu.VMEM)
@@ -1236,7 +1274,7 @@
         functools.partial(mlp_kernel, count),
         out_shape=out_shape,
         in_specs=[anywhere] * 2 + [vmem] * 2 + [anywhere] * 4,
-        out_specs=[vmem] * len(out_shape),
+        out_specs=[vmem] * 2 + [anywhere] * 2 + [vmem] * (len(out_shape) - 4),
         scratch_shapes=scratch,
         compiler_params=pltpu.CompilerParams(
             collective_id=collective_id, has_side_effects=True, vmem_limit_bytes=VMEM_LIMIT
@@ -1245,56 +1283,59 @@
     )(*arrays, x, g, whole, *expert_weights)
 
 
-def sum_more_kernel(parts, *refs):
-    ins, adds, small = refs[:parts], refs[parts : 2 * parts], refs[2 * parts]
-    outs, small_out = refs[2 * parts + 1 : 3 * parts + 1], refs[3 * parts + 1]
-    got, half, far = (refs[(3 + i) * parts + 2 : (4 + i) * parts + 2] for i in range(3))
-    small_got, small_half, small_far, send_sem, recv_sem = refs[6 * parts + 2 :]
-    w = lax.axis_index("wa")
-    core, place = w % 2, w // 2
-    beside, across = {"wa": w + 1 - 2 * core}, {"wa": (w + 2) % 4}
-    width = D // 2
-    quarter = D // 4
-    mine = pl.ds(pl.multiple_of(core * width, width), width)
-    theirs = pl.ds(pl.multiple_of((1 - core) * width, width), width)
-    own = pl.ds(pl.multiple_of(place * quarter, quarter), quarter)
+def combine_kernel(
+    gate_high, gate_rest, pick, widen, g, returned, back, shared, shared_back,
+    mixed, mixed_in, probs, half, got, far, send_sem, recv_sem,
+):
+    low = mixed.dtype
+    _, _, _, place, core = token_places()
+    beside, across = wa_places()
     greet([beside, across])
     copies = Copies(send_sem, recv_sem)
-    one = [copies.start(ins[a].at[:, theirs], got[a], beside) for a in range(parts)]
-    one.append(copies.start(small, small_got, beside))
-    two = []
-    for a in range(parts):
-        one[a].wait_recv()
-        half[a][...] = ins[a][:, mine] + got[a][...]
-        half[a][:, own] = half[a][:, own] + adds[a][...]
-        two.append(copies.start(half[a], far[a], across))
-    one[parts].wait_recv()
-    small_half[...] = small[...] + small_got[...]
-    two.append(copies.start(small_half, small_far, across))
-    three = []
-    for a in range(parts):
-        two[a].wait_recv()
-        outs[a][:, mine] = half[a][...] + far[a][...]
-        three.append(copies.start(outs[a].at[:, mine], outs[a].at[:, mine], beside))
-    two[parts].wait_recv()
-    small_out[...] = small_half[...] + small_far[...]
-    for copy in three:
+    mine, other = quarter_columns(place, core), quarter_columns(1 - place, core)
+    routed = over(gate_high[...], returned[...], (1, 0)) + over(gate_rest[...], returned[...], (1, 0))
+    mixed[:, mine] = (routed + shared[...].astype(jnp.float32)).astype(low)
+    first, last = [], []
+
+    def spread(out):
+        part = out.at[:, mine]
+        first.append(copies.start(part, part, across))
+        last.append(copies.start(part, part, beside))
+
+    spread(mixed)
+    rows = over(pick[...], back[...], (1, 0))
+    mixed_in[:, mine] = (rows + shared_back[...].astype(jnp.float32)).astype(low)
+    spread(mixed_in)
+    rest = jnp.where(pick[...] > 0, over(g[...], returned[...], (1, 1)), 0.0)
+    total = jnp.zeros(probs.shape, jnp.float32)
+    for _ in range(3):
+        term = rest.astype(low)
+        rest = rest - term.astype(jnp.float32)
+        total = total + over(term, widen[...], (1, 1))
+    half[...] = total
+    one = copies.start(half, got, beside)
+    for copy, out in zip(first, (mixed, mixed_in)):
         copy.wait_recv()
-    copies.finish()
-
-
-def sum_more(arrays, adds, small, collective_id, name):
-    parts = len(arrays)
-    rows = arrays[0].shape[0]
-    dtype = arrays[0].dtype
-    scratch = [pltpu.VMEM((rows, D // 2), dtype)] * (3 * parts)
-    scratch += [pltpu.VMEM(small.shape, small.dtype)] * 3
-    scratch += [pltpu.SemaphoreType.DMA((3 * parts + 2,))] * 2
-    out_shape = [jax.ShapeDtypeStruct(x.shape, x.dtype) for x in (*arrays, small)]
-    return vmem_call(
-        functools.partial(sum_more_kernel, parts), out_shape, (*arrays, *adds, small), scratch,
-        collective_id, name,
-    )
+        part = out.at[:, other]
+        last.append(copies.start(part, part, beside))
+    one.wait()
+    half[...] = half[...] + got[...]
+    two = copies.start(half, far, across)
+    two.wait_recv()
+    probs[...] = half[...] + far[...]
+    for copy in last:
+        copy.wait_recv()
+    for copy in copies.started:
+        if copy is not one:
+            copy.wait_send()
+
+
+def combine(operands, collective_id):
+    tokens, low = operands[0].shape[0], operands[0].dtype
+    out_shape = [jax.ShapeDtypeStruct((tokens, D), low)] * 2
+    out_shape += [jax.ShapeDtypeStruct((tokens, HD), jnp.float32)]
+    scratch = [pltpu.VMEM((tokens, HD), jnp.float32)] * 3 + [pltpu.SemaphoreType.DMA((8,))] * 2
+    return vmem_call(combine_kernel, out_shape, operands, scratch, collective_id, "combine")
 
 
 def swish_parts(pre, lin, act_grads):
@@ -1304,26 +1345,44 @@
     return swish * lin, act_grads * lin * slope, act_grads * swish
 
 
-def expert_grads_kernel(rows, grads, act, pre_grad, lin_grad, gate_grad, up_grad, down_grad):
-    for at in range(0, D, 512):
-        here = slice(at, at + 512)
-        down_grad[0, :, here] = over(act[0], grads[0, :, here], (0, 0))
-        gate_grad[0, :, here] = over(pre_grad[0], rows[0, :, here], (0, 0))
-        up_grad[0, :, here] = over(lin_grad[0], rows[0, :, here], (0, 0))
+def expert_grads_kernel(*refs):
+    hbm, outs, held, results = refs[:5], refs[5:8], refs[8:13], refs[13]
+    load_sem, out_sem = refs[14:]
+    loads = [
+        [
+            pltpu.make_async_copy(src.at[e], dst.at[e], load_sem.at[e, k])
+            for k, (src, dst) in enumerate(zip(hbm, held))
+        ]
+        for e in range(2)
+    ]
+    for load in loads[0] + loads[1]:
+        load.start()
+    rows, grads, act, pre_grad, lin_grad = held
+    stores = []
+    for e in range(2):
+        for load in loads[e]:
+            load.wait()
+        for k, (left, right) in enumerate(((pre_grad, rows), (lin_grad, rows), (act, grads))):
+            results[e, k] = over(left[e], right[e], (0, 0))
+            store = pltpu.make_async_copy(results.at[e, k], outs[k].at[e], out_sem.at[e, k])
+            store.start()
+            stores.append(store)
+    for store in stores:
+        store.wait()
 
 
 def expert_grads(*operands):
     shape = jax.ShapeDtypeStruct((2, operands[2].shape[2], D), jnp.float32)
-
-    def spec(x):
-        return pl.BlockSpec((1, *x.shape[1:]), lambda e: (e, 0, 0))
-
+    scratch = [pltpu.VMEM(x.shape, x.dtype) for x in operands]
+    scratch += [pltpu.VMEM((2, 3, *shape.shape[1:]), jnp.float32)]
+    scratch += [pltpu.SemaphoreType.DMA((2, 5)), pltpu.SemaphoreType.DMA((2, 3))]
+    anywhere = pl.BlockSpec(memory_space=pl.ANY)
     return pl.pallas_call(
         expert_grads_kernel,
-        grid=(2,),
         out_shape=[shape] * 3,
-        in_specs=[spec(x) for x in operands],
-        out_specs=[spec(shape)] * 3,
+        in_specs=[anywhere] * 5,
+        out_specs=[anywhere] * 3,
+        scratch_shapes=scratch,
         compiler_params=pltpu.CompilerParams(vmem_limit_bytes=VMEM_LIMIT),
         name="expert_grads",
     )(*operands)
@@ -1465,13 +1524,20 @@
     gate_grad_turned, up_grad_turned, expert_down_grad = expert_grads(rows_in, grads_in, *kept)
     returned, rows_back = returned.reshape(-1, D // 4), rows_back.reshape(-1, D // 4)
 
-    routed = (dot(gate_high, returned, (1, 0)) + dot(gate_rest, returned, (1, 0))).astype(low)
-    routed_in = dot(pick, rows_back, (1, 0)).astype(low)
-    slot_grads = jnp.where(taken, dot(grad_quarter, returned, (1, 1)), 0.0)
-    prob_part = dot(slot_grads, widen.astype(jnp.float32), (1, 1), precision=PRECISE)
-    prob_part = jnp.pad(prob_part, ((0, 0), (0, HD - experts_all)))
-    mixed, mixed_in, prob_grads = sum_more(
-        (shared_part, shared_in_part), (routed, routed_in), prob_part, 7, "sum_mlp"
+    widen_all = jnp.pad(widen, ((0, HD - experts_all), (0, 0)))
+    mixed, mixed_in, prob_grads = combine(
+        (
+            gate_high,
+            gate_rest,
+            pick,
+            widen_all,
+            grad_quarter,
+            returned,
+            rows_back,
+            shared_part,
+            shared_in_part,
+        ),
+        7,
     )
     block_out = (hidden_state + mixed.astype(jnp.float32)).astype(low)
     prob_grads = prob_grads[:, :experts_all]

time: 443 us -> 434 us (0.980)
  matrix products: 18.9 us -> 13.7 us
    pallas_call x5, Pallas kernels: 229 us -> 223 us  [vmem_call(): pl.pallas_call(kernel, out_shape=out_shape, in_specs=[pl.BlockSpec(memory...]
    dot_general x16 -> x11, matrix products: 18.9 us -> 13.7 us  [dot(): lax.dot_general(left, right, ((over[:1], over[1:]), ((), ())), preferred_...]
  transfers between devices with their start and end apart: 1 -> 1, of which waited for: 0 -> 0; matrix products, arithmetic and copies ran while one was open for 4% -> 5% of each run, Pallas kernels for 28% -> 29%
where the time goes in v6:
time: 434 us; the launch traced here: 430 us
  Pallas kernels  371 us (85%)
  other arithmetic  18.1 us (4%)
  between operations  14.8 us (3%)
  matrix products  13.7 us (3%)
  local copies, waits for them, and re-layouts  12.6 us (3%)
    pallas_call x5, Pallas kernels, vmem_call(): pl.pallas_call(kernel, out_shape=out_shape, in_specs=[pl.BlockSpec(memory...  223 us
    pallas_call x1, Pallas kernels, mlp(): pl.pallas_call(functools.partial(mlp_kernel, count), out_shape=out_shape,...  139 us
    dot_general x11, matrix products, dot(): lax.dot_general(left, right, ((over[:1], over[1:]), ((), ())), preferred_...  13.7 us
    pallas_call x1, Pallas kernels, expert_grads(): pl.pallas_call(expert_grads_kernel, out_shape=[shape] * 3, in_specs=[anyw...  9.72 us
  transfers between devices with their start and end apart: 1, of which 0 were waited for; matrix products, arithmetic and copies ran while one was open for 5% of the time, Pallas kernels for 29%

profile of v6, /device:TPU:1, one launch (start us, length us, event | category | flops | bytes accessed | tf_op | source)
XLA Modules:
  0.0 430.4 jit_solution(16139634611338127526)
XLA Ops:
  7.2 0.0 copy-start
  7.2 0.0 all-gather.2.cloned.1.call-start
  7.2 1.8 fusion.25
  9.0 0.0 all-gather.2.cloned.1.call-update
  9.1 0.7 convert_element_type.125
  9.7 0.8 copy.34
  10.5 0.8 constant_dynamic-update-slice_fusion.2
  11.3 0.8 constant_dynamic-update-slice_fusion.1
  12.2 0.8 constant_dynamic-update-slice_fusion.refs_10_
  13.0 1.3 fusion.15
  14.3 0.8 multiply_convert_fusion.1.w
  15.1 0.9 fusion.4.x
  16.1 44.3 %gather_head.1 = (bf16[4,128,2048]{2,1,0:T(8,128)(2,1)}, bf16[4,2,4,64,384]{4,3,2,1,0:T(8,128)(2,1)}) custom-call(bf16[128,2048]{1,0:T(8,128)(2,1)} %fusion.4.x, bf16[64,1536]{1,0:T(8,128)(2,1)} %multiply_convert_fusion.1.w), custom_call_target="tpu_custom_call" | custom-call | tf_op jit(solution)/shard_map/gather_head/pallas_call | solution.py:123
  60.4 0.1 convert_bitcast_fusion
  60.5 1.0 fusion.32
  61.5 1.0 pad_maximum_fusion.1
  62.5 4.2 project_head.1
  66.8 0.1 fusion.58
  66.9 0.6 pad_maximum_fusion.3.own
  67.5 75.3 %attention.1 = (bf16[128,2048]{1,0:T(8,128)(2,1)}, bf16[128,512]{1,0:T(8,128)(2,1)}, bf16[4,2,4,128,128]{4,3,2,1,0:T(8,128)(2,1)}, bf16[4,2,4,128,128]{4,3,2,1,0...) custom-call(bf16[4,128,128]{2,1,0:T(8,128)(2,1)} %bitcast.79, ...), custom_call_target="tpu_custom_call" | custom-call | tf_op jit(solution)/shard_map/attention/pallas_call | solution.py:123
  142.8 1.3 slice_convert_fusion
  144.1 0.0 copy-start.30
  144.1 0.3 copy.46
  144.5 0.3 multiply_reduce_fusion.2
  144.7 0.2 multiply_convert_fusion.refs_2_
  145.0 0.0 copy-start.2
  145.0 1.6 fusion.75
  146.6 0.1 copy.36
  146.7 0.2 fusion.41
  146.9 0.0 copy-start.28
  146.9 0.9 constant_dynamic-slice_fusion.g
  147.9 0.7 pad_convert_fusion.widen
  148.6 1.2 fusion.76
  149.8 1.5 convolution_convert_fusion.2
  151.3 0.3 fusion.6.gate_rest
  151.6 0.3 fusion.5.gate_high
  151.9 0.4 fusion.79
  152.4 1.4 add_convert_fusion
  153.8 138.6 %mlp.1 = (bf16[2,512,2048]{2,1,0:T(8,128)(2,1)}, bf16[2,512,2048]{2,1,0:T(8,128)(2,1)}, bf16[32,2,16,512]{3,2,1,0:T(8,128)(2,1)}, bf16[32,2,16,512]{3,2,1,0:T(8,...) custom-call(bf16[32,2,16,512]{3,2,1,0:T(8,128)(2,1)} %bitcast.69, ...), custom_call_target="tpu_custom_call" | custom-call | tf_op jit(solution)/shard_map/mlp/pallas_call | solution.py:1273
  292.4 16.7 %combine.1 = (bf16[128,2048]{1,0:T(8,128)(2,1)}, bf16[128,2048]{1,0:T(8,128)(2,1)}, f32[128,128]{1,0:T(8,128)}) custom-call(bf16[128,1024]{1,0:T(8,128)(2,1)} %copy-done.10, bf16[128,1024]{1,0:T(8,128)(2,1)} %copy-done.9, bf16[128,1024]{1,0:T(8,128)(2,1)} %get-tuple-element.103.pick, bf16[128,1024]{1,0:T(8,128)(2,1)} %pad_convert_fusion.widen, ...), custom_call_target="tpu_custom_call" | custom-call | tf_op jit(solution)/shard_map/combine/pallas_call | solution.py:123
  309.2 1.1 multiply_reduce_fusion.3
  310.3 1.4 convolution_convert_fusion.1
  311.8 2.4 multiply_reduce_fusion
  314.2 1.3 multiply_add_fusion
  315.5 0.6 copy-done.5
  316.1 1.1 fusion.7.refs_0_
  317.3 0.3 copy.42
  317.6 2.1 convolution_convert_fusion
  319.6 0.9 pad.31.clone
  320.5 82.3 %attention_back.1 = (bf16[128,2048]{1,0:T(8,128)(2,1)}, bf16[4,64,384]{2,1,0:T(8,128)(2,1)}, f32[64,128]{1,0:T(8,128)}, f32[64,512]{1,0:T(8,128)}, f32[64,128]{1,0:T(8,128)}) custom-call(bf16[128,512]{1,0:T(8,128)(2,1)} %fusion.7.refs_0_, bf16[4,128,128]{2,1,0:T(8,128)(2,1)} %bitcast.80, bf16[4,2,4,128,128]{4,3,2,1,0:T(8,128)(2,1)} %get-tuple-element.64.refs_2_, ...), custom_call_target="tpu_custom_call" | custom-call | tf_op jit(solution)/shard_map/attention_back/pallas_call | solution.py:123
  402.9 1.4 fusion.14
  404.3 2.5 fusion.13
  406.8 0.7 slice_reduce_fusion
  407.5 0.1 convert_multiply_fusion.2
  407.7 0.7 copy.50
  408.3 0.7 copy.51
  409.0 0.7 copy.52
  409.7 0.6 reduce_sum.79
  410.3 9.7 %expert_grads.1 = (f32[2,352,2048]{2,1,0:T(8,128)}, f32[2,352,2048]{2,1,0:T(8,128)}, f32[2,352,2048]{2,1,0:T(8,128)}) custom-call(bf16[2,512,2048]{2,1,0:T(8,128)(2,1)} %get-tuple-element.77.refs_0_, bf16[2,512,2048]{2,1,0:T(8,128)(2,1)} %get-tuple-element.78.refs_1_, bf16[2,512,352]{2,1,0:T(8,128)(2,1)} %get-tuple-element.79.refs_2_, ...), custom_call_target="tpu_custom_call" | custom-call | tf_op jit(solution)/shard_map/expert_grads/pallas_call | solution.py:1380
  420.0 0.7 copy.64
  420.7 0.6 copy.65
  421.3 0.7 copy.66
  422.0 0.7 copy.67
  422.7 0.7 copy.68
  (79 shorter events, 0.3 us)
Async XLA Ops:
  7.2 7.9 %copy-start = (bf16[128,2048]{1,0:T(8,128)(2,1)S(1)}, bf16[128,2048]{1,0:T(8,128)(2,1)}, u32[]{:S(2)}) copy-start(bf16[128,2048]{1,0:T(8,128)(2,1)} %param.16) | copy-start | bytes 1572868
  7.2 146.6 %all-gather.2.cloned.1.call-start = ((), (), s32[]{:S(2)}) async-start(), calls=%async_computation | async-start | bytes 9732096 | tf_op jit(solution)/shard_map/all_gather | solution.py:1446
  9.7 51.8 %copy-start.31 = (f32[64]{0:T(128)}, f32[64]{0:T(128)S(1)}, u32[]{:S(2)}) copy-start(f32[64]{0:T(128)S(1)} %convert_element_type.125) | copy-start | bytes 772
  13.0 53.8 %copy-start.8 = (bf16[64,1536]{1,0:T(8,128)(2,1)}, bf16[64,1536]{1,0:T(8,128)(2,1)S(1)}, u32[]{:S(2)}) copy-start(bf16[64,1536]{1,0:T(8,128)(2,1)S(1)} %constant_dynamic-update-slice_fusion.refs_10_) | copy-start | bytes 589828
  14.3 46.1 %copy-start.26 = (f32[128]{0:T(128)}, f32[128]{0:T(128)S(1)}, u32[]{:S(2)}) copy-start(f32[128]{0:T(128)S(1)} %add_rsqrt_fusion.1) | copy-start | bytes 1540
  61.5 5.3 %copy-start.23 = (bf16[64,64]{1,0:T(8,128)(2,1)S(1)}, bf16[64,64]{1,0:T(8,128)(2,1)}, u32[]{:S(2)}) copy-start(bf16[64,64]{1,0:T(8,128)(2,1)} %param.25) | copy-start | bytes 24580
  61.5 5.3 %copy-start.21 = (bf16[512,64]{0,1:T(8,128)(2,1)S(1)}, bf16[512,64]{0,1:T(8,128)(2,1)}, u32[]{:S(2)}) copy-start(bf16[512,64]{0,1:T(8,128)(2,1)} %param.23) | copy-start | bytes 196612
  142.8 1.7 copy-start.3
  144.1 4.5 %copy-start.30 = (s32[128,6]{0,1:T(8,128)S(1)}, s32[128,6]{0,1:T(8,128)}, u32[]{:S(2)}) copy-start(s32[128,6]{0,1:T(8,128)} %param.18) | copy-start | bytes 9220
  144.4 5.4 %copy-start.19 = (f32[2048,1]{0,1:T(1,128)}, f32[2048,1]{0,1:T(1,128)S(1)}, u32[]{:S(2)}) copy-start(f32[2048,1]{0,1:T(1,128)S(1)} %copy.46) | copy-start | bytes 24580
  144.7 1.9 copy-start.33
  145.0 6.6 %copy-start.2 = (bf16[128,2048]{1,0:T(8,128)(2,1)}, bf16[128,2048]{1,0:T(8,128)(2,1)S(1)}, u32[]{:S(2)}) copy-start(bf16[128,2048]{1,0:T(8,128)(2,1)S(1)} %multiply_convert_fusion.refs_2_) | copy-start | bytes 1572868
  146.6 5.8 %copy-start.24 = (f32[128]{0:T(128)}, f32[128]{0:T(128)S(1)}, u32[]{:S(2)}) copy-start(f32[128]{0:T(128)S(1)} %get-tuple-element.101) | copy-start | bytes 1540
  146.9 5.5 %copy-start.28 = (f32[128]{0:T(128)}, f32[128]{0:T(128)S(1)}, u32[]{:S(2)}) copy-start(f32[128]{0:T(128)S(1)} %fusion.41) | copy-start | bytes 1540
  147.8 4.5 %copy-start.7 = (bf16[128,512]{1,0:T(8,128)(2,1)}, bf16[128,512]{1,0:T(8,128)(2,1)S(1)}, u32[]{:S(2)}) copy-start(bf16[128,512]{1,0:T(8,128)(2,1)S(1)} %constant_dynamic-slice_fusion.g) | copy-start | bytes 393220
  151.6 2.2 copy-start.9
  151.9 1.9 copy-start.10
  292.4 16.8 %copy-start.25 = (f32[128]{0:T(128)S(1)}, f32[128]{0:T(128)}, u32[]{:S(2)}) copy-start(f32[128]{0:T(128)} %copy-done.24) | copy-start | bytes 1540
  292.4 16.8 %copy-start.29 = (f32[128]{0:T(128)S(1)}, f32[128]{0:T(128)}, u32[]{:S(2)}) copy-start(f32[128]{0:T(128)} %copy-done.28) | copy-start | bytes 1540
  292.4 19.4 %copy-start.20 = (f32[2048,1]{0,1:T(1,128)S(1)}, f32[2048,1]{0,1:T(1,128)}, u32[]{:S(2)}) copy-start(f32[2048,1]{0,1:T(1,128)} %copy-done.19) | copy-start | bytes 24580
  292.4 19.4 %copy-start.34 = (f32[128]{0:T(128)S(1)}, f32[128]{0:T(128)}, u32[]{:S(2)}) copy-start(f32[128]{0:T(128)} %copy-done.33) | copy-start | bytes 1540
  309.1 5.1 %copy-start.4 = (bf16[128,2048]{1,0:T(8,128)(2,1)S(1)}, bf16[128,2048]{1,0:T(8,128)(2,1)}, u32[]{:S(2)}) copy-start(bf16[128,2048]{1,0:T(8,128)(2,1)} %get-tuple-element.55) | copy-start | bytes 1572868
  309.2 5.1 %copy-start.6 = (bf16[128,2048]{1,0:T(8,128)(2,1)S(1)}, bf16[128,2048]{1,0:T(8,128)(2,1)}, u32[]{:S(2)}) copy-start(bf16[128,2048]{1,0:T(8,128)(2,1)} %refs_3_.1) | copy-start | bytes 1572868
  309.2 5.1 %copy-start.11 = (bf16[128,2048]{1,0:T(8,128)(2,1)S(1)}, bf16[128,2048]{1,0:T(8,128)(2,1)}, u32[]{:S(2)}) copy-start(bf16[128,2048]{1,0:T(8,128)(2,1)} %get-tuple-element.61) | copy-start | bytes 1572868
  314.2 1.9 copy-start.5
  315.5 4.1 copy-start.1
  315.5 2.0 copy-start.16
  320.5 82.3 %copy-start.27 = (f32[128]{0:T(128)S(1)}, f32[128]{0:T(128)}, u32[]{:S(2)}) copy-start(f32[128]{0:T(128)} %copy-done.26) | copy-start | bytes 1540
  402.8 4.0 copy-start.18
  402.8 4.7 %copy-start.15 = (bf16[4,64,384]{2,1,0:T(8,128)(2,1)S(1)}, bf16[4,64,384]{2,1,0:T(8,128)(2,1)}, u32[]{:S(2)}) copy-start(bf16[4,64,384]{2,1,0:T(8,128)(2,1)} %get-tuple-element.71) | copy-start | bytes 589828
  402.9 4.7 %copy-start.32 = (f32[64]{0:T(128)S(1)}, f32[64]{0:T(128)}, u32[]{:S(2)}) copy-start(f32[64]{0:T(128)} %copy-done.31) | copy-start | bytes 772
  404.3 5.4 %copy-start.22 = (f32[64,128]{1,0:T(8,128)S(1)}, f32[64,128]{1,0:T(8,128)}, u32[]{:S(2)}) copy-start(f32[64,128]{1,0:T(8,128)} %get-tuple-element.70) | copy-start | bytes 98308
  410.3 9.7 %copy-start.17 = (f32[64,512]{1,0:T(8,128)S(1)}, f32[64,512]{1,0:T(8,128)}, u32[]{:S(2)}) copy-start(f32[64,512]{1,0:T(8,128)} %get-tuple-element.72) | copy-start | bytes 393220
  410.3 11.0 %copy-start.14 = (f32[64,704]{1,0:T(8,128)S(1)}, f32[64,704]{1,0:T(8,128)}, u32[]{:S(2)}) copy-start(f32[64,704]{1,0:T(8,128)} %get-tuple-element.132) | copy-start | bytes 540676
  410.3 11.7 %copy-start.13 = (f32[64,704]{1,0:T(8,128)S(1)}, f32[64,704]{1,0:T(8,128)}, u32[]{:S(2)}) copy-start(f32[64,704]{1,0:T(8,128)} %get-tuple-element.133) | copy-start | bytes 540676
  410.3 12.4 %copy-start.12 = (f32[64,704]{1,0:T(8,128)S(1)}, f32[64,704]{1,0:T(8,128)}, u32[]{:S(2)}) copy-start(f32[64,704]{1,0:T(8,128)} %get-tuple-element.76) | copy-start | bytes 540676
Sparse Core Ops, SparseCore 0:
  11.6 120.4 all-gather.1

commit v7 on v6

--- a/solution.py
+++ b/solution.py
@@ -1443,10 +1443,11 @@
             [jnp.pad(x, ((0, 0), (0, -x.shape[1] % HD))) for x in arrays], axis=1
         )
 
+    gate_router = jnp.concatenate([shared_gate, router_weight], axis=1)
+    up_gain = jnp.concatenate([shared_up, mlp_gain[:, None]], axis=1)
     shared_whole = lax.all_gather(
-        beside((shared_gate, shared_up, shared_down.T)), groups, axis=0, tiled=True
-    )
-    router_own = jnp.concatenate([router_weight, mlp_gain[:, None]], axis=1)
+        beside((gate_router, up_gain, shared_down.T)), groups, axis=0, tiled=True
+    )
     tokens_f = tokens.astype(jnp.float32)
     inv_one = lax.rsqrt(jnp.mean(tokens_f * tokens_f, axis=-1, keepdims=True) + EPSILON)
     unit_one = tokens_f * inv_one
@@ -1463,13 +1464,12 @@
         x.reshape(by_head) for x in project(head_rows, head_weights, cosine, sine)
     )
     attn_out, attended, head_keys, head_values, probs, exact, whole = attention(
-        head_queries, own_keys, own_values, beside((output_weight.T, router_own)), 2
+        head_queries, own_keys, own_values, output_weight.T, 2
     )
     attn_out = attn_out.astype(jnp.float32)
-    whole = whole.reshape(D, -1)
-    turned = whole[:, :head_cols]
-    full_router = whole[:, head_cols : head_cols + experts_all]
-    gain_two = whole[:, head_cols + experts_all].astype(jnp.float32)
+    turned = whole.reshape(D, head_cols)
+    full_router = shared_whole[:, hidden_cols : hidden_cols + experts_all]
+    gain_two = shared_whole[:, shared_step(hidden_cols) + hidden_cols].astype(jnp.float32)
     hidden_state = tokens_f + attn_out
     inv_two = lax.rsqrt(jnp.mean(hidden_state * hidden_state, axis=-1, keepdims=True) + EPSILON)
     unit_two = hidden_state * inv_two

time: 434 us -> 434 us (level)
  transfers between devices with their start and end apart: 1 -> 1, of which waited for: 0 -> 0; matrix products, arithmetic and copies ran while one was open for 5% -> 3% of each run, Pallas kernels for 29% -> 28%
where the time goes in v7:
time: 434 us; the launch traced here: 429 us
  Pallas kernels  367 us (85%)
  other arithmetic  18.7 us (4%)
  between operations  14.8 us (3%)
  local copies, waits for them, and re-layouts  14.4 us (3%)
  matrix products  14.1 us (3%)
    pallas_call x5, Pallas kernels, vmem_call(): pl.pallas_call(kernel, out_shape=out_shape, in_specs=[pl.BlockSpec(memory...  220 us
    pallas_call x1, Pallas kernels, mlp(): pl.pallas_call(functools.partial(mlp_kernel, count), out_shape=out_shape,...  138 us
    dot_general x11, matrix products, dot(): lax.dot_general(left, right, ((over[:1], over[1:]), ((), ())), preferred_...  14.1 us
    pallas_call x1, Pallas kernels, expert_grads(): pl.pallas_call(expert_grads_kernel, out_shape=[shape] * 3, in_specs=[anyw...  9.72 us
  transfers between devices with their start and end apart: 1, of which 0 were waited for; matrix products, arithmetic and copies ran while one was open for 3% of the time, Pallas kernels for 28%

profile of v7, /device:TPU:1, one launch (start us, length us, event | category | flops | bytes accessed | tf_op | source)
XLA Modules:
  0.0 429.3 jit_solution(16994675581585524779)
XLA Ops:
  7.2 0.0 copy-start
  7.2 0.0 all-gather.2.cloned.1.call-start
  7.2 0.8 copy.34
  8.0 1.0 fusion.23
  9.0 0.9 pad.20
  9.9 1.7 concatenate.25
  11.6 0.0 all-gather.2.cloned.1.call-update
  11.7 0.7 convert_element_type.123
  12.3 0.8 constant_dynamic-update-slice_fusion.2
  13.2 0.8 constant_dynamic-update-slice_fusion.1
  14.0 0.8 constant_dynamic-update-slice_fusion.refs_10_
  14.9 1.3 fusion.10
  16.2 0.0 copy-start.23
  16.2 0.8 multiply_convert_fusion.1.w
  17.0 0.9 fusion.2.x
  17.9 46.5 %gather_head.1 = (bf16[4,128,2048]{2,1,0:T(8,128)(2,1)}, bf16[4,2,4,64,384]{4,3,2,1,0:T(8,128)(2,1)}) custom-call(bf16[128,2048]{1,0:T(8,128)(2,1)} %fusion.2.x, bf16[64,1536]{1,0:T(8,128)(2,1)} %multiply_convert_fusion.1.w), custom_call_target="tpu_custom_call" | custom-call | tf_op jit(solution)/shard_map/gather_head/pallas_call | solution.py:123
  64.4 0.1 convert_bitcast_fusion
  64.5 1.0 fusion.24
  65.5 1.0 pad_maximum_fusion.1
  66.5 4.2 project_head.1
  70.7 69.8 %attention.1 = (bf16[128,2048]{1,0:T(8,128)(2,1)}, bf16[128,512]{1,0:T(8,128)(2,1)}, bf16[4,2,4,128,128]{4,3,2,1,0:T(8,128)(2,1)}, bf16[4,2,4,128,128]{4,3,2,1,0...) custom-call(bf16[4,128,128]{2,1,0:T(8,128)(2,1)} %bitcast.76, ...), custom_call_target="tpu_custom_call" | custom-call | tf_op jit(solution)/shard_map/attention/pallas_call | solution.py:123
  140.5 1.0 constant_dynamic-slice_fusion.g
  141.6 0.7 pad_convert_fusion.widen
  142.3 1.3 multiply_reduce_fusion.2
  143.6 1.2 fusion.65
  144.9 1.4 convert_reduce_fusion
  146.3 0.2 multiply_convert_fusion.refs_2_
  146.5 0.0 copy-start.2
  146.6 1.8 fusion.64
  148.4 0.0 copy-start.21
  148.4 0.1 copy.35
  148.5 0.2 fusion.33
  148.7 0.0 copy-start.25
  148.7 0.3 fusion.4.gate_rest
  149.0 0.3 fusion.3.gate_high
  149.3 0.0 copy-start.10
  149.3 1.5 convolution_convert_fusion.2
  150.8 0.4 fusion.68
  151.3 1.4 add_convert_fusion
  152.7 137.9 %mlp.1 = (bf16[2,512,2048]{2,1,0:T(8,128)(2,1)}, bf16[2,512,2048]{2,1,0:T(8,128)(2,1)}, bf16[32,2,16,512]{3,2,1,0:T(8,128)(2,1)}, bf16[32,2,16,512]{3,2,1,0:T(8,...) custom-call(bf16[32,2,16,512]{3,2,1,0:T(8,128)(2,1)} %bitcast.69, ...), custom_call_target="tpu_custom_call" | custom-call | tf_op jit(solution)/shard_map/mlp/pallas_call | solution.py:1273
  290.6 17.4 %combine.1 = (bf16[128,2048]{1,0:T(8,128)(2,1)}, bf16[128,2048]{1,0:T(8,128)(2,1)}, f32[128,128]{1,0:T(8,128)}) custom-call(bf16[128,1024]{1,0:T(8,128)(2,1)} %copy-done.10, bf16[128,1024]{1,0:T(8,128)(2,1)} %copy-done.9, bf16[128,1024]{1,0:T(8,128)(2,1)} %get-tuple-element.103.pick, bf16[128,1024]{1,0:T(8,128)(2,1)} %pad_convert_fusion.widen, ...), custom_call_target="tpu_custom_call" | custom-call | tf_op jit(solution)/shard_map/combine/pallas_call | solution.py:123
  308.0 1.0 multiply_reduce_fusion.3
  309.1 1.4 convolution_convert_fusion.1
  310.5 2.6 multiply_reduce_fusion
  313.1 0.3 copy.40
  313.4 0.9 pad.23.clone
  314.3 2.3 multiply_add_fusion
  316.7 1.1 convolution_convert_fusion.3.refs_0_
  317.8 2.0 convolution_convert_fusion
  319.9 81.9 %attention_back.1 = (bf16[128,2048]{1,0:T(8,128)(2,1)}, bf16[4,64,384]{2,1,0:T(8,128)(2,1)}, f32[64,128]{1,0:T(8,128)}, f32[64,512]{1,0:T(8,128)}, f32[64,128]{1,0:T(8,128)}) custom-call(bf16[128,512]{1,0:T(8,128)(2,1)} %convolution_convert_fusion.3.refs_0_, bf16[4,128,128]{2,1,0:T(8,128)(2,1)} %bitcast.77, ...), custom_call_target="tpu_custom_call" | custom-call | tf_op jit(solution)/shard_map/attention_back/pallas_call | solution.py:123
  401.8 1.4 fusion.9
  403.2 2.5 fusion.8
  405.8 0.7 slice_reduce_fusion
  406.5 0.1 convert_multiply_fusion.2
  406.6 0.7 copy.47
  407.3 0.7 copy.48
  407.9 0.7 copy.49
  408.6 0.6 reduce_sum.79
  409.2 9.7 %expert_grads.1 = (f32[2,352,2048]{2,1,0:T(8,128)}, f32[2,352,2048]{2,1,0:T(8,128)}, f32[2,352,2048]{2,1,0:T(8,128)}) custom-call(bf16[2,512,2048]{2,1,0:T(8,128)(2,1)} %get-tuple-element.77.refs_0_, bf16[2,512,2048]{2,1,0:T(8,128)(2,1)} %get-tuple-element.78.refs_1_, bf16[2,512,352]{2,1,0:T(8,128)(2,1)} %get-tuple-element.79.refs_2_, ...), custom_call_target="tpu_custom_call" | custom-call | tf_op jit(solution)/shard_map/expert_grads/pallas_call | solution.py:1380
  419.0 0.7 copy.61
  419.6 0.6 copy.62
  420.2 0.7 copy.63
  420.9 0.7 copy.64
  421.6 0.7 copy.65
  (72 shorter events, 0.3 us)
Async XLA Ops:
  7.2 9.8 %copy-start = (bf16[128,2048]{1,0:T(8,128)(2,1)S(1)}, bf16[128,2048]{1,0:T(8,128)(2,1)}, u32[]{:S(2)}) copy-start(bf16[128,2048]{1,0:T(8,128)(2,1)} %param.16) | copy-start | bytes 1572868
  7.2 137.7 %all-gather.2.cloned.1.call-start = ((), (), s32[]{:S(2)}) async-start(), calls=%async_computation | async-start | bytes 9732096 | tf_op jit(solution)/shard_map/all_gather | solution.py:1448
  12.3 3.8 copy-start.28
  14.9 55.8 %copy-start.8 = (bf16[64,1536]{1,0:T(8,128)(2,1)}, bf16[64,1536]{1,0:T(8,128)(2,1)S(1)}, u32[]{:S(2)}) copy-start(bf16[64,1536]{1,0:T(8,128)(2,1)S(1)} %constant_dynamic-update-slice_fusion.refs_10_) | copy-start | bytes 589828
  16.2 0.8 copy-start.23
  66.5 77.1 %copy-start.27 = (s32[128,6]{0,1:T(8,128)S(1)}, s32[128,6]{0,1:T(8,128)}, u32[]{:S(2)}) copy-start(s32[128,6]{0,1:T(8,128)} %param.18) | copy-start | bytes 9220
  140.5 5.8 %copy-start.3 = (bf16[128,2048]{1,0:T(8,128)(2,1)S(1)}, bf16[128,2048]{1,0:T(8,128)(2,1)}, u32[]{:S(2)}) copy-start(bf16[128,2048]{1,0:T(8,128)(2,1)} %get-tuple-element.55) | copy-start | bytes 1572868
  141.5 9.7 %copy-start.6 = (bf16[128,512]{1,0:T(8,128)(2,1)}, bf16[128,512]{1,0:T(8,128)(2,1)S(1)}, u32[]{:S(2)}) copy-start(bf16[128,512]{1,0:T(8,128)(2,1)S(1)} %constant_dynamic-slice_fusion.g) | copy-start | bytes 393220
  143.6 2.7 copy-start.30
  146.3 4.9 %copy-start.18 = (f32[2048]{0:T(1024)}, f32[2048]{0:T(1024)S(1)}, u32[]{:S(2)}) copy-start(f32[2048]{0:T(1024)S(1)} %convert_reduce_fusion) | copy-start | bytes 24580
  146.5 4.7 %copy-start.2 = (bf16[128,2048]{1,0:T(8,128)(2,1)}, bf16[128,2048]{1,0:T(8,128)(2,1)S(1)}, u32[]{:S(2)}) copy-start(bf16[128,2048]{1,0:T(8,128)(2,1)S(1)} %multiply_convert_fusion.refs_2_) | copy-start | bytes 1572868
  148.4 4.3 copy-start.21
  148.7 4.0 copy-start.25
  149.0 3.7 copy-start.9
  149.3 1.5 copy-start.10
  290.6 17.5 %copy-start.22 = (f32[128]{0:T(128)S(1)}, f32[128]{0:T(128)}, u32[]{:S(2)}) copy-start(f32[128]{0:T(128)} %copy-done.21) | copy-start | bytes 1540
  290.6 17.5 %copy-start.26 = (f32[128]{0:T(128)S(1)}, f32[128]{0:T(128)}, u32[]{:S(2)}) copy-start(f32[128]{0:T(128)} %copy-done.25) | copy-start | bytes 1540
  290.6 19.9 %copy-start.19 = (f32[2048]{0:T(1024)S(1)}, f32[2048]{0:T(1024)}, u32[]{:S(2)}) copy-start(f32[2048]{0:T(1024)} %copy-done.18) | copy-start | bytes 24580
  290.6 19.9 %copy-start.31 = (f32[128]{0:T(128)S(1)}, f32[128]{0:T(128)}, u32[]{:S(2)}) copy-start(f32[128]{0:T(128)} %copy-done.30) | copy-start | bytes 1540
  310.5 3.8 copy-start.4
  310.5 3.8 copy-start.5
  313.4 3.3 copy-start.7
  314.3 3.5 copy-start.15
  316.7 3.2 copy-start.1
  319.9 81.9 %copy-start.24 = (f32[128]{0:T(128)S(1)}, f32[128]{0:T(128)}, u32[]{:S(2)}) copy-start(f32[128]{0:T(128)} %copy-done.23) | copy-start | bytes 1540
  401.7 4.0 copy-start.17
  401.7 4.7 %copy-start.14 = (bf16[4,64,384]{2,1,0:T(8,128)(2,1)S(1)}, bf16[4,64,384]{2,1,0:T(8,128)(2,1)}, u32[]{:S(2)}) copy-start(bf16[4,64,384]{2,1,0:T(8,128)(2,1)} %get-tuple-element.71) | copy-start | bytes 589828
  401.7 4.7 %copy-start.29 = (f32[64]{0:T(128)S(1)}, f32[64]{0:T(128)}, u32[]{:S(2)}) copy-start(f32[64]{0:T(128)} %copy-done.28) | copy-start | bytes 772
  401.8 6.8 %copy-start.20 = (f32[64,128]{1,0:T(8,128)S(1)}, f32[64,128]{1,0:T(8,128)}, u32[]{:S(2)}) copy-start(f32[64,128]{1,0:T(8,128)} %get-tuple-element.70) | copy-start | bytes 98308
  409.2 9.7 %copy-start.16 = (f32[64,512]{1,0:T(8,128)S(1)}, f32[64,512]{1,0:T(8,128)}, u32[]{:S(2)}) copy-start(f32[64,512]{1,0:T(8,128)} %get-tuple-element.72) | copy-start | bytes 393220
  409.2 11.0 %copy-start.13 = (f32[64,704]{1,0:T(8,128)S(1)}, f32[64,704]{1,0:T(8,128)}, u32[]{:S(2)}) copy-start(f32[64,704]{1,0:T(8,128)} %get-tuple-element.132) | copy-start | bytes 540676
  409.2 11.7 %copy-start.12 = (f32[64,704]{1,0:T(8,128)S(1)}, f32[64,704]{1,0:T(8,128)}, u32[]{:S(2)}) copy-start(f32[64,704]{1,0:T(8,128)} %get-tuple-element.133) | copy-start | bytes 540676
  409.2 12.4 %copy-start.11 = (f32[64,704]{1,0:T(8,128)S(1)}, f32[64,704]{1,0:T(8,128)}, u32[]{:S(2)}) copy-start(f32[64,704]{1,0:T(8,128)} %get-tuple-element.76) | copy-start | bytes 540676
Sparse Core Ops, SparseCore 0:
  11.8 120.6 all-gather.1
